TPU v7x, 512 devices: a whole 4x8x8 slice. The times are simulated.
512 devices in a mesh: dp: 16 (over z, core), enc: 32 (over y, x).
Axes of the slice: x: 4, y: 8, z: 8, core: 2. Of those that a mesh axis runs over, the one named last changes fastest.
Arguments:
- patches: bfloat16 [512, 128, 640], P(('dp', 'enc')), may hold values from -6 to 6
- lengths: int32 [512], P('dp'), may hold values from 32 to 128, as said below
- offsets: int32 [512], P('dp'), may hold values from 0 to 8064, as said below
- w_qkv: bfloat16 [640, 1920], P(None, 'enc')
- w_out: bfloat16 [640, 640], P(None, 'enc'), may hold values from -0.25 to 0.25
- d_embeds: bfloat16 [131072, 640], P(('dp', 'enc')), may hold values from -24 to 24
Outputs:
- embeds: bfloat16 [131072, 640], P(('dp', 'enc'))
- d_patches: bfloat16 [512, 128, 640], P(('dp', 'enc'))
- grad_qkv: float32 [640, 1920], P(None, 'enc')
- grad_out: float32 [640, 640], P(None, 'enc')
Inputs may be any that keep to these rules, and one draw needn't show every extreme that they name: `lengths`: each group of 32 images holds one image of exactly 128 patches. Within a group the positions offsets[i] to offsets[i] + lengths[i] - 1 of different images never meet, and offsets[i] + 128 <= 8192.
All inputs are finite; a program needn't handle non-finite values.
Results may differ from a plain program's by a relative error of at most 0.02.
The roundings to bfloat16 on the way count: a program that leaves them out, or rounds other values in their place, can miss the bound.
Values may be sent and summed in bfloat16 or wider, within the bound.
No kernel may reach another device: no remote copies, remote signals or barrier semaphores. Data moves between devices by JAX's collectives and lax.ppermute only.
A program may use at most 64 MiB of HBM per device.

v0:
```python
import math

import jax
import jax.numpy as jnp
from jax import lax
from jax.sharding import PartitionSpec as P

HEADS = 8
HEAD_DIM = 80


def lowered(term):
    return lax.optimization_barrier(term.astype(jnp.bfloat16)).astype(jnp.float32)


def normalize(patch_block):
    values_f = patch_block.astype(jnp.float32)
    inverse = lax.rsqrt(jnp.mean(values_f * values_f, axis=-1, keepdims=True) + 1e-06)
    return (values_f, inverse, (values_f * inverse).astype(jnp.bfloat16))


def attention_weights(queries, keys_in, allowed):
    scores = jnp.einsum(
        "gqhe,gkhe->ghqk", queries, keys_in, preferred_element_type=jnp.float32
    ) * HEAD_DIM ** (-0.5)
    allowed = allowed[:, None]
    scores = jnp.where(allowed, scores, -1e30)
    highest = jnp.max(scores, axis=-1, keepdims=True)
    weights = jnp.where(allowed, jnp.exp(scores - highest), 0.0)
    return weights / jnp.sum(weights, axis=-1, keepdims=True)


def attend_forward(head_inputs, allowed):
    queries, keys_in, values_in = head_inputs
    weights_low = attention_weights(queries, keys_in, allowed).astype(jnp.bfloat16)
    return jnp.einsum(
        "ghqk,gkhe->gqhe", weights_low, values_in, preferred_element_type=jnp.float32
    ).astype(jnp.bfloat16)


def attend_backward(head_inputs, allowed):
    queries, keys_in, values_in, d_context = head_inputs
    weights = attention_weights(queries, keys_in, allowed)
    weights_low = weights.astype(jnp.bfloat16)
    d_weights = jnp.einsum(
        "gqhe,gkhe->ghqk", d_context, values_in, preferred_element_type=jnp.float32
    )
    d_values = jnp.einsum(
        "ghqk,gqhe->gkhe", weights_low, d_context, preferred_element_type=jnp.float32
    )
    d_scores = (
        weights
        * (d_weights - jnp.sum(d_weights * weights, axis=-1, keepdims=True))
        * HEAD_DIM ** (-0.5)
    ).astype(jnp.bfloat16)
    d_queries = jnp.einsum("ghqk,gkhe->gqhe", d_scores, keys_in, preferred_element_type=jnp.float32)
    d_keys = jnp.einsum("ghqk,gqhe->gkhe", d_scores, queries, preferred_element_type=jnp.float32)
    return (d_queries, d_keys, d_values)


def attend(step_fn, head_inputs, present):
    return step_fn(head_inputs, present[:, None, :])


def local(patches, lengths, offsets, w_qkv, w_out, d_embeds):
    slot_count, capacity, feature_count = patches.shape
    owners = lax.axis_size("enc")
    my_index = lax.axis_index("enc")
    row_count = slot_count * capacity
    own_lengths = lax.dynamic_slice_in_dim(lengths, my_index * slot_count, slot_count)
    own_offsets = lax.dynamic_slice_in_dim(offsets, my_index * slot_count, slot_count)
    qkv_full, out_full = (
        lax.all_gather(w_qkv, "enc", axis=1, tiled=True),
        lax.all_gather(w_out, "enc", axis=1, tiled=True),
    )
    values_f, inverse, normed = normalize(patches)
    normed_rows = normed.reshape(row_count, feature_count)
    projected = jnp.dot(normed_rows, qkv_full, preferred_element_type=jnp.float32).astype(
        jnp.bfloat16
    )
    projected = projected.reshape(slot_count, capacity, 3, HEADS, HEAD_DIM)
    head_inputs = (projected[:, :, 0], projected[:, :, 1], projected[:, :, 2])
    slot_iota = lax.broadcasted_iota(jnp.int32, (slot_count, capacity), 1)
    present = slot_iota < own_lengths[:, None]
    context = attend(attend_forward, head_inputs, present).reshape(row_count, HEADS * HEAD_DIM)
    layer_out = values_f + jnp.dot(context, out_full, preferred_element_type=jnp.float32).reshape(
        slot_count, capacity, feature_count
    )
    outgoing = jnp.where(present[:, :, None], layer_out, 0.0).astype(jnp.bfloat16)
    per_owner = capacity // owners
    owner_ids = lax.broadcasted_iota(jnp.int32, (slot_count, owners, per_owner), 1)
    within = lax.broadcasted_iota(jnp.int32, (slot_count, owners, per_owner), 2)
    source_rows = within * owners + (owner_ids - own_offsets[:, None, None]) % owners
    sending = jnp.take_along_axis(
        outgoing, source_rows.reshape(slot_count, owners * per_owner, 1), axis=1
    )
    arrived = lax.all_to_all(
        sending.reshape(slot_count, owners, per_owner, feature_count),
        "enc",
        split_axis=1,
        concat_axis=1,
        tiled=True,
    )
    group_offsets = offsets.reshape(owners, slot_count).T
    first_row = (group_offsets + (my_index - group_offsets) % owners) // owners
    target_rows = (first_row[:, :, None] + within).reshape(-1)
    embeds = (
        jnp.zeros(d_embeds.shape, jnp.bfloat16)
        .at[target_rows]
        .add(arrived.reshape(-1, feature_count))
    )
    returning = d_embeds[target_rows].reshape(slot_count, owners, per_owner, feature_count)
    came_back = lax.all_to_all(returning, "enc", split_axis=1, concat_axis=1, tiled=True)
    positions = own_offsets[:, None] + slot_iota
    pick_rows = positions % owners * per_owner + slot_iota // owners
    grad_rows = jnp.take_along_axis(
        came_back.reshape(slot_count, owners * per_owner, feature_count),
        pick_rows[:, :, None],
        axis=1,
    )
    grad_rows = jnp.where(present[:, :, None], grad_rows, jnp.zeros((), jnp.bfloat16))
    grad_flat = grad_rows.reshape(row_count, feature_count)
    d_context = jnp.dot(grad_flat, out_full.T, preferred_element_type=jnp.float32).astype(
        jnp.bfloat16
    )
    out_term = lowered(jnp.dot(context.T, grad_flat, preferred_element_type=jnp.float32))
    backward_inputs = head_inputs + (d_context.reshape(slot_count, capacity, HEADS, HEAD_DIM),)
    d_parts = attend(attend_backward, backward_inputs, present)
    d_qkv = jnp.stack(d_parts, axis=2).astype(jnp.bfloat16).reshape(row_count, 3 * HEADS * HEAD_DIM)
    qkv_term = lowered(jnp.dot(normed_rows.T, d_qkv, preferred_element_type=jnp.float32))
    qkv_share, out_share = (
        lax.psum_scatter(
            qkv_term.astype(jnp.bfloat16), "enc", scatter_dimension=1, tiled=True
        ).astype(jnp.float32),
        lax.psum_scatter(
            out_term.astype(jnp.bfloat16), "enc", scatter_dimension=1, tiled=True
        ).astype(jnp.float32),
    )
    d_normed = jnp.dot(d_qkv, qkv_full.T, preferred_element_type=jnp.float32).reshape(
        slot_count, capacity, feature_count
    )
    d_inputs = grad_rows.astype(jnp.float32) + inverse * (
        d_normed
        - values_f * inverse * inverse * jnp.mean(d_normed * values_f, axis=-1, keepdims=True)
    )
    qkv_total, out_total = lax.psum((qkv_share, out_share), "dp")
    factor = 1.0 / math.sqrt(row_count * owners * lax.axis_size("dp"))
    return (embeds, d_inputs.astype(jnp.bfloat16), qkv_total * factor, out_total * factor)


def solution(mesh):
    return jax.shard_map(
        local,
        mesh=mesh,
        in_specs=(
            P(("dp", "enc"), None, None),
            P("dp"),
            P("dp"),
            P(None, "enc"),
            P(None, "enc"),
            P(("dp", "enc"), None),
        ),
        out_specs=(
            P(("dp", "enc"), None),
            P(("dp", "enc"), None, None),
            P(None, "enc"),
            P(None, "enc"),
        ),
        check_vma=False,
    )
```

profile of v0, /device:TPU:1, one launch (start us, length us, event | category | flops | bytes accessed | tf_op | source)
XLA Modules:
  0.0 414.3 jit_solution(4378696136195114668)
XLA Ops:
  7.2 0.7 all-gather.4.cloned.1.call-update
  7.9 0.7 and_select_fusion.3
  8.9 0.9 gather_fusion
  9.8 0.7 reshape.517
  10.5 10.5 %all-to-all-start.1 = ((bf16[1,32,4,640]{3,2,0,1:T(4,128)(2,1)}), bf16[1,32,4,640]{3,2,0,1:T(4,128)(2,1)S(1)}, u32[]{:S(2)}, u32[]{:S(2)}) async-start(bf16[1,32,4,640]{3,2,0,1:T(4,128)(2,1)} %bitcast.22), calls=%async_computation.1 | async-start | bytes 327680 | tf_op jit(solution)/shard_map/all_to_all | solution.py:113
  21.1 1.3 dynamic_slice.7
  22.4 1.2 dynamic_slice.6
  23.6 40.7 %all-gather.1 = bf16[32,20,640]{2,1,0:T(8,128)(2,1)S(1)} all-gather(bf16[1,20,640]{2,1,0:T(8,128)(2,1)} %bitcast.139), channel_id=1, replica_groups=mesh['dp'=16,'enc'=32] {'enc'}, dimensions={0}, use_global_device_ids=true | all-gather | bytes 844800 | tf_op jit(solution)/shard_map/all_gather | solution.py:74
  64.3 0.2 reshape.564
  64.5 0.6 fusion.50
  65.2 0.6 and_bitcast_fusion
  65.8 0.1 fusion.25
  65.9 0.7 iota_compare_fusion
  66.7 0.9 gather_fusion.2
  67.6 0.4 convolution_convert_fusion.3
  67.9 0.8 copy.33
  68.7 28.8 %all-gather.4.cloned.1.call-done = bf16[32,60,640]{2,1,0:T(8,128)(2,1)} async-done(((bf16[1,60,640]{2,1,0:T(8,128)(2,1)}), bf16[32,60,640]{2,1,0:T(8,128)(2,1)}) %all-gather.4.cloned.1.call-update) | async-done | bytes 2457616 | tf_op jit(solution)/shard_map/all_gather | solution.py:73
  97.5 2.7 reshape.562
  100.2 0.9 convolution_convert_fusion.1
  101.1 1.0 copy.29
  102.1 2.2 fusion.62
  104.3 2.1 convolution_convert_fusion.4
  106.4 2.1 convolution_bitcast_fusion.1
  108.5 1.1 fusion.35
  109.6 2.5 convolution_bitcast_fusion.2
  112.1 2.5 convolution_bitcast_fusion.3
  114.6 1.2 maximum_convert_fusion
  115.8 0.8 copy-done.2
  116.6 2.3 convolution_convert_fusion
  118.9 1.4 convolution_convert_fusion.2
  120.4 0.6 iota_subtract_fusion
  121.2 1.3 dynamic-slice
  123.8 1.5 fusion.13
  125.3 0.9 gather_fusion.1
  126.3 0.7 reshape.515
  127.0 5.3 %all-to-all-start = ((bf16[1,32,4,640]{3,2,0,1:T(4,128)(2,1)}), bf16[1,32,4,640]{3,2,0,1:T(4,128)(2,1)S(1)}, u32[]{:S(2)}, u32[]{:S(2)}) async-start(bf16[1,32,4,640]{3,2,0,1:T(4,128)(2,1)} %bitcast.20), calls=%async_computation | async-start | bytes 327680 | tf_op jit(solution)/shard_map/all_to_all | solution.py:97
  132.4 1.7 fusion.26
  134.2 0.9 fusion.24
  135.0 7.0 %all-to-all-done = bf16[1,32,4,640]{3,2,0,1:T(4,128)(2,1)S(1)} async-done(((bf16[1,32,4,640]{3,2,0,1:T(4,128)(2,1)}), bf16[1,32,4,640]{3,2,0,1:T(4,128)(2,1)S(1)}, u32[]{:S(2)}, u32[]{:S(2)}) %all-to-all-start) | async-done | bytes 163872 | tf_op jit(solution)/shard_map/all_to_all | solution.py:97
  142.0 2.2 scatter_custom_fusion
  144.2 144.8 %all-reduce.8.cloned.1.call-done = (bf16[640,1920]{1,0:T(8,128)(2,1)}, bf16[640,640]{1,0:T(8,128)(2,1)}) async-done(((bf16[640,1920]{1,0:T(8,128)(2,1)}, bf16[640,640]{1,0:T(8,128)(2,1)}), (bf16[640,1920]{1,0:T(8,128)(2,1)}, bf16[640,640]{1,0:T(8,128)(2,1)})) %all-reduce.8.cloned.1.call-update) | async-done | bytes 3276816
  289.0 1.8 dynamic-slice_convert_fusion.1
  290.8 1.1 dynamic-slice_convert_fusion
  291.9 50.9 %psum.15 = f32[640,20]{1,0:T(8,128)S(1)} all-reduce(f32[640,20]{1,0:T(8,128)S(1)} %dynamic-slice_convert_fusion), channel_id=1, replica_groups=mesh['dp'=16,'enc'=32] {'dp'}, use_global_device_ids=true, to_apply=%region_9.11 | all-reduce | flops 12800 | bytes 102400 | tf_op jit(solution)/shard_map/psum | solution.py:146
  342.9 0.8 copy.38
  343.7 62.3 %all-reduce.6.cloned.1.call-done = f32[640,60]{1,0:T(8,128)} async-done(((f32[640,60]{1,0:T(8,128)}), f32[640,60]{1,0:T(8,128)}) %all-reduce.6.cloned.1.call-update) | async-done | bytes 153616 | tf_op jit(solution)/shard_map/psum | solution.py:146
  406.0 1.0 broadcast_multiply_fusion.1
  407.0 0.8 copy.37
  (42 shorter events, 0.9 us)
Async XLA Ops:
  7.2 1.8 copy-start
  7.2 90.3 %all-gather.4.cloned.1.call-start = ((), (), s32[]{:S(2)}) async-start(), calls=%async_computation.3 | async-start | bytes 2703360 | tf_op jit(solution)/shard_map/all_gather | solution.py:73
  8.9 56.9 %copy-start.1 = (bf16[1,128,640]{2,1,0:T(8,128)(2,1)S(1)}, bf16[1,128,640]{2,1,0:T(8,128)(2,1)}, u32[]{:S(2)}) copy-start(bf16[1,128,640]{2,1,0:T(8,128)(2,1)} %param.8) | copy-start | bytes 491524
  10.5 56.1 %all-to-all-start.1 = ((bf16[1,32,4,640]{3,2,0,1:T(4,128)(2,1)}), bf16[1,32,4,640]{3,2,0,1:T(4,128)(2,1)S(1)}, u32[]{:S(2)}, u32[]{:S(2)}) async-start(bf16[1,32,4,640]{3,2,0,1:T(4,128)(2,1)} %bitcast.22), calls=%async_computation.1 | async-start | bytes 327680 | tf_op jit(solution)/shard_map/all_to_all | solution.py:113
  21.0 268.0 %all-reduce.8.cloned.1.call-start = ((), (), s32[]{:S(2)}) async-start(), calls=%async_computation.4 | async-start | bytes 6553600
  64.5 4.2 %copy-start.3 = (bf16[640,640]{1,0:T(8,128)(2,1)}, bf16[640,640]{1,0:T(8,128)(2,1)S(1)}, u32[]{:S(2)}) copy-start(bf16[640,640]{1,0:T(8,128)(2,1)S(1)} %reshape.564) | copy-start | bytes 2457604
  67.6 1.2 copy-start.4
  102.1 6.4 %copy-start.6 = (bf16[128,1920]{0,1:T(8,128)(2,1)S(1)}, bf16[128,1920]{0,1:T(8,128)(2,1)}, u32[]{:S(2)}) copy-start(bf16[128,1920]{0,1:T(8,128)(2,1)} %copy.29) | copy-start | bytes 1474564
  104.3 4.2 %copy-start.7 = (bf16[128,640]{0,1:T(8,128)(2,1)S(1)}, bf16[128,640]{0,1:T(8,128)(2,1)}, u32[]{:S(2)}) copy-start(bf16[128,640]{0,1:T(8,128)(2,1)} %copy.33) | copy-start | bytes 491524
  114.6 4.3 %copy-start.5 = (bf16[128,640]{1,0:T(8,128)(2,1)S(1)}, bf16[128,640]{1,0:T(8,128)(2,1)}, u32[]{:S(2)}) copy-start(bf16[128,640]{1,0:T(8,128)(2,1)} %copy-done.4) | copy-start | bytes 491524
  114.6 4.3 %copy-start.8 = (bf16[8,80,128]{2,1,0:T(8,128)(2,1)S(1)}, bf16[8,80,128]{2,1,0:T(8,128)(2,1)}, u32[]{:S(2)}) copy-start(bf16[8,80,128]{2,1,0:T(8,128)(2,1)} %convolution_convert_fusion.4) | copy-start | bytes 491524
  115.8 0.8 copy-start.2
  127.0 15.0 %all-to-all-start = ((bf16[1,32,4,640]{3,2,0,1:T(4,128)(2,1)}), bf16[1,32,4,640]{3,2,0,1:T(4,128)(2,1)S(1)}, u32[]{:S(2)}, u32[]{:S(2)}) async-start(bf16[1,32,4,640]{3,2,0,1:T(4,128)(2,1)} %bitcast.20), calls=%async_computation | async-start | bytes 327680 | tf_op jit(solution)/shard_map/all_to_all | solution.py:97
  132.4 273.6 %all-reduce.6.cloned.1.call-start = ((), (), s32[]{:S(2)}) async-start(), calls=%async_computation.2 | async-start | bytes 655360 | tf_op jit(solution)/shard_map/psum | solution.py:146
Sparse Core Ops, SparseCore 0:
  11.2 86.2 all-gather.3
  120.4 168.5 all-reduce.7
  291.5 114.4 all-reduce.5
where the time goes:
time: 415 us; the launch traced here: 414 us
  waiting for transfers between devices  244 us (59%)
  blocking collectives  91.6 us (22%)
  matrix products  20.8 us (5%)
  starting transfers between devices  15.9 us (4%)
  local copies, waits for them, and re-layouts  15.5 us (4%)
  between operations  15.3 us (4%)
  other arithmetic  11.6 us (3%)
    unnamed x4, waiting for transfers between devices  146 us
    psum x1, waiting for transfers between devices, local(): qkv_total, out_total = lax.psum((qkv_share, out_share), 'dp')  62.3 us
    psum x1, blocking collectives, local(): qkv_total, out_total = lax.psum((qkv_share, out_share), 'dp')  50.9 us
    all_gather x1, blocking collectives, local(): lax.all_gather(w_out, 'enc', axis=1, tiled=True)  40.7 us
    all_gather x1, waiting for transfers between devices, local(): lax.all_gather(w_qkv, 'enc', axis=1, tiled=True)  28.8 us
    all_to_all x1, starting transfers between devices, local(): lax.all_to_all(returning, 'enc', split_axis=1, concat_axis=1, tiled=True)  10.5 us
  transfers between devices with their start and end apart: 5, of which 4 were waited for; matrix products, arithmetic and copies ran while one was open for 5% of the time, Pallas kernels for 0%

commit v1 on v0

v1 whole, which is shorter than its diff:
```python
import functools
import math

import jax
import jax.numpy as jnp
from jax import lax
from jax.experimental import pallas as pl
from jax.experimental.pallas import tpu as pltpu
from jax.sharding import Mesh, PartitionSpec as P

HEADS = 8
HEAD_DIM = 80
D = 640
CAP = 128
NX, NY, NZ = 4, 8, 8
OWNERS = NX * NY
QP, OP = 30, 10
PIECE = QP + OP
ROWS = NY * PIECE
W_EMB = CAP // OWNERS
EX = NY * W_EMB
EY = NX * W_EMB
SCALE = HEAD_DIM ** (-0.5)
BF = jnp.bfloat16
F32 = jnp.float32
VMEM_LIMIT = 56 * 1024 * 1024

PIECES = [(x, y) for x in range(NX) for y in range(NY)]


def dot(a, b, ca, cb):
    return lax.dot_general(a, b, (((ca,), (cb,)), ((), ())), preferred_element_type=F32)


def call(kernel, out_shape, scratch, *args, smem=1):
    specs = [pl.BlockSpec(memory_space=pltpu.SMEM)] * smem + [
        pl.BlockSpec(memory_space=pltpu.VMEM)
    ] * (len(args) - smem)
    return pl.pallas_call(
        kernel,
        out_shape=out_shape,
        in_specs=specs,
        out_specs=jax.tree.map(lambda _: pl.BlockSpec(memory_space=pltpu.VMEM), out_shape),
        scratch_shapes=scratch,
        compiler_params=pltpu.CompilerParams(vmem_limit_bytes=VMEM_LIMIT),
    )(*args)


def sds(shape, dtype=BF):
    return jax.ShapeDtypeStruct(shape, dtype)


def target_rows(offsets, owner, within):
    return ((offsets + ((owner - offsets) & (OWNERS - 1))) >> 5) + within


def pre_kernel(info, offs, d_embeds, wq, wo, send, fq, fo):
    core, owner = info[0], info[1]
    seq_rows = d_embeds.shape[0]
    shape = (CAP, seq_rows)
    within = lax.broadcasted_iota(jnp.int32, (CAP, 1), 0) & (W_EMB - 1)
    rows = target_rows(offs[...], owner, within)
    pick = (lax.broadcasted_iota(jnp.int32, shape, 1) == rows).astype(F32).astype(BF)
    fetched = dot(pick, d_embeds[...], 1, 0).astype(BF)
    fq[...] = wq[...].astype(F32)
    fo[...] = wo[...].astype(F32)
    first = core == 0
    half_q = jnp.where(first, fq[0:QP], fq[QP : 2 * QP])
    half_o = jnp.where(first, fo[0:OP], fo[OP : 2 * OP])
    fq[0:QP] = half_q
    fq[QP:PIECE] = half_o
    piece = fq[0:PIECE].astype(BF)
    for y in range(NY):
        send[y, 0:EY] = fetched[y * EY : (y + 1) * EY]
        send[y, EY : EY + PIECE] = piece


def normalize(patches):
    values_f = patches[...].astype(F32)
    inverse = lax.rsqrt(jnp.mean(values_f * values_f, axis=-1, keepdims=True) + 1e-06)
    return values_f, inverse, (values_f * inverse).astype(BF)


def fwd_kernel(
    info, patches, own, other, going, qkv_t, prob, ctx_t, pa, pb, qf, layer_t
):
    core, length, offset = info[0], info[2], info[3]
    first = core == 0
    values_f, _, normed = normalize(patches)
    for x in range(NX):
        block = slice(x * ROWS, (x + 1) * ROWS)
        pa[block] = dot(own[x, EX:], normed, 1, 1)
        pb[block] = dot(other[x, EX:], normed, 1, 1)
    for n, (x, y) in enumerate(PIECES):
        low, dest = n * PIECE, 2 * QP * (NX * y + x)
        mine, theirs = pa[low : low + QP], pb[low : low + QP]
        qf[dest : dest + QP] = jnp.where(first, mine, theirs)
        qf[dest + QP : dest + 2 * QP] = jnp.where(first, theirs, mine)
    qkv_t[...] = qf[...].astype(BF)
    allowed = lax.broadcasted_iota(jnp.int32, (CAP, CAP), 1) < length
    for h in range(HEADS):
        q, k, v = (
            qkv_t[pl.ds(part * D + h * HEAD_DIM, HEAD_DIM), :] for part in range(3)
        )
        scores = jnp.where(allowed, dot(q, k, 0, 0) * SCALE, -1e30)
        highest = jnp.max(scores, axis=-1, keepdims=True)
        weights = jnp.where(allowed, jnp.exp(scores - highest), 0.0)
        weights = weights / jnp.sum(weights, axis=-1, keepdims=True)
        prob[h] = weights
        ctx_t[pl.ds(h * HEAD_DIM, HEAD_DIM), :] = dot(v, weights.astype(BF), 1, 1).astype(BF)
    context = ctx_t[...]
    for x in range(NX):
        block = slice(x * ROWS, (x + 1) * ROWS)
        pa[block] = dot(own[x, EX:], context, 1, 0)
        pb[block] = dot(other[x, EX:], context, 1, 0)
    for n, (x, y) in enumerate(PIECES):
        low, dest = n * PIECE + QP, 2 * OP * (NX * y + x)
        mine, theirs = pa[low : low + OP], pb[low : low + OP]
        layer_t[dest : dest + OP] = jnp.where(first, mine, theirs)
        layer_t[dest + OP : dest + 2 * OP] = jnp.where(first, theirs, mine)
    layer_out = values_f + layer_t[...].T
    slot = lax.broadcasted_iota(jnp.int32, (CAP, 1), 0)
    outgoing = jnp.where(slot < length, layer_out, 0.0).astype(BF)
    row = lax.broadcasted_iota(jnp.int32, (CAP, CAP), 0)
    x, y, w = row >> 5, (row >> 2) & 7, row & 3
    source = w * OWNERS + ((NX * y + x - offset) & (OWNERS - 1))
    order = (lax.broadcasted_iota(jnp.int32, (CAP, CAP), 1) == source).astype(F32).astype(BF)
    going[...] = dot(order, outgoing, 1, 0).astype(BF)


def bwd_kernel(
    info, patches, own, other, qkv_t, prob, ctx_t, going,
    part_own, part_other, d_patches, grad_t, dq, la, lb,
):
    core, length, offset = info[0], info[2], info[3]
    first = core == 0
    values_f, inverse, normed = normalize(patches)
    came = jnp.concatenate([own[x, 0:EX] for x in range(NX)], axis=0)
    slot = lax.broadcasted_iota(jnp.int32, (CAP, CAP), 0)
    owner = (slot + offset) & (OWNERS - 1)
    source = (owner & 3) * EX + (owner >> 2) * W_EMB + (slot >> 5)
    column = lax.broadcasted_iota(jnp.int32, (CAP, CAP), 1)
    pick = ((column == source) & (slot < length)).astype(F32).astype(BF)
    grad_f = dot(pick, came, 1, 0)
    grad_t[...] = grad_f.T
    la[...] = jnp.zeros_like(la)
    lb[...] = jnp.zeros_like(lb)
    for n, (x, y) in enumerate(PIECES):
        low, src = n * PIECE + QP, 2 * OP * (NX * y + x)
        one, two = grad_t[src : src + OP], grad_t[src + OP : src + 2 * OP]
        la[low : low + OP, CAP:] = jnp.where(first, one, two)
        lb[low : low + OP, CAP:] = jnp.where(first, two, one)

    def back(ref, lanes):
        total = None
        for half, weights in ((la, own), (lb, other)):
            for x in range(NX):
                left = half[x * ROWS : (x + 1) * ROWS, lanes].T.astype(BF)
                term = dot(left, weights[x, EX:], 1, 0)
                total = term if total is None else total + term
        return total

    d_ctx_t = back(None, slice(CAP, 2 * CAP)).astype(BF).astype(F32).T.astype(BF)
    for h in range(HEADS):
        at = [pl.ds(part * D + h * HEAD_DIM, HEAD_DIM) for part in range(3)]
        q, k, v = (qkv_t[rows, :] for rows in at)
        dc = d_ctx_t[h * HEAD_DIM : (h + 1) * HEAD_DIM]
        weights = prob[h]
        d_prob = dot(dc, v, 0, 0)
        dq[at[2], :] = dot(dc, weights.astype(BF), 1, 0)
        inner = jnp.sum(d_prob * weights, axis=-1, keepdims=True)
        d_scores = (weights * (d_prob - inner) * SCALE).astype(BF)
        dq[at[0], :] = dot(k, d_scores, 1, 1)
        dq[at[1], :] = dot(q, d_scores, 1, 0)
    for n, (x, y) in enumerate(PIECES):
        low, src = n * PIECE, 2 * QP * (NX * y + x)
        one, two = dq[src : src + QP], dq[src + QP : src + 2 * QP]
        la[low : low + QP, 0:CAP] = jnp.where(first, one, two)
        lb[low : low + QP, 0:CAP] = jnp.where(first, two, one)
    context = ctx_t[...].astype(F32).T.astype(BF)
    right = jnp.concatenate([normed, context], axis=0)
    for x in range(NX):
        block = slice(x * ROWS, (x + 1) * ROWS)
        part_own[x, 0:EX] = going[x * EX : (x + 1) * EX]
        part_other[x, 0:EX] = jnp.zeros((EX, D), BF)
        part_own[x, EX:] = dot(la[block].astype(BF), right, 1, 0).astype(BF)
        part_other[x, EX:] = dot(lb[block].astype(BF), right, 1, 0).astype(BF)
    d_normed = back(None, slice(0, CAP))
    d_patches[...] = (
        grad_f
        + inverse
        * (
            d_normed
            - values_f * inverse * inverse * jnp.mean(d_normed * values_f, axis=-1, keepdims=True)
        )
    ).astype(BF)


def place_kernel(info, offs, came, embeds):
    owner = info[1]
    rows = jnp.concatenate([came[y, 0:EY] for y in range(NY)], axis=0)
    within = lax.broadcasted_iota(jnp.int32, (1, CAP), 1) & (W_EMB - 1)
    target = target_rows(offs[...], owner, within)
    shape = (embeds.shape[0], CAP)
    place = (lax.broadcasted_iota(jnp.int32, shape, 0) == target).astype(F32).astype(BF)
    embeds[...] = dot(place, rows, 1, 0).astype(BF)


def swap(a):
    return lax.ppermute(a, "core", [(0, 1), (1, 0)])


def exchange(a, axis):
    return lax.all_to_all(a, axis, split_axis=0, concat_axis=0, tiled=True)


def local(patches, lengths, offsets, w_qkv, w_out, d_embeds):
    core = lax.axis_index("core")
    owner = lax.axis_index("y") * NX + lax.axis_index("x")
    seq_rows = d_embeds.shape[0]
    info = jnp.stack([core, owner, lengths[owner], offsets[owner]]).astype(jnp.int32)
    offs = jnp.repeat(offsets, W_EMB)
    tokens = patches.reshape(CAP, D)

    send = call(
        pre_kernel,
        sds((NY, EY + PIECE, D)),
        [pltpu.VMEM((2 * QP, D), F32), pltpu.VMEM((2 * OP, D), F32)],
        info, offs.reshape(CAP, 1), d_embeds, w_qkv.T, w_out.T,
    )
    got = exchange(send, "y")
    rows = got[:, :EY].reshape(NY, NX, W_EMB, D).transpose(1, 0, 2, 3).reshape(NX, EX, D)
    shards = jnp.broadcast_to(got[:, EY:].reshape(1, ROWS, D), (NX, ROWS, D))
    own = exchange(jnp.concatenate([rows, shards], axis=1), "x")
    other = swap(own)

    pieces = NX * ROWS
    going, qkv_t, prob, ctx_t = call(
        fwd_kernel,
        (sds((CAP, D)), sds((3 * D, CAP)), sds((HEADS, CAP, CAP), F32), sds((D, CAP))),
        [
            pltpu.VMEM((pieces, CAP), F32),
            pltpu.VMEM((pieces, CAP), F32),
            pltpu.VMEM((3 * D, CAP), F32),
            pltpu.VMEM((D, CAP), F32),
        ],
        info, tokens, own, other,
    )
    part_own, part_other, d_patches = call(
        bwd_kernel,
        (sds((NX, EX + ROWS, D)), sds((NX, EX + ROWS, D)), sds((CAP, D))),
        [
            pltpu.VMEM((D, CAP), F32),
            pltpu.VMEM((3 * D, CAP), F32),
            pltpu.VMEM((pieces, 2 * CAP), F32),
            pltpu.VMEM((pieces, 2 * CAP), F32),
        ],
        info, tokens, own, other, qkv_t, prob, ctx_t, going,
    )

    pair = (part_own.astype(F32) + swap(part_other).astype(F32)).astype(BF)
    got = exchange(pair, "x")
    rows = got[:, :EX].reshape(NX, NY, W_EMB, D).transpose(1, 0, 2, 3).reshape(NY, EY, D)
    total = jnp.sum(got[:, EX:].astype(F32), axis=0).astype(BF).reshape(NY, PIECE, D)
    got = exchange(jnp.concatenate([rows, total], axis=1), "y")
    embeds = call(
        place_kernel, sds((seq_rows, D)), [], info, offs.reshape(1, CAP), got
    )
    total = jnp.sum(got[:, EY:].astype(F32), axis=0).astype(BF)
    got = exchange(jnp.broadcast_to(total[None], (NZ, PIECE, D)), "z")
    factor = 1.0 / math.sqrt(CAP * OWNERS * 2 * NZ)
    mine = jnp.sum(got.astype(F32), axis=0) * factor
    theirs = swap(mine)
    low, high = jnp.where(core == 0, mine, theirs), jnp.where(core == 0, theirs, mine)
    grad_qkv = jnp.concatenate([low[:QP], high[:QP]], axis=0).T
    grad_out = jnp.concatenate([low[QP:], high[QP:]], axis=0).T
    return embeds, d_patches.reshape(patches.shape), grad_qkv, grad_out


def solution(mesh):
    axes = Mesh(mesh.devices.reshape(NZ, 2, NY, NX), ("z", "core", "y", "x"))
    group, plane = ("z", "core"), ("y", "x")
    return jax.shard_map(
        local,
        mesh=axes,
        in_specs=(
            P(group + plane, None, None),
            P(group),
            P(group),
            P(None, plane),
            P(None, plane),
            P(group + plane, None),
        ),
        out_specs=(
            P(group + plane, None),
            P(group + plane, None, None),
            P(None, plane),
            P(None, plane),
        ),
        check_vma=False,
    )
```

time: 415 us -> 170 us (0.41)
  waiting for transfers between devices: 244 us -> 6.9 us
  blocking collectives: 91.6 us -> 115 us
  matrix products: 20.8 us -> 0 us
  Pallas kernels: 0 us -> 20.4 us
  between operations: 15.3 us -> 0.81 us
  local copies, waits for them, and re-layouts: 15.5 us -> 6.3 us
  other arithmetic: 11.6 us -> 5.73 us
    unnamed x4 -> x0, waiting for transfers between devices: 146 us -> none
    all_to_all x0 -> x5, blocking collectives: none -> 115 us  [exchange(): return lax.all_to_all(a, axis, split_axis=0, concat_axis=0, tiled=True)]
    psum x1 -> x0, waiting for transfers between devices: 62.3 us -> none  [local(): qkv_total, out_total = lax.psum((qkv_share, out_share), 'dp')]
    psum x1 -> x0, blocking collectives: 50.9 us -> none  [local(): qkv_total, out_total = lax.psum((qkv_share, out_share), 'dp')]
    all_gather x1 -> x0, blocking collectives: 40.7 us -> none  [local(): lax.all_gather(w_out, 'enc', axis=1, tiled=True)]
    all_gather x1 -> x0, waiting for transfers between devices: 28.8 us -> none  [local(): lax.all_gather(w_qkv, 'enc', axis=1, tiled=True)]
    pallas_call x0 -> x4, Pallas kernels: none -> 20.4 us  [call(): pl.pallas_call(kernel, out_shape=out_shape, in_specs=specs, out_specs=jax...]
    dot_general x11 -> x0, matrix products: 18.5 us -> none  [the longest x1 2.53 us: attend_backward(): jnp.einsum('ghqk,gqhe->gkhe', d_scores, queries, preferred_element_type=j...]
  transfers between devices with their start and end apart: 5 -> 3, of which waited for: 4 -> 2; matrix products, arithmetic and copies ran while one was open for 5% -> 0% of each run, Pallas kernels for 0% -> 1%
where the time goes in v1:
time: 170 us; the launch traced here: 169 us
  blocking collectives  115 us (68%)
  Pallas kernels  20.4 us (12%)
  starting transfers between devices  14.6 us (9%)
  waiting for transfers between devices  6.9 us (4%)
  local copies, waits for them, and re-layouts  6.3 us (4%)
  other arithmetic  5.73 us (3%)
    all_to_all x5, blocking collectives, exchange(): return lax.all_to_all(a, axis, split_axis=0, concat_axis=0, tiled=True)  115 us
    pallas_call x4, Pallas kernels, call(): pl.pallas_call(kernel, out_shape=out_shape, in_specs=specs, out_specs=jax...  20.4 us
    ppermute x3, starting transfers between devices, swap(): return lax.ppermute(a, 'core', [(0, 1), (1, 0)])  14.6 us
    ppermute x3, waiting for transfers between devices, swap(): return lax.ppermute(a, 'core', [(0, 1), (1, 0)])  6.9 us
  transfers between devices with their start and end apart: 3, of which 2 were waited for; matrix products, arithmetic and copies ran while one was open for 0% of the time, Pallas kernels for 1%

profile of v1, /device:TPU:1, one launch (start us, length us, event | category | flops | bytes accessed | tf_op | source)
XLA Modules:
  0.0 169.3 jit_solution(14571983122878372894)
XLA Ops:
  0.6 1.2 dynamic_slice.7
  1.9 1.2 dynamic_slice.6
  3.1 0.7 broadcast_in_dim.16
  3.8 0.7 reshape_reshape.8.offs
  4.6 1.9 %pad_add_fusion.info = s32[4]{0:T(128)} fusion(s32[1]{0:T(128)} %dynamic_slice.7, s32[1]{0:T(128)} %dynamic_slice.6, s32[1]{0:T(128)} %bitcast.1, s32[1]{0:T(128)} %bitcast), kind=kLoop, calls=%fused_computation.13 | loop fusion | flops 12 | bytes 32 | tf_op jit(solution)/shard_map/stack | solution.py:221
  6.4 2.1 %shard_map.93 = bf16[8,56,640]{2,1,0:T(8,128)(2,1)} custom-call(s32[4]{0:T(128)} %pad_add_fusion.info, s32[128,1]{1,0:T(8,128)} %reshape_reshape.8.offs, bf16[256,640]{1,0:T(8,128)(2,1)} %d_embeds.1, bf16[60,640]{1,0:T(8,128)(2,1)} %bitcast.24, bf16[20,640]{1,0:T(8,128)(2,1)} %bitcast.25), custom_call_target="tpu_custom_call" | custom-call | tf_op jit(solution)/shard_map/pallas_call | solution.py:39
  8.5 23.0 %all_to_all.25 = bf16[8,56,640]{2,1,0:T(8,128)(2,1)S(1)} all-to-all(bf16[8,56,640]{2,1,0:T(8,128)(2,1)} %shard_map.93), channel_id=1, replica_groups=mesh['z'=8,'core'=2,'y'=8,'x'=4] {'y'}, dimensions={0} | all-to-all | bytes 1146880 | tf_op jit(solution)/shard_map/all_to_all | solution.py:214
  31.5 0.1 copy.22
  31.7 0.1 broadcast_in_dim.18
  31.8 0.2 pad_maximum_fusion
  32.0 25.5 %all_to_all.26.own = bf16[4,352,640]{2,1,0:T(8,128)(2,1)S(1)} all-to-all(bf16[4,352,640]{2,1,0:T(8,128)(2,1)S(1)} %pad_maximum_fusion), channel_id=1, replica_groups=mesh['z'=8,'core'=2,'y'=8,'x'=4] {'x'}, dimensions={0} | all-to-all | bytes 3604480 | tf_op jit(solution)/shard_map/all_to_all | solution.py:214
  57.5 0.0 copy-start
  57.5 5.8 %collective-permute-start = (bf16[4,352,640]{2,1,0:T(8,128)(2,1)S(1)}, bf16[4,352,640]{2,1,0:T(8,128)(2,1)S(1)}, u32[]{:S(2)}, u32[]{:S(2)}) collective-permute-start(bf16[4,352,640]{2,1,0:T(8,128)(2,1)S(1)} %all_to_all.26.own), channel_id=1, source_target_pairs={{0,32},{32,0},{1,33},{33,1},{2,34},{34,2},{3,35},{35,3},{4,36},{36... | collective-permute-start | bytes 5406728 | tf_op jit(solution)/shard_map/ppermute | solution.py:210
  63.3 3.3 %collective-permute-done.other = bf16[4,352,640]{2,1,0:T(8,128)(2,1)S(1)} collective-permute-done((bf16[4,352,640]{2,1,0:T(8,128)(2,1)S(1)}, bf16[4,352,640]{2,1,0:T(8,128)(2,1)S(1)}, u32[]{:S(2)}, u32[]{:S(2)}) %collective-permute-start) | collective-permute-done | bytes 1802272 | tf_op jit(solution)/shard_map/ppermute | solution.py:210
  66.7 0.0 copy-start.1
  66.7 0.0 copy-done
  66.7 1.2 copy-done.1
  67.9 6.8 %shard_map.94 = (bf16[128,640]{1,0:T(8,128)(2,1)}, bf16[1920,128]{1,0:T(8,128)(2,1)}, f32[8,128,128]{2,1,0:T(8,128)}, bf16[640,128]{1,0:T(8,128)(2,1)}) custom-call(s32[4]{0:T(128)} %pad_add_fusion.info, bf16[128,640]{1,0:T(8,128)(2,1)} %bitcast.22, bf16[4,352,640]{2,1,0:T(8,128)(2,1)} %copy-done, bf16[4,352,640]{2,1,0:T(8,128)(2,1)} %copy-done.1), custom_call_target="tpu_custom_call" | custom-call | tf_op jit(solution)/shard_map/pallas_call | solution.py:39
  74.7 9.5 %shard_map.95 = (bf16[4,352,640]{2,1,0:T(8,128)(2,1)}, bf16[4,352,640]{2,1,0:T(8,128)(2,1)}, bf16[128,640]{1,0:T(8,128)(2,1)}) custom-call(s32[4]{0:T(128)} %pad_add_fusion.info, bf16[128,640]{1,0:T(8,128)(2,1)} %bitcast.23, bf16[4,352,640]{2,1,0:T(8,128)(2,1)} %copy-done, bf16[4,352,640]{2,1,0:T(8,128)(2,1)} %copy-done.1, ...), custom_call_target="tpu_custom_call" | custom-call | tf_op jit(solution)/shard_map/pallas_call | solution.py:39
  84.2 2.3 %collective-permute-start.1 = (bf16[4,352,640]{2,1,0:T(8,128)(2,1)}, bf16[4,352,640]{2,1,0:T(8,128)(2,1)S(1)}, u32[]{:S(2)}, u32[]{:S(2)}) collective-permute-start(bf16[4,352,640]{2,1,0:T(8,128)(2,1)} %get-tuple-element.16), channel_id=1, source_target_pairs={{0,32},{32,0},{1,33},{33,1},{2,34},{34,2},{3,35},{35,3},{4,36},{36... | collective-permute-start | bytes 5406728 | tf_op jit(solution)/shard_map/ppermute | solution.py:210
  86.4 3.6 %collective-permute-done.1 = bf16[4,352,640]{2,1,0:T(8,128)(2,1)S(1)} collective-permute-done((bf16[4,352,640]{2,1,0:T(8,128)(2,1)}, bf16[4,352,640]{2,1,0:T(8,128)(2,1)S(1)}, u32[]{:S(2)}, u32[]{:S(2)}) %collective-permute-start.1) | collective-permute-done | bytes 1802272 | tf_op jit(solution)/shard_map/ppermute | solution.py:210
  90.0 2.0 %add_convert_fusion = bf16[4,352,640]{2,1,0:T(8,128)(2,1)S(1)} fusion(bf16[4,352,640]{2,1,0:T(8,128)(2,1)S(1)} %collective-permute-done.1, bf16[4,352,640]{2,1,0:T(8,128)(2,1)} %get-tuple-element.15), kind=kLoop, calls=%fused_computation | loop fusion | flops 3604480 | bytes 5406720 | tf_op jit(solution)/shard_map/convert_element_type | solution.py:261
  92.0 25.4 %all_to_all.27 = bf16[4,352,640]{2,1,0:T(8,128)(2,1)S(1)} all-to-all(bf16[4,352,640]{2,1,0:T(8,128)(2,1)S(1)} %add_convert_fusion), channel_id=1, replica_groups=mesh['z'=8,'core'=2,'y'=8,'x'=4] {'x'}, dimensions={0} | all-to-all | bytes 3604480 | tf_op jit(solution)/shard_map/all_to_all | solution.py:214
  117.4 0.1 copy.21
  117.5 0.2 slice_reduce_fusion
  117.8 0.1 pad_maximum_fusion.1
  117.8 19.5 %all_to_all.28.came = bf16[8,56,640]{2,1,0:T(8,128)(2,1)S(1)} all-to-all(bf16[8,56,640]{2,1,0:T(8,128)(2,1)S(1)} %pad_maximum_fusion.1), channel_id=1, replica_groups=mesh['z'=8,'core'=2,'y'=8,'x'=4] {'y'}, dimensions={0} | all-to-all | bytes 1146880 | tf_op jit(solution)/shard_map/all_to_all | solution.py:214
  137.3 0.0 copy-start.2
  137.3 0.1 slice_reduce_fusion.1
  137.4 21.2 %all_to_all.29 = bf16[8,40,640]{2,1,0:T(8,128)(2,1)S(1)} all-to-all(bf16[8,40,640]{2,1,0:T(8,128)(2,1)S(1)} %broadcast_in_dim.19), channel_id=1, replica_groups=mesh['z'=8,'core'=2,'y'=8,'x'=4] {'z'}, dimensions={0} | all-to-all | bytes 819200 | tf_op jit(solution)/shard_map/all_to_all | solution.py:214
  158.6 0.1 convert_reduce_fusion
  158.7 6.6 %collective-permute-start.2 = (f32[40,640]{1,0:T(8,128)S(1)}, f32[40,640]{1,0:T(8,128)S(1)}, u32[]{:S(2)}, u32[]{:S(2)}) collective-permute-start(f32[40,640]{1,0:T(8,128)S(1)} %broadcast_multiply_fusion), channel_id=1, source_target_pairs={{0,32},{32,0},{1,33},{33,1},{2,34},{34,2},{3,35},{35,3},{4,36},{36... | collective-permute-start | bytes 307208 | tf_op jit(solution)/shard_map/ppermute | solution.py:210
  165.3 0.6 reshape_reshape.6.offs
  165.9 0.0 copy-done.2
  165.9 2.0 %shard_map.96 = bf16[256,640]{1,0:T(8,128)(2,1)} custom-call(s32[4]{0:T(128)} %pad_add_fusion.info, s32[1,128]{1,0:T(1,128)} %reshape_reshape.6.offs, bf16[8,56,640]{2,1,0:T(8,128)(2,1)} %copy-done.2), custom_call_target="tpu_custom_call" | custom-call | tf_op jit(solution)/shard_map/pallas_call | solution.py:39
  167.9 0.0 collective-permute-done.2
  168.0 0.6 maximum_bitcast_fusion.1
  168.7 0.7 maximum_bitcast_fusion
  (14 shorter events, 0.3 us)
Async XLA Ops:
  57.5 9.2 %copy-start = (bf16[4,352,640]{2,1,0:T(8,128)(2,1)}, bf16[4,352,640]{2,1,0:T(8,128)(2,1)S(1)}, u32[]{:S(2)}) copy-start(bf16[4,352,640]{2,1,0:T(8,128)(2,1)S(1)} %all_to_all.26.own) | copy-start | bytes 5406724
  57.5 9.2 %collective-permute-start = (bf16[4,352,640]{2,1,0:T(8,128)(2,1)S(1)}, bf16[4,352,640]{2,1,0:T(8,128)(2,1)S(1)}, u32[]{:S(2)}, u32[]{:S(2)}) collective-permute-start(bf16[4,352,640]{2,1,0:T(8,128)(2,1)S(1)} %all_to_all.26.own), channel_id=1, source_target_pairs={{0,32},{32,0},{1,33},{33,1},{2,34},{34,2},{3,35},{35,3},{4,36},{36... | collective-permute-start | bytes 5406728 | tf_op jit(solution)/shard_map/ppermute | solution.py:210
  66.7 1.2 copy-start.1
  84.2 5.8 %collective-permute-start.1 = (bf16[4,352,640]{2,1,0:T(8,128)(2,1)}, bf16[4,352,640]{2,1,0:T(8,128)(2,1)S(1)}, u32[]{:S(2)}, u32[]{:S(2)}) collective-permute-start(bf16[4,352,640]{2,1,0:T(8,128)(2,1)} %get-tuple-element.16), channel_id=1, source_target_pairs={{0,32},{32,0},{1,33},{33,1},{2,34},{34,2},{3,35},{35,3},{4,36},{36... | collective-permute-start | bytes 5406728 | tf_op jit(solution)/shard_map/ppermute | solution.py:210
  137.3 28.5 %copy-start.2 = (bf16[8,56,640]{2,1,0:T(8,128)(2,1)}, bf16[8,56,640]{2,1,0:T(8,128)(2,1)S(1)}, u32[]{:S(2)}) copy-start(bf16[8,56,640]{2,1,0:T(8,128)(2,1)S(1)} %all_to_all.28.came) | copy-start | bytes 1720324
  158.7 9.2 %collective-permute-start.2 = (f32[40,640]{1,0:T(8,128)S(1)}, f32[40,640]{1,0:T(8,128)S(1)}, u32[]{:S(2)}, u32[]{:S(2)}) collective-permute-start(f32[40,640]{1,0:T(8,128)S(1)} %broadcast_multiply_fusion), channel_id=1, source_target_pairs={{0,32},{32,0},{1,33},{33,1},{2,34},{34,2},{3,35},{35,3},{4,36},{36... | collective-permute-start | bytes 307208 | tf_op jit(solution)/shard_map/ppermute | solution.py:210

commit v2 on v1

v2 whole, which is shorter than its diff:
```python
import math

import jax
import jax.numpy as jnp
from jax import lax
from jax.experimental import pallas as pl
from jax.experimental.pallas import tpu as pltpu
from jax.sharding import Mesh, PartitionSpec as P

HEADS = 8
HEAD_DIM = 80
D = 640
CAP = 128
NX, NY, NZ = 4, 8, 8
OWNERS = NX * NY
QP, OP = 30, 10
PIECE = QP + OP
W_EMB = CAP // OWNERS
EX = NY * W_EMB
EY = NX * W_EMB
SCALE = HEAD_DIM ** (-0.5)
BF = jnp.bfloat16
F32 = jnp.float32
VMEM_LIMIT = 20 * 1024 * 1024
TEAM = 2 * NX
QB, OB = NY * QP, NY * OP
LB = D // CAP


def dot(a, b, ca, cb):
    return lax.dot_general(a, b, (((ca,), (cb,)), ((), ())), preferred_element_type=F32)


def call(kernel, out_shape, scratch, *args, smem=1, space=pltpu.VMEM, limit=VMEM_LIMIT):
    specs = [pl.BlockSpec(memory_space=pltpu.SMEM)] * smem + [
        pl.BlockSpec(memory_space=space)
    ] * (len(args) - smem)
    return pl.pallas_call(
        kernel,
        out_shape=out_shape,
        in_specs=specs,
        out_specs=jax.tree.map(lambda _: pl.BlockSpec(memory_space=pltpu.VMEM), out_shape),
        scratch_shapes=scratch,
        compiler_params=pltpu.CompilerParams(vmem_limit_bytes=limit),
    )(*args)


def sds(shape, dtype=BF):
    return jax.ShapeDtypeStruct(shape, dtype)


def here():
    return lax.axis_index("core"), lax.axis_index("y") * NX + lax.axis_index("x")


def target_rows(offsets):
    owner = here()[1]
    lane = lax.broadcasted_iota(jnp.int32, (1, CAP), 1)
    offset = jnp.zeros((1, CAP), jnp.int32)
    for image in range(OWNERS):
        offset = jnp.where(lane >> 2 == image, offsets[image], offset)
    return ((offset + ((owner - offset) & (OWNERS - 1))) >> 5) + (lane & (W_EMB - 1))


def one_hot(hit):
    return hit.astype(F32).astype(BF)


def reorder(rows, source):
    row = lax.broadcasted_iota(jnp.int32, (CAP, CAP), 0)
    column = lax.broadcasted_iota(jnp.int32, (CAP, CAP), 1)
    return dot(one_hot(column == source(row)), rows, 1, 0).astype(BF)


def put_rows(ref, first, rows):
    core = here()[0]
    for x in range(NX):
        for lane in range(LB):
            part = rows[x * EX : (x + 1) * EX, lane * CAP : (lane + 1) * CAP]
            ref[core * NX + x, first + lane * EX : first + (lane + 1) * EX] = part
        ref[(1 - core) * NX + x, first : first + LB * EX] = jnp.zeros((LB * EX, CAP), BF)


def get_rows(ref, first):
    core = here()[0]
    parts = []
    for x in range(NX):
        lanes = [
            ref[core * NX + x, first + lane * EX : first + (lane + 1) * EX] for lane in range(LB)
        ]
        parts.append(jnp.concatenate(lanes, axis=1))
    return jnp.concatenate(parts, axis=0)


def blocks():
    for core in range(2):
        for x in range(NX):
            for y in range(NY):
                yield core * NX + x, y, 2 * (NX * y + x) + core


def pre_kernel(offsets, *refs):
    sources, send, targets, sems, fq, fo = refs[:3], refs[3], refs[4:7], refs[7], *refs[8:]
    copies = [
        pltpu.make_async_copy(source, target, sems.at[n])
        for n, (source, target) in enumerate(zip(sources, targets, strict=True))
    ]
    for copy in copies:
        copy.start()
    for copy in copies:
        copy.wait()
    d_embeds, wq, wo = targets
    first = here()[0] == 0
    seq_rows = d_embeds.shape[0]
    row = lax.broadcasted_iota(jnp.int32, (seq_rows, CAP), 0)
    pick = one_hot(row == target_rows(offsets))
    fetched = dot(pick, d_embeds[...], 0, 0).astype(BF)
    fq[...] = wq[...].astype(F32)
    fo[...] = wo[...].astype(F32)
    half_q = jnp.where(first, fq[0:QP], fq[QP : 2 * QP])
    half_o = jnp.where(first, fo[0:OP], fo[OP : 2 * OP])
    fq[0:QP] = half_q
    fq[QP:PIECE] = half_o
    piece = fq[0:PIECE].astype(BF)
    for y in range(NY):
        send[y, 0:EY] = fetched[y * EY : (y + 1) * EY]
        send[y, EY : EY + PIECE] = piece


def normalize(patches):
    values_f = patches.astype(F32)
    inverse = lax.rsqrt(jnp.mean(values_f * values_f, axis=-1, keepdims=True) + 1e-06)
    return values_f, inverse, (values_f * inverse).astype(BF)


def qkv_kernel(mine, theirs, got, send, w_block, out_block, normed, tmp, fq, fo):
    core = here()[0]
    for y in range(NY):
        tmp[...] = got[y, EY : EY + PIECE].astype(F32)
        fq[y * QP : (y + 1) * QP] = tmp[0:QP]
        fo[y * OP : (y + 1) * OP] = tmp[QP:PIECE]
    weights = fq[...].astype(BF)
    w_block[...] = weights
    out_block[...] = fo[...].astype(BF)
    for side, patches in ((core, mine), (1 - core, theirs)):
        for x in range(NX):
            member = side * NX + x
            low = normalize(patches[x * CAP : (x + 1) * CAP])[2]
            normed[member] = low
            send[member, 0:QB] = dot(weights, low, 1, 1).astype(BF)
    rows = jnp.concatenate([got[y, 0:EY] for y in range(NY)], axis=0)
    rows = reorder(rows, lambda r: ((r >> 2) & 7) * EY + (r >> 5) * W_EMB + (r & 3))
    put_rows(send, QB, rows)


def fwd_kernel(lengths, got, qkv_t, prob, ctx_t, context, pa, qf):
    length = lengths[here()[1]]
    for member in range(TEAM):
        pa[member * QB : (member + 1) * QB] = got[member, 0:QB].astype(F32)
    for member, y, half in blocks():
        low = member * QB + y * QP
        qf[half * QP : (half + 1) * QP] = pa[low : low + QP]
    qkv_t[...] = qf[...].astype(BF)
    allowed = lax.broadcasted_iota(jnp.int32, (CAP, CAP), 1) < length
    for h in range(HEADS):
        q, k, v = (
            qkv_t[part * D + h * HEAD_DIM : part * D + (h + 1) * HEAD_DIM] for part in range(3)
        )
        scores = jnp.where(allowed, dot(q, k, 0, 0) * SCALE, -1e30)
        highest = jnp.max(scores, axis=-1, keepdims=True)
        weights = jnp.where(allowed, jnp.exp(scores - highest), 0.0)
        weights = weights / jnp.sum(weights, axis=-1, keepdims=True)
        prob[h] = weights
        ctx_t[h * HEAD_DIM : (h + 1) * HEAD_DIM] = dot(v, weights.astype(BF), 1, 1).astype(BF)
    context[...] = ctx_t[...].astype(F32).T.astype(BF)


def bwd_kernel(
    lengths, offsets, patches, got, qkv_t, prob, ctx_t, context, out_mine, out_theirs,
    send, grad, gt, gp, lt, oa, dq, dp,
):
    core, me = here()
    x_here = lax.axis_index("x")
    length, offset = lengths[me], offsets[me]
    came = get_rows(got, QB)
    slot = lax.broadcasted_iota(jnp.int32, (CAP, CAP), 0)
    owner = (slot + offset) & (OWNERS - 1)
    source = (owner & 3) * EX + (owner >> 2) * W_EMB + (slot >> 5)
    column = lax.broadcasted_iota(jnp.int32, (CAP, CAP), 1)
    grad_f = dot(one_hot((column == source) & (slot < length)), came, 1, 0)
    grad[...] = grad_f.astype(BF)
    gt[...] = grad_f.T
    for member, y, half in blocks():
        gp[member, y * OP : (y + 1) * OP] = gt[half * OP : (half + 1) * OP]
    out_blocks = [
        (side * NX + ((x_here - step) & (NX - 1)), ref[step * OB : (step + 1) * OB])
        for side, ref in ((core, out_mine), (1 - core, out_theirs))
        for step in range(NX)
    ]
    d_ctx = None
    for member, rows in out_blocks:
        term = dot(gp[member].T.astype(BF), rows, 1, 0)
        d_ctx = term if d_ctx is None else d_ctx + term
    d_ctx_t = d_ctx.astype(BF).astype(F32).T.astype(BF)
    for h in range(HEADS):
        at = [slice(part * D + h * HEAD_DIM, part * D + (h + 1) * HEAD_DIM) for part in range(3)]
        q, k, v = (qkv_t[rows] for rows in at)
        dc = d_ctx_t[h * HEAD_DIM : (h + 1) * HEAD_DIM]
        weights = prob[h]
        d_prob = dot(dc, v, 0, 0)
        dq[at[2]] = dot(dc, weights.astype(BF), 1, 0)
        inner = jnp.sum(d_prob * weights, axis=-1, keepdims=True)
        d_scores = (weights * (d_prob - inner) * SCALE).astype(BF)
        dq[at[0]] = dot(k, d_scores, 1, 1)
        dq[at[1]] = dot(q, d_scores, 1, 0)
    for member, y, half in blocks():
        low = member * QB + y * QP
        dp[low : low + QP] = dq[half * QP : (half + 1) * QP]
    for member in range(TEAM):
        send[member, 0:QB] = dp[member * QB : (member + 1) * QB].astype(BF)
        rows = gp[member].astype(BF)
        part = dot(rows, context[...], 1, 0).astype(BF)
        for lane in range(LB):
            low = QB + lane * OB
            send[member, low : low + OB] = part[:, lane * CAP : (lane + 1) * CAP]
    for member, rows in out_blocks:
        oa[member] = dot(rows, ctx_t[...], 1, 0)
    for member, y, half in blocks():
        lt[half * OP : (half + 1) * OP] = oa[member, y * OP : (y + 1) * OP]
    layer_out = patches[...].astype(F32) + lt[...].T
    token = lax.broadcasted_iota(jnp.int32, (CAP, 1), 0)
    outgoing = jnp.where(token < length, layer_out, 0.0).astype(BF)
    going = reorder(
        outgoing,
        lambda r: (r & 3) * OWNERS + ((NX * ((r >> 2) & 7) + (r >> 5) - offset) & (OWNERS - 1)),
    )
    put_rows(send, QB + LB * OB, going)


def grads_kernel(got, normed, send, fq, fo, tmp):
    total = None
    for member in range(TEAM):
        term = dot(got[member, 0:QB], normed[member], 1, 0)
        total = term if total is None else total + term
    fq[...] = total
    for lane in range(LB):
        low = QB + lane * OB
        total = got[0, low : low + OB].astype(F32)
        for member in range(1, TEAM):
            total += got[member, low : low + OB].astype(F32)
        fo[:, lane * CAP : (lane + 1) * CAP] = total
    rows = get_rows(got, QB + LB * OB)
    rows = reorder(rows, lambda r: ((r >> 2) & 3) * EX + (r >> 4) * W_EMB + (r & 3))
    for y in range(NY):
        tmp[0:QP] = fq[y * QP : (y + 1) * QP]
        tmp[QP:PIECE] = fo[y * OP : (y + 1) * OP]
        send[y, 0:EY] = rows[y * EY : (y + 1) * EY]
        send[y, EY : EY + PIECE] = tmp[...].astype(BF)


def terms_kernel(got, weights, mine, theirs):
    core = here()[0]
    for side, out in ((core, mine), (1 - core, theirs)):
        for x in range(NX):
            out[x] = dot(got[side * NX + x, 0:QB], weights[...], 0, 0).astype(BF)


def pair_kernel(mine, theirs, own, *others):
    x = lax.axis_index("x")
    for step, out in enumerate((own, *others)):
        image = (x + step) & (NX - 1)
        out[...] = (mine[image].astype(F32) + theirs[image].astype(F32)).astype(BF)


def patches_kernel(patches, grad, *refs):
    *terms, d_patches = refs
    d_normed = terms[0][...].astype(F32)
    for term in terms[1:]:
        d_normed += term[...].astype(F32)
    values_f, inverse, _ = normalize(patches[...])
    mean = jnp.mean(d_normed * values_f, axis=-1, keepdims=True)
    d_inputs = inverse * (d_normed - values_f * inverse * inverse * mean)
    d_patches[...] = (grad[...].astype(F32) + d_inputs).astype(BF)


def place_kernel(offsets, came, embeds):
    rows = jnp.concatenate([came[y, 0:EY] for y in range(NY)], axis=0)
    row = lax.broadcasted_iota(jnp.int32, (embeds.shape[0], CAP), 0)
    embeds[...] = dot(one_hot(row == target_rows(offsets)), rows, 1, 0).astype(BF)


def to_right(a, step):
    return lax.ppermute(a, "x", [(x, (x + step) % NX) for x in range(NX)])


def swap(a):
    return lax.ppermute(a, "core", [(0, 1), (1, 0)])


def together(*arrays):
    return lax.optimization_barrier(arrays)


def exchange(a, axis):
    return lax.all_to_all(a, axis, split_axis=0, concat_axis=0, tiled=True)


def gather(a, axis):
    return lax.all_gather(a, axis, axis=0, tiled=True)


def local(patches, lengths, offsets, w_qkv, w_out, d_embeds):
    core = lax.axis_index("core")
    seq_rows = d_embeds.shape[0]
    tokens = patches.reshape(CAP, D)
    team = ("core", "x")
    scratch = pltpu.VMEM

    send = call(
        pre_kernel,
        sds((NY, EY + PIECE, D)),
        [
            scratch(d_embeds.shape, BF),
            scratch((2 * QP, D), BF),
            scratch((2 * OP, D), BF),
            pltpu.SemaphoreType.DMA((3,)),
            scratch((2 * QP, D), F32),
            scratch((2 * OP, D), F32),
        ],
        offsets, d_embeds, w_qkv.T, w_out.T, space=pltpu.HBM, limit=None,
    )
    got = exchange(send, "y")
    mine = gather(tokens, "x")
    theirs = swap(mine)
    send, w_block, out_block, normed = call(
        qkv_kernel,
        (sds((TEAM, QB + LB * EX, CAP)), sds((QB, D)), sds((OB, D)), sds((TEAM, CAP, D))),
        [scratch((PIECE, D), F32), scratch((QB, D), F32), scratch((OB, D), F32)],
        mine, theirs, got, smem=0,
    )
    got, *near = together(
        exchange(send, team), *[to_right(out_block, step) for step in range(1, NX)]
    )
    out_mine = jnp.concatenate([out_block, *near], axis=0)
    out_theirs = swap(out_mine)
    qkv_t, prob, ctx_t, context = call(
        fwd_kernel,
        (sds((3 * D, CAP)), sds((HEADS, CAP, CAP), F32), sds((D, CAP)), sds((CAP, D))),
        [scratch((3 * D, CAP), F32), scratch((3 * D, CAP), F32)],
        lengths, got,
    )
    send, grad = call(
        bwd_kernel,
        (sds((TEAM, QB + LB * (OB + EX), CAP)), sds((CAP, D))),
        [
            scratch((D, CAP), F32),
            scratch((TEAM, OB, CAP), F32),
            scratch((D, CAP), F32),
            scratch((TEAM, OB, CAP), F32),
            scratch((3 * D, CAP), F32),
            scratch((3 * D, CAP), F32),
        ],
        lengths, offsets, tokens, got, qkv_t, prob, ctx_t, context, out_mine, out_theirs,
        smem=2,
    )
    got = exchange(send, team)
    send = call(
        grads_kernel,
        sds((NY, EY + PIECE, D)),
        [scratch((QB, D), F32), scratch((OB, D), F32), scratch((PIECE, D), F32)],
        got, normed, smem=0,
    )
    send, got = together(send, got)
    term, other = call(
        terms_kernel,
        (sds((NX, CAP, D)), sds((NX, CAP, D))),
        [], got, w_block, smem=0,
    )
    got = exchange(send, "y")
    own, *others = call(
        pair_kernel, (sds((CAP, D)),) * NX, [], term, swap(other), smem=0
    )
    right, across, left = others
    got, right, left, across = together(got, to_right(right, 1), to_right(left, NX - 1), across)
    terms = (own, right, left, to_right(across, 2))
    embeds = call(place_kernel, sds((seq_rows, D)), [], offsets, got)
    total = jnp.sum(got[:, EY:].astype(F32), axis=0).astype(BF)
    got = exchange(jnp.broadcast_to(total[None], (NZ, PIECE, D)), "z")
    d_patches = call(
        patches_kernel, sds((CAP, D)), [],
        tokens, grad, *terms, smem=0,
    )
    got, d_patches, embeds = together(got, d_patches, embeds)
    factor = 1.0 / math.sqrt(CAP * OWNERS * 2 * NZ)
    own = jnp.sum(got.astype(F32), axis=0) * factor
    other = swap(own)
    low, high = jnp.where(core == 0, own, other), jnp.where(core == 0, other, own)
    grad_qkv = jnp.concatenate([low[:QP], high[:QP]], axis=0).T
    grad_out = jnp.concatenate([low[QP:], high[QP:]], axis=0).T
    return embeds, d_patches.reshape(patches.shape), grad_qkv, grad_out


def solution(mesh):
    axes = Mesh(mesh.devices.reshape(NZ, 2, NY, NX), ("z", "core", "y", "x"))
    group, plane = ("z", "core"), ("y", "x")
    return jax.shard_map(
        local,
        mesh=axes,
        in_specs=(
            P(group + plane, None, None),
            P(group),
            P(group),
            P(None, plane),
            P(None, plane),
            P(group + plane, None),
        ),
        out_specs=(
            P(group + plane, None),
            P(group + plane, None, None),
            P(None, plane),
            P(None, plane),
        ),
        check_vma=False,
    )
```

time: 170 us -> 148 us (0.87)
  blocking collectives: 115 us -> 36.4 us
  starting transfers between devices: 14.6 us -> 61.4 us
  waiting for transfers between devices: 6.9 us -> 28.4 us
  local copies, waits for them, and re-layouts: 6.3 us -> 1.96 us
  other arithmetic: 5.73 us -> 1.46 us
  Pallas kernels: 20.4 us -> 17.2 us
    all_to_all x5 -> x1, blocking collectives: 115 us -> 24.2 us  [exchange(): return lax.all_to_all(a, axis, split_axis=0, concat_axis=0, tiled=True)]
    all_to_all x0 -> x4, starting transfers between devices: none -> 27.3 us  [exchange(): return lax.all_to_all(a, axis, split_axis=0, concat_axis=0, tiled=True)]
    ppermute x0 -> x6, starting transfers between devices: none -> 19.9 us  [to_right(): return lax.ppermute(a, 'x', [(x, (x + step) % NX) for x in range(NX)])]
    ppermute x0 -> x6, waiting for transfers between devices: none -> 13.3 us  [to_right(): return lax.ppermute(a, 'x', [(x, (x + step) % NX) for x in range(NX)])]
    all_gather x0 -> x1, blocking collectives: none -> 12.2 us  [gather(): return lax.all_gather(a, axis, axis=0, tiled=True)]
    all_to_all x0 -> x4, waiting for transfers between devices: none -> 10.8 us  [exchange(): return lax.all_to_all(a, axis, split_axis=0, concat_axis=0, tiled=True)]
    pallas_call x4 -> x9, Pallas kernels: 20.4 us -> 17.2 us  [call(): pl.pallas_call(kernel, out_shape=out_shape, in_specs=specs, out_specs=jax...]
    ppermute x3 -> x4, waiting for transfers between devices: 6.9 us -> 4.33 us  [swap(): return lax.ppermute(a, 'core', [(0, 1), (1, 0)])]
  transfers between devices with their start and end apart: 3 -> 14, of which waited for: 2 -> 10; matrix products, arithmetic and copies ran while one was open for 0% -> 0% of each run, Pallas kernels for 1% -> 4%
where the time goes in v2:
time: 148 us
  starting transfers between devices  61.4 us (41%)
  blocking collectives  36.4 us (25%)
  waiting for transfers between devices  28.4 us (19%)
  Pallas kernels  17.2 us (12%)
  local copies, waits for them, and re-layouts  1.96 us (1%)
    all_to_all x4, starting transfers between devices, exchange(): return lax.all_to_all(a, axis, split_axis=0, concat_axis=0, tiled=True)  27.3 us
    all_to_all x1, blocking collectives, exchange(): return lax.all_to_all(a, axis, split_axis=0, concat_axis=0, tiled=True)  24.2 us
    ppermute x6, starting transfers between devices, to_right(): return lax.ppermute(a, 'x', [(x, (x + step) % NX) for x in range(NX)])  19.9 us
    pallas_call x9, Pallas kernels, call(): pl.pallas_call(kernel, out_shape=out_shape, in_specs=specs, out_specs=jax...  17.2 us
    ppermute x4, starting transfers between devices, swap(): return lax.ppermute(a, 'core', [(0, 1), (1, 0)])  14.2 us
    ppermute x6, waiting for transfers between devices, to_right(): return lax.ppermute(a, 'x', [(x, (x + step) % NX) for x in range(NX)])  13.3 us
    all_gather x1, blocking collectives, gather(): return lax.all_gather(a, axis, axis=0, tiled=True)  12.2 us
    all_to_all x4, waiting for transfers between devices, exchange(): return lax.all_to_all(a, axis, split_axis=0, concat_axis=0, tiled=True)  10.8 us
  transfers between devices with their start and end apart: 14, of which 10 were waited for; matrix products, arithmetic and copies ran while one was open for 0% of the time, Pallas kernels for 4%

profile of v2, /device:TPU:1, one launch (start us, length us, event | category | flops | bytes accessed | tf_op | source)
XLA Modules:
  0.0 147.7 jit_solution(10825711669571534128)
XLA Ops:
  0.6 0.0 copy-start
  0.6 2.9 %shard_map.93 = bf16[8,56,640]{2,1,0:T(8,128)(2,1)} custom-call(s32[32]{0:T(128)} %offsets.5, bf16[256,640]{1,0:T(8,128)(2,1)} %refs_0_.1, bf16[60,640]{1,0:T(8,128)(2,1)} %bitcast.14, bf16[20,640]{1,0:T(8,128)(2,1)} %bitcast.15), custom_call_target="tpu_custom_call" | custom-call | tf_op jit(solution)/shard_map/pallas_call | solution.py:38
  3.6 7.7 %all-to-all-start = ((bf16[8,56,640]{2,1,0:T(8,128)(2,1)}), bf16[8,56,640]{2,1,0:T(8,128)(2,1)S(1)}, u32[]{:S(2)}, u32[]{:S(2)}) async-start(bf16[8,56,640]{2,1,0:T(8,128)(2,1)} %shard_map.93), calls=%async_computation | async-start | bytes 1146880 | tf_op jit(solution)/shard_map/all_to_all | solution.py:305
  11.2 0.0 copy-done
  11.2 12.2 %all-gather = bf16[1,512,640]{2,1,0:T(8,128)(2,1)S(1)} all-gather(bf16[1,128,640]{2,1,0:T(8,128)(2,1)S(1)} %copy-done), channel_id=2, replica_groups=mesh['z'=8,'core'=2,'y'=8,'x'=4] {'x'}, dimensions={1}, use_global_device_ids=true | all-gather | bytes 819200 | tf_op jit(solution)/shard_map/all_gather | solution.py:309
  23.4 6.4 %collective-permute-start = (bf16[512,640]{1,0:T(8,128)(2,1)S(1)}, bf16[512,640]{1,0:T(8,128)(2,1)S(1)}, u32[]{:S(2)}, u32[]{:S(2)}) collective-permute-start(bf16[512,640]{1,0:T(8,128)(2,1)S(1)} %bitcast.9), channel_id=1, source_target_pairs={{0,32},{32,0},{1,33},{33,1},{2,34},{34,2},{3,35},{35,3},{4,36},{36... | collective-permute-start | bytes 1966088 | tf_op jit(solution)/shard_map/ppermute | solution.py:297
  29.8 1.7 %collective-permute-done.theirs = bf16[512,640]{1,0:T(8,128)(2,1)S(1)} collective-permute-done((bf16[512,640]{1,0:T(8,128)(2,1)S(1)}, bf16[512,640]{1,0:T(8,128)(2,1)S(1)}, u32[]{:S(2)}, u32[]{:S(2)}) %collective-permute-start) | collective-permute-done | bytes 655392 | tf_op jit(solution)/shard_map/ppermute | solution.py:297
  31.5 0.0 all-to-all-done.got
  31.5 2.1 %shard_map.94 = (bf16[8,400,128]{2,1,0:T(8,128)(2,1)}, bf16[240,640]{1,0:T(8,128)(2,1)S(1)}, bf16[80,640]{1,0:T(8,128)(2,1)S(1)}, bf16[8,128,640]{2,1,0:T(8,128)(2,1)S(1)}) custom-call(bf16[512,640]{1,0:T(8,128)(2,1)S(1)} %bitcast.10, bf16[512,640]{1,0:T(8,128)(2,1)S(1)} %collective-permute-done.theirs, bf16[8,56,640]{2,1,0:T(8,128)(2,1)S(1)} %all-to-all-done.got), custom_call_target="tpu_custom_call" | custom-call | tf_op jit(solution)/shard_map/pallas_call | solution.py:38
  33.6 1.1 copy-done.1
  34.7 4.0 %all-to-all-start.1 = ((bf16[8,400,128]{2,1,0:T(8,128)(2,1)}), bf16[8,400,128]{2,1,0:T(8,128)(2,1)S(1)}, u32[]{:S(2)}, u32[]{:S(2)}) async-start(bf16[8,400,128]{2,1,0:T(8,128)(2,1)} %get-tuple-element.33), calls=%async_computation.1 | async-start | bytes 1638400 | tf_op jit(solution)/shard_map/all_to_all | solution.py:305
  38.7 3.3 %collective-permute-start.1 = (bf16[80,640]{1,0:T(8,128)(2,1)S(1)}, bf16[80,640]{1,0:T(8,128)(2,1)S(1)}, u32[]{:S(2)}, u32[]{:S(2)}) collective-permute-start(bf16[80,640]{1,0:T(8,128)(2,1)S(1)} %get-tuple-element.34), channel_id=1, source_target_pairs={{0,1},{1,2},{2,3},{3,0},{4,5},{5,6},{6,7},{7,4},{8,9},{9,10},{10,1... | collective-permute-start | bytes 307208 | tf_op jit(solution)/shard_map/ppermute | solution.py:293
  41.9 4.3 %collective-permute-start.2 = (bf16[80,640]{1,0:T(8,128)(2,1)S(1)}, bf16[80,640]{1,0:T(8,128)(2,1)S(1)}, u32[]{:S(2)}, u32[]{:S(2)}) collective-permute-start(bf16[80,640]{1,0:T(8,128)(2,1)S(1)} %get-tuple-element.34), channel_id=1, source_target_pairs={{0,2},{1,3},{2,0},{3,1},{4,6},{5,7},{6,4},{7,5},{8,10},{9,11},{10,... | collective-permute-start | bytes 307208 | tf_op jit(solution)/shard_map/ppermute | solution.py:293
  46.3 3.1 %collective-permute-start.3 = (bf16[80,640]{1,0:T(8,128)(2,1)S(1)}, bf16[80,640]{1,0:T(8,128)(2,1)S(1)}, u32[]{:S(2)}, u32[]{:S(2)}) collective-permute-start(bf16[80,640]{1,0:T(8,128)(2,1)S(1)} %get-tuple-element.34), channel_id=1, source_target_pairs={{0,3},{1,0},{2,1},{3,2},{4,7},{5,4},{6,5},{7,6},{8,11},{9,8},{10,9... | collective-permute-start | bytes 307208 | tf_op jit(solution)/shard_map/ppermute | solution.py:293
  49.4 4.0 %collective-permute-done.1 = bf16[80,640]{1,0:T(8,128)(2,1)S(1)} collective-permute-done((bf16[80,640]{1,0:T(8,128)(2,1)S(1)}, bf16[80,640]{1,0:T(8,128)(2,1)S(1)}, u32[]{:S(2)}, u32[]{:S(2)}) %collective-permute-start.1) | collective-permute-done | bytes 102432 | tf_op jit(solution)/shard_map/ppermute | solution.py:293
  53.4 2.4 %collective-permute-done.2 = bf16[80,640]{1,0:T(8,128)(2,1)S(1)} collective-permute-done((bf16[80,640]{1,0:T(8,128)(2,1)S(1)}, bf16[80,640]{1,0:T(8,128)(2,1)S(1)}, u32[]{:S(2)}, u32[]{:S(2)}) %collective-permute-start.2) | collective-permute-done | bytes 102432 | tf_op jit(solution)/shard_map/ppermute | solution.py:293
  55.7 0.0 collective-permute-done.3
  55.7 0.0 all-to-all-done.1.got
  55.8 2.8 %collective-permute-start.4 = (bf16[320,640]{1,0:T(8,128)(2,1)S(1)}, bf16[320,640]{1,0:T(8,128)(2,1)S(1)}, u32[]{:S(2)}, u32[]{:S(2)}) collective-permute-start(bf16[320,640]{1,0:T(8,128)(2,1)S(1)} %constant_dynamic-update-slice_fusion.out_mine), channel_id=1, source_target_pairs={{0,32},{32,0},{1,33},{33,1},{2,34},{34,2},{3,35},{35,3},{4,36},{36... | collective-permute-start | bytes 1228808 | tf_op jit(solution)/shard_map/ppermute | solution.py:297
  58.6 0.0 copy-done.4
  58.6 2.3 %shard_map.95 = (bf16[1920,128]{1,0:T(8,128)(2,1)S(1)}, f32[8,128,128]{2,1,0:T(8,128)S(1)}, bf16[640,128]{1,0:T(8,128)(2,1)S(1)}, bf16[128,640]{1,0:T(8,128)(2,1)S(1)}) custom-call(s32[32]{0:T(128)S(1)} %copy-done.4, bf16[8,400,128]{2,1,0:T(8,128)(2,1)S(1)} %all-to-all-done.1.got), custom_call_target="tpu_custom_call" | custom-call | tf_op jit(solution)/shard_map/pallas_call | solution.py:38
  60.9 0.0 collective-permute-done.4.out_theirs
  60.9 4.9 %shard_map.96 = (bf16[8,800,128]{2,1,0:T(8,128)(2,1)S(1)}, bf16[128,640]{1,0:T(8,128)(2,1)S(1)}) custom-call(s32[32]{0:T(128)S(1)} %copy-done.4, s32[32]{0:T(128)S(1)} %copy-done.3, bf16[128,640]{1,0:T(8,128)(2,1)S(1)} %bitcast.11, bf16[8,400,128]{2,1,0:T(8,128)(2,1)S(1)} %all-to-all-done.1.got, bf16[1920,128]{1,0:T(8,128)(2,1)S(1)} %get-tuple-element.36.qkv_t, ...), custom_call_target="tpu_custom_call" | custom-call | tf_op jit(solution)/shard_map/pallas_call | solution.py:38
  65.8 24.2 %all_to_all.25.got = bf16[8,800,128]{2,1,0:T(8,128)(2,1)S(1)} all-to-all(bf16[8,800,128]{2,1,0:T(8,128)(2,1)S(1)} %get-tuple-element.43), channel_id=1, replica_groups=mesh['z'=8,'core'=2,'y'=8,'x'=4] {'core','x'}, dimensions={0} | all-to-all | bytes 3276800 | tf_op jit(solution)/shard_map/all_to_all | solution.py:305
  90.0 1.8 %shard_map.97 = bf16[8,56,640]{2,1,0:T(8,128)(2,1)} custom-call(bf16[8,800,128]{2,1,0:T(8,128)(2,1)S(1)} %all_to_all.25.got, bf16[8,128,640]{2,1,0:T(8,128)(2,1)S(1)} %copy-done.2), custom_call_target="tpu_custom_call" | custom-call | tf_op jit(solution)/shard_map/pallas_call | solution.py:38
  91.9 6.8 %all-to-all-start.3 = ((bf16[8,56,640]{2,1,0:T(8,128)(2,1)}), bf16[8,56,640]{2,1,0:T(8,128)(2,1)S(1)}, u32[]{:S(2)}, u32[]{:S(2)}) async-start(bf16[8,56,640]{2,1,0:T(8,128)(2,1)} %shard_map.97), calls=%async_computation.3 | async-start | bytes 1146880 | tf_op jit(solution)/shard_map/all_to_all | solution.py:305
  98.6 0.6 shard_map.98
  99.3 2.6 %collective-permute-start.5 = (bf16[4,128,640]{2,1,0:T(8,128)(2,1)S(1)}, bf16[4,128,640]{2,1,0:T(8,128)(2,1)S(1)}, u32[]{:S(2)}, u32[]{:S(2)}) collective-permute-start(bf16[4,128,640]{2,1,0:T(8,128)(2,1)S(1)} %get-tuple-element.49), channel_id=1, source_target_pairs={{0,32},{32,0},{1,33},{33,1},{2,34},{34,2},{3,35},{35,3},{4,36},{36... | collective-permute-start | bytes 1966088 | tf_op jit(solution)/shard_map/ppermute | solution.py:297
  101.9 1.7 %collective-permute-done.5.theirs = bf16[4,128,640]{2,1,0:T(8,128)(2,1)S(1)} collective-permute-done((bf16[4,128,640]{2,1,0:T(8,128)(2,1)S(1)}, bf16[4,128,640]{2,1,0:T(8,128)(2,1)S(1)}, u32[]{:S(2)}, u32[]{:S(2)}) %collective-permute-start.5) | collective-permute-done | bytes 655392 | tf_op jit(solution)/shard_map/ppermute | solution.py:297
  103.6 0.2 shard_map.99
  103.7 2.4 %collective-permute-start.6 = (bf16[128,640]{1,0:T(8,128)(2,1)S(1)}, bf16[128,640]{1,0:T(8,128)(2,1)S(1)}, u32[]{:S(2)}, u32[]{:S(2)}) collective-permute-start(bf16[128,640]{1,0:T(8,128)(2,1)S(1)} %get-tuple-element.50), channel_id=1, source_target_pairs={{0,1},{1,2},{2,3},{3,0},{4,5},{5,6},{6,7},{7,4},{8,9},{9,10},{10,1... | collective-permute-start | bytes 491528 | tf_op jit(solution)/shard_map/ppermute | solution.py:293
  106.1 4.1 %collective-permute-start.7 = (bf16[128,640]{1,0:T(8,128)(2,1)S(1)}, bf16[128,640]{1,0:T(8,128)(2,1)S(1)}, u32[]{:S(2)}, u32[]{:S(2)}) collective-permute-start(bf16[128,640]{1,0:T(8,128)(2,1)S(1)} %get-tuple-element.51), channel_id=1, source_target_pairs={{0,3},{1,0},{2,1},{3,2},{4,7},{5,4},{6,5},{7,6},{8,11},{9,8},{10,9... | collective-permute-start | bytes 491528 | tf_op jit(solution)/shard_map/ppermute | solution.py:293
  110.2 2.0 %collective-permute-done.6.refs_1_ = bf16[128,640]{1,0:T(8,128)(2,1)S(1)} collective-permute-done((bf16[128,640]{1,0:T(8,128)(2,1)S(1)}, bf16[128,640]{1,0:T(8,128)(2,1)S(1)}, u32[]{:S(2)}, u32[]{:S(2)}) %collective-permute-start.6) | collective-permute-done | bytes 163872 | tf_op jit(solution)/shard_map/ppermute | solution.py:293
  112.2 0.9 collective-permute-done.7.refs_2_
  113.1 4.6 %all-to-all-done.3.came = bf16[8,56,640]{2,1,0:T(8,128)(2,1)S(1)} async-done(((bf16[8,56,640]{2,1,0:T(8,128)(2,1)}), bf16[8,56,640]{2,1,0:T(8,128)(2,1)S(1)}, u32[]{:S(2)}, u32[]{:S(2)}) %all-to-all-start.3) | async-done | bytes 573472 | tf_op jit(solution)/shard_map/all_to_all | solution.py:305
  117.7 0.1 slice_reduce_fusion
  117.7 0.8 broadcast_in_dim.2
  118.5 8.9 %all-to-all-start.4 = ((bf16[8,40,640]{2,1,0:T(8,128)(2,1)}), bf16[8,40,640]{2,1,0:T(8,128)(2,1)S(1)}, u32[]{:S(2)}, u32[]{:S(2)}) async-start(bf16[8,40,640]{2,1,0:T(8,128)(2,1)} %broadcast_in_dim.2), calls=%async_computation.4 | async-start | bytes 819200 | tf_op jit(solution)/shard_map/all_to_all | solution.py:305
  127.4 2.8 %collective-permute-start.8 = (bf16[128,640]{1,0:T(8,128)(2,1)S(1)}, bf16[128,640]{1,0:T(8,128)(2,1)S(1)}, u32[]{:S(2)}, u32[]{:S(2)}) collective-permute-start(bf16[128,640]{1,0:T(8,128)(2,1)S(1)} %get-tuple-element.58), channel_id=1, source_target_pairs={{0,2},{1,3},{2,0},{3,1},{4,6},{5,7},{6,4},{7,5},{8,10},{9,11},{10,... | collective-permute-start | bytes 491528 | tf_op jit(solution)/shard_map/ppermute | solution.py:293
  130.2 1.5 %shard_map.101 = bf16[256,640]{1,0:T(8,128)(2,1)} custom-call(s32[32]{0:T(128)S(1)} %copy-done.3, bf16[8,56,640]{2,1,0:T(8,128)(2,1)S(1)} %all-to-all-done.3.came), custom_call_target="tpu_custom_call" | custom-call | tf_op jit(solution)/shard_map/pallas_call | solution.py:38
  131.7 4.0 %collective-permute-done.8.refs_3_ = bf16[128,640]{1,0:T(8,128)(2,1)S(1)} collective-permute-done((bf16[128,640]{1,0:T(8,128)(2,1)S(1)}, bf16[128,640]{1,0:T(8,128)(2,1)S(1)}, u32[]{:S(2)}, u32[]{:S(2)}) %collective-permute-start.8) | collective-permute-done | bytes 163872 | tf_op jit(solution)/shard_map/ppermute | solution.py:293
  135.7 0.9 shard_map.100
  136.6 6.2 %all-to-all-done.4 = bf16[8,40,640]{2,1,0:T(8,128)(2,1)S(1)} async-done(((bf16[8,40,640]{2,1,0:T(8,128)(2,1)}), bf16[8,40,640]{2,1,0:T(8,128)(2,1)S(1)}, u32[]{:S(2)}, u32[]{:S(2)}) %all-to-all-start.4) | async-done | bytes 409632 | tf_op jit(solution)/shard_map/all_to_all | solution.py:305
  142.9 0.1 convert_reduce_fusion
  142.9 2.4 %collective-permute-start.9 = (f32[40,640]{1,0:T(8,128)S(1)}, f32[40,640]{1,0:T(8,128)S(1)}, u32[]{:S(2)}, u32[]{:S(2)}) collective-permute-start(f32[40,640]{1,0:T(8,128)S(1)} %broadcast_multiply_fusion), channel_id=1, source_target_pairs={{0,32},{32,0},{1,33},{33,1},{2,34},{34,2},{3,35},{35,3},{4,36},{36... | collective-permute-start | bytes 307208 | tf_op jit(solution)/shard_map/ppermute | solution.py:297
  145.4 0.9 collective-permute-done.9
  146.4 0.6 maximum_bitcast_fusion.1
  147.0 0.7 maximum_bitcast_fusion
  (16 shorter events, 0.1 us)
Async XLA Ops:
  0.6 10.6 %copy-start = (bf16[1,128,640]{2,1,0:T(8,128)(2,1)S(1)}, bf16[1,128,640]{2,1,0:T(8,128)(2,1)}, u32[]{:S(2)}) copy-start(bf16[1,128,640]{2,1,0:T(8,128)(2,1)} %param.6) | copy-start | bytes 491524
  3.6 27.9 %all-to-all-start = ((bf16[8,56,640]{2,1,0:T(8,128)(2,1)}), bf16[8,56,640]{2,1,0:T(8,128)(2,1)S(1)}, u32[]{:S(2)}, u32[]{:S(2)}) async-start(bf16[8,56,640]{2,1,0:T(8,128)(2,1)} %shard_map.93), calls=%async_computation | async-start | bytes 1146880 | tf_op jit(solution)/shard_map/all_to_all | solution.py:305
  23.4 8.1 %collective-permute-start = (bf16[512,640]{1,0:T(8,128)(2,1)S(1)}, bf16[512,640]{1,0:T(8,128)(2,1)S(1)}, u32[]{:S(2)}, u32[]{:S(2)}) collective-permute-start(bf16[512,640]{1,0:T(8,128)(2,1)S(1)} %bitcast.9), channel_id=1, source_target_pairs={{0,32},{32,0},{1,33},{33,1},{2,34},{34,2},{3,35},{35,3},{4,36},{36... | collective-permute-start | bytes 1966088 | tf_op jit(solution)/shard_map/ppermute | solution.py:297
  33.6 1.1 copy-start.1
  34.7 23.9 %copy-start.4 = (s32[32]{0:T(128)S(1)}, s32[32]{0:T(128)}, u32[]{:S(2)}) copy-start(s32[32]{0:T(128)} %lengths.3) | copy-start | bytes 388
  34.7 26.2 %copy-start.3 = (s32[32]{0:T(128)S(1)}, s32[32]{0:T(128)}, u32[]{:S(2)}) copy-start(s32[32]{0:T(128)} %offsets.5) | copy-start | bytes 388
  34.7 21.1 %all-to-all-start.1 = ((bf16[8,400,128]{2,1,0:T(8,128)(2,1)}), bf16[8,400,128]{2,1,0:T(8,128)(2,1)S(1)}, u32[]{:S(2)}, u32[]{:S(2)}) async-start(bf16[8,400,128]{2,1,0:T(8,128)(2,1)} %get-tuple-element.33), calls=%async_computation.1 | async-start | bytes 1638400 | tf_op jit(solution)/shard_map/all_to_all | solution.py:305
  38.7 14.7 %collective-permute-start.1 = (bf16[80,640]{1,0:T(8,128)(2,1)S(1)}, bf16[80,640]{1,0:T(8,128)(2,1)S(1)}, u32[]{:S(2)}, u32[]{:S(2)}) collective-permute-start(bf16[80,640]{1,0:T(8,128)(2,1)S(1)} %get-tuple-element.34), channel_id=1, source_target_pairs={{0,1},{1,2},{2,3},{3,0},{4,5},{5,6},{6,7},{7,4},{8,9},{9,10},{10,1... | collective-permute-start | bytes 307208 | tf_op jit(solution)/shard_map/ppermute | solution.py:293
  41.9 13.8 %collective-permute-start.2 = (bf16[80,640]{1,0:T(8,128)(2,1)S(1)}, bf16[80,640]{1,0:T(8,128)(2,1)S(1)}, u32[]{:S(2)}, u32[]{:S(2)}) collective-permute-start(bf16[80,640]{1,0:T(8,128)(2,1)S(1)} %get-tuple-element.34), channel_id=1, source_target_pairs={{0,2},{1,3},{2,0},{3,1},{4,6},{5,7},{6,4},{7,5},{8,10},{9,11},{10,... | collective-permute-start | bytes 307208 | tf_op jit(solution)/shard_map/ppermute | solution.py:293
  46.3 9.5 %collective-permute-start.3 = (bf16[80,640]{1,0:T(8,128)(2,1)S(1)}, bf16[80,640]{1,0:T(8,128)(2,1)S(1)}, u32[]{:S(2)}, u32[]{:S(2)}) collective-permute-start(bf16[80,640]{1,0:T(8,128)(2,1)S(1)} %get-tuple-element.34), channel_id=1, source_target_pairs={{0,3},{1,0},{2,1},{3,2},{4,7},{5,4},{6,5},{7,6},{8,11},{9,8},{10,9... | collective-permute-start | bytes 307208 | tf_op jit(solution)/shard_map/ppermute | solution.py:293
  55.8 5.1 %collective-permute-start.4 = (bf16[320,640]{1,0:T(8,128)(2,1)S(1)}, bf16[320,640]{1,0:T(8,128)(2,1)S(1)}, u32[]{:S(2)}, u32[]{:S(2)}) collective-permute-start(bf16[320,640]{1,0:T(8,128)(2,1)S(1)} %constant_dynamic-update-slice_fusion.out_mine), channel_id=1, source_target_pairs={{0,32},{32,0},{1,33},{33,1},{2,34},{34,2},{3,35},{35,3},{4,36},{36... | collective-permute-start | bytes 1228808 | tf_op jit(solution)/shard_map/ppermute | solution.py:297
  65.8 24.2 %copy-start.2 = (bf16[8,128,640]{2,1,0:T(8,128)(2,1)S(1)}, bf16[8,128,640]{2,1,0:T(8,128)(2,1)}, u32[]{:S(2)}) copy-start(bf16[8,128,640]{2,1,0:T(8,128)(2,1)} %copy-done.1) | copy-start | bytes 3932164
  91.9 25.8 %all-to-all-start.3 = ((bf16[8,56,640]{2,1,0:T(8,128)(2,1)}), bf16[8,56,640]{2,1,0:T(8,128)(2,1)S(1)}, u32[]{:S(2)}, u32[]{:S(2)}) async-start(bf16[8,56,640]{2,1,0:T(8,128)(2,1)} %shard_map.97), calls=%async_computation.3 | async-start | bytes 1146880 | tf_op jit(solution)/shard_map/all_to_all | solution.py:305
  99.3 4.3 %collective-permute-start.5 = (bf16[4,128,640]{2,1,0:T(8,128)(2,1)S(1)}, bf16[4,128,640]{2,1,0:T(8,128)(2,1)S(1)}, u32[]{:S(2)}, u32[]{:S(2)}) collective-permute-start(bf16[4,128,640]{2,1,0:T(8,128)(2,1)S(1)} %get-tuple-element.49), channel_id=1, source_target_pairs={{0,32},{32,0},{1,33},{33,1},{2,34},{34,2},{3,35},{35,3},{4,36},{36... | collective-permute-start | bytes 1966088 | tf_op jit(solution)/shard_map/ppermute | solution.py:297
  103.7 8.5 %collective-permute-start.6 = (bf16[128,640]{1,0:T(8,128)(2,1)S(1)}, bf16[128,640]{1,0:T(8,128)(2,1)S(1)}, u32[]{:S(2)}, u32[]{:S(2)}) collective-permute-start(bf16[128,640]{1,0:T(8,128)(2,1)S(1)} %get-tuple-element.50), channel_id=1, source_target_pairs={{0,1},{1,2},{2,3},{3,0},{4,5},{5,6},{6,7},{7,4},{8,9},{9,10},{10,1... | collective-permute-start | bytes 491528 | tf_op jit(solution)/shard_map/ppermute | solution.py:293
  106.1 7.0 %collective-permute-start.7 = (bf16[128,640]{1,0:T(8,128)(2,1)S(1)}, bf16[128,640]{1,0:T(8,128)(2,1)S(1)}, u32[]{:S(2)}, u32[]{:S(2)}) collective-permute-start(bf16[128,640]{1,0:T(8,128)(2,1)S(1)} %get-tuple-element.51), channel_id=1, source_target_pairs={{0,3},{1,0},{2,1},{3,2},{4,7},{5,4},{6,5},{7,6},{8,11},{9,8},{10,9... | collective-permute-start | bytes 491528 | tf_op jit(solution)/shard_map/ppermute | solution.py:293
  118.5 24.4 %all-to-all-start.4 = ((bf16[8,40,640]{2,1,0:T(8,128)(2,1)}), bf16[8,40,640]{2,1,0:T(8,128)(2,1)S(1)}, u32[]{:S(2)}, u32[]{:S(2)}) async-start(bf16[8,40,640]{2,1,0:T(8,128)(2,1)} %broadcast_in_dim.2), calls=%async_computation.4 | async-start | bytes 819200 | tf_op jit(solution)/shard_map/all_to_all | solution.py:305
  127.4 8.3 %collective-permute-start.8 = (bf16[128,640]{1,0:T(8,128)(2,1)S(1)}, bf16[128,640]{1,0:T(8,128)(2,1)S(1)}, u32[]{:S(2)}, u32[]{:S(2)}) collective-permute-start(bf16[128,640]{1,0:T(8,128)(2,1)S(1)} %get-tuple-element.58), channel_id=1, source_target_pairs={{0,2},{1,3},{2,0},{3,1},{4,6},{5,7},{6,4},{7,5},{8,10},{9,11},{10,... | collective-permute-start | bytes 491528 | tf_op jit(solution)/shard_map/ppermute | solution.py:293
  142.9 3.4 %collective-permute-start.9 = (f32[40,640]{1,0:T(8,128)S(1)}, f32[40,640]{1,0:T(8,128)S(1)}, u32[]{:S(2)}, u32[]{:S(2)}) collective-permute-start(f32[40,640]{1,0:T(8,128)S(1)} %broadcast_multiply_fusion), channel_id=1, source_target_pairs={{0,32},{32,0},{1,33},{33,1},{2,34},{34,2},{3,35},{35,3},{4,36},{36... | collective-permute-start | bytes 307208 | tf_op jit(solution)/shard_map/ppermute | solution.py:297

commit v3 on v2

--- a/solution.py
+++ b/solution.py
@@ -107,13 +107,13 @@
     ]
     for copy in copies:
         copy.start()
-    for copy in copies:
-        copy.wait()
     d_embeds, wq, wo = targets
     first = here()[0] == 0
     seq_rows = d_embeds.shape[0]
     row = lax.broadcasted_iota(jnp.int32, (seq_rows, CAP), 0)
     pick = one_hot(row == target_rows(offsets))
+    for copy in copies:
+        copy.wait()
     fetched = dot(pick, d_embeds[...], 0, 0).astype(BF)
     fq[...] = wq[...].astype(F32)
     fo[...] = wo[...].astype(F32)
@@ -175,9 +175,16 @@
     context[...] = ctx_t[...].astype(F32).T.astype(BF)
 
 
+def out_blocks(core, x_here, mine, theirs):
+    for side, ref in ((core, mine), (1 - core, theirs)):
+        for step in range(NX):
+            member = side * NX + ((x_here - step) & (NX - 1))
+            yield member, ref[step * OB : (step + 1) * OB]
+
+
 def bwd_kernel(
-    lengths, offsets, patches, got, qkv_t, prob, ctx_t, context, out_mine, out_theirs,
-    send, grad, gt, gp, lt, oa, dq, dp,
+    lengths, offsets, got, qkv_t, prob, context, out_mine, out_theirs, send,
+    grad, gt, gp, dq, dp,
 ):
     core, me = here()
     x_here = lax.axis_index("x")
@@ -192,13 +199,8 @@
     gt[...] = grad_f.T
     for member, y, half in blocks():
         gp[member, y * OP : (y + 1) * OP] = gt[half * OP : (half + 1) * OP]
-    out_blocks = [
-        (side * NX + ((x_here - step) & (NX - 1)), ref[step * OB : (step + 1) * OB])
-        for side, ref in ((core, out_mine), (1 - core, out_theirs))
-        for step in range(NX)
-    ]
     d_ctx = None
-    for member, rows in out_blocks:
+    for member, rows in out_blocks(core, x_here, out_mine, out_theirs):
         term = dot(gp[member].T.astype(BF), rows, 1, 0)
         d_ctx = term if d_ctx is None else d_ctx + term
     d_ctx_t = d_ctx.astype(BF).astype(F32).T.astype(BF)
@@ -223,7 +225,14 @@
         for lane in range(LB):
             low = QB + lane * OB
             send[member, low : low + OB] = part[:, lane * CAP : (lane + 1) * CAP]
-    for member, rows in out_blocks:
+
+
+def out_kernel(lengths, offsets, patches, ctx_t, out_mine, out_theirs, *refs):
+    along, (lt, oa, rows_x) = refs[:NX], refs[NX:]
+    core, me = here()
+    x_here = lax.axis_index("x")
+    length, offset = lengths[me], offsets[me]
+    for member, rows in out_blocks(core, x_here, out_mine, out_theirs):
         oa[member] = dot(rows, ctx_t[...], 1, 0)
     for member, y, half in blocks():
         lt[half * OP : (half + 1) * OP] = oa[member, y * OP : (y + 1) * OP]
@@ -234,10 +243,15 @@
         outgoing,
         lambda r: (r & 3) * OWNERS + ((NX * ((r >> 2) & 7) + (r >> 5) - offset) & (OWNERS - 1)),
     )
-    put_rows(send, QB + LB * OB, going)
-
-
-def grads_kernel(got, normed, send, fq, fo, tmp):
+    for x in range(NX):
+        rows_x[x] = going[x * EX : (x + 1) * EX]
+    for step, out in enumerate(along):
+        out[...] = rows_x[(x_here + step) & (NX - 1)]
+
+
+def grads_kernel(got, normed, *refs):
+    near, (send, fq, fo, tmp, rows_x) = refs[:NX], refs[NX:]
+    x_here = lax.axis_index("x")
     total = None
     for member in range(TEAM):
         term = dot(got[member, 0:QB], normed[member], 1, 0)
@@ -249,7 +263,9 @@
         for member in range(1, TEAM):
             total += got[member, low : low + OB].astype(F32)
         fo[:, lane * CAP : (lane + 1) * CAP] = total
-    rows = get_rows(got, QB + LB * OB)
+    for step, ref in enumerate(near):
+        rows_x[(x_here - step) & (NX - 1)] = ref[...]
+    rows = jnp.concatenate([rows_x[x] for x in range(NX)], axis=0)
     rows = reorder(rows, lambda r: ((r >> 2) & 3) * EX + (r >> 4) * W_EMB + (r & 3))
     for y in range(NY):
         tmp[0:QP] = fq[y * QP : (y + 1) * QP]
@@ -289,8 +305,22 @@
     embeds[...] = dot(one_hot(row == target_rows(offsets)), rows, 1, 0).astype(BF)
 
 
+def join_kernel(own, other, grad_qkv, grad_out):
+    first = here()[0] == 0
+    low = jnp.where(first, own[...], other[...])
+    high = jnp.where(first, other[...], own[...])
+    for out, rows in ((grad_qkv, slice(0, QP)), (grad_out, slice(QP, PIECE))):
+        size = rows.stop - rows.start
+        out[0:size] = low[rows]
+        out[size : 2 * size] = high[rows]
+
+
+def along_x(a, target):
+    return lax.ppermute(a, "x", [(x, target(x)) for x in range(NX)])
+
+
 def to_right(a, step):
-    return lax.ppermute(a, "x", [(x, (x + step) % NX) for x in range(NX)])
+    return along_x(a, lambda x: (x + step) % NX)
 
 
 def swap(a):
@@ -310,7 +340,6 @@
 
 
 def local(patches, lengths, offsets, w_qkv, w_out, d_embeds):
-    core = lax.axis_index("core")
     seq_rows = d_embeds.shape[0]
     tokens = patches.reshape(CAP, D)
     team = ("core", "x")
@@ -351,24 +380,30 @@
     )
     send, grad = call(
         bwd_kernel,
-        (sds((TEAM, QB + LB * (OB + EX), CAP)), sds((CAP, D))),
+        (sds((TEAM, QB + LB * OB, CAP)), sds((CAP, D))),
         [
-            scratch((D, CAP), F32),
-            scratch((TEAM, OB, CAP), F32),
             scratch((D, CAP), F32),
             scratch((TEAM, OB, CAP), F32),
             scratch((3 * D, CAP), F32),
             scratch((3 * D, CAP), F32),
         ],
-        lengths, offsets, tokens, got, qkv_t, prob, ctx_t, context, out_mine, out_theirs,
-        smem=2,
-    )
-    got = exchange(send, team)
+        lengths, offsets, got, qkv_t, prob, context, out_mine, out_theirs, smem=2,
+    )
+    send, ctx_t = together(send, ctx_t)
+    rows_x = scratch((NX, EX, D), BF)
+    along = call(
+        out_kernel,
+        (sds((EX, D)),) * NX,
+        [scratch((D, CAP), F32), scratch((TEAM, OB, CAP), F32), rows_x],
+        lengths, offsets, tokens, ctx_t, out_mine, out_theirs, smem=2,
+    )
+    near = [a if step == 0 else to_right(a, step) for step, a in enumerate(along)]
+    got, *near = together(exchange(send, team), *near)
     send = call(
         grads_kernel,
         sds((NY, EY + PIECE, D)),
-        [scratch((QB, D), F32), scratch((OB, D), F32), scratch((PIECE, D), F32)],
-        got, normed, smem=0,
+        [scratch((QB, D), F32), scratch((OB, D), F32), scratch((PIECE, D), F32), rows_x],
+        got, normed, *near, smem=0,
     )
     send, got = together(send, got)
     term, other = call(
@@ -377,12 +412,11 @@
         [], got, w_block, smem=0,
     )
     got = exchange(send, "y")
-    own, *others = call(
+    own, right, across, left = call(
         pair_kernel, (sds((CAP, D)),) * NX, [], term, swap(other), smem=0
     )
-    right, across, left = others
-    got, right, left, across = together(got, to_right(right, 1), to_right(left, NX - 1), across)
-    terms = (own, right, left, to_right(across, 2))
+    got, right, across, left = together(got, to_right(right, 1), across, left)
+    terms = own, right, to_right(across, 2), to_right(left, NX - 1)
     embeds = call(place_kernel, sds((seq_rows, D)), [], offsets, got)
     total = jnp.sum(got[:, EY:].astype(F32), axis=0).astype(BF)
     got = exchange(jnp.broadcast_to(total[None], (NZ, PIECE, D)), "z")
@@ -394,10 +428,10 @@
     factor = 1.0 / math.sqrt(CAP * OWNERS * 2 * NZ)
     own = jnp.sum(got.astype(F32), axis=0) * factor
     other = swap(own)
-    low, high = jnp.where(core == 0, own, other), jnp.where(core == 0, other, own)
-    grad_qkv = jnp.concatenate([low[:QP], high[:QP]], axis=0).T
-    grad_out = jnp.concatenate([low[QP:], high[QP:]], axis=0).T
-    return embeds, d_patches.reshape(patches.shape), grad_qkv, grad_out
+    grad_qkv, grad_out = call(
+        join_kernel, (sds((2 * QP, D), F32), sds((2 * OP, D), F32)), [], own, other, smem=0
+    )
+    return embeds, d_patches.reshape(patches.shape), grad_qkv.T, grad_out.T
 
 
 def solution(mesh):

time: 148 us -> 147 us (level)
  blocking collectives: 36.4 us -> 12.2 us
  starting transfers between devices: 61.4 us -> 78.7 us
  waiting for transfers between devices: 28.4 us -> 31.1 us
  local copies, waits for them, and re-layouts: 1.96 us -> 4.33 us
    all_to_all x1 -> x0, blocking collectives: 24.2 us -> none  [exchange(): return lax.all_to_all(a, axis, split_axis=0, concat_axis=0, tiled=True)]
    ppermute x6 -> x9, starting transfers between devices: 19.9 us -> 30.6 us  [along_x(): return lax.ppermute(a, 'x', [(x, target(x)) for x in range(NX)])]
    ppermute x6 -> x9, waiting for transfers between devices: 13.3 us -> 23.3 us  [along_x(): return lax.ppermute(a, 'x', [(x, target(x)) for x in range(NX)])]
    all_to_all x4 -> x5, waiting for transfers between devices: 10.8 us -> 3.4 us  [exchange(): return lax.all_to_all(a, axis, split_axis=0, concat_axis=0, tiled=True)]
    all_to_all x4 -> x5, starting transfers between devices: 27.3 us -> 30.8 us  [exchange(): return lax.all_to_all(a, axis, split_axis=0, concat_axis=0, tiled=True)]
    ppermute x4, starting transfers between devices: 14.2 us -> 17.3 us  [swap(): return lax.ppermute(a, 'core', [(0, 1), (1, 0)])]
    unnamed x13 -> x15, local copies, waits for them, and re-layouts: 1.13 us -> 3.52 us
    pallas_call x9 -> x11, Pallas kernels: 17.2 us -> 18.6 us  [call(): pl.pallas_call(kernel, out_shape=out_shape, in_specs=specs, out_specs=jax...]
  transfers between devices with their start and end apart: 14 -> 18, of which waited for: 10 -> 11; matrix products, arithmetic and copies ran while one was open for 0% -> 0% of each run, Pallas kernels for 4% -> 5%
where the time goes in v3:
time: 147 us; the launch traced here: 146 us
  starting transfers between devices  78.7 us (54%)
  waiting for transfers between devices  31.1 us (21%)
  Pallas kernels  18.6 us (13%)
  blocking collectives  12.2 us (8%)
  local copies, waits for them, and re-layouts  4.33 us (3%)
    all_to_all x5, starting transfers between devices, exchange(): return lax.all_to_all(a, axis, split_axis=0, concat_axis=0, tiled=True)  30.8 us
    ppermute x9, starting transfers between devices, along_x(): return lax.ppermute(a, 'x', [(x, target(x)) for x in range(NX)])  30.6 us
    ppermute x9, waiting for transfers between devices, along_x(): return lax.ppermute(a, 'x', [(x, target(x)) for x in range(NX)])  23.3 us
    pallas_call x11, Pallas kernels, call(): pl.pallas_call(kernel, out_shape=out_shape, in_specs=specs, out_specs=jax...  18.6 us
    ppermute x4, starting transfers between devices, swap(): return lax.ppermute(a, 'core', [(0, 1), (1, 0)])  17.3 us
    all_gather x1, blocking collectives, gather(): return lax.all_gather(a, axis, axis=0, tiled=True)  12.2 us
    ppermute x4, waiting for transfers between devices, swap(): return lax.ppermute(a, 'core', [(0, 1), (1, 0)])  4.33 us
    unnamed x15, local copies, waits for them, and re-layouts  3.52 us
  transfers between devices with their start and end apart: 18, of which 11 were waited for; matrix products, arithmetic and copies ran while one was open for 0% of the time, Pallas kernels for 5%

profile of v3, /device:TPU:1, one launch (start us, length us, event | category | flops | bytes accessed | tf_op | source)
XLA Modules:
  0.0 146.0 jit_solution(12612729809249193255)
XLA Ops:
  0.6 2.9 %shard_map.93 = bf16[8,56,640]{2,1,0:T(8,128)(2,1)} custom-call(s32[32]{0:T(128)} %offsets.7, bf16[256,640]{1,0:T(8,128)(2,1)} %refs_0_.1, bf16[60,640]{1,0:T(8,128)(2,1)} %bitcast.12, bf16[20,640]{1,0:T(8,128)(2,1)} %bitcast.13), custom_call_target="tpu_custom_call" | custom-call | tf_op jit(solution)/shard_map/pallas_call | solution.py:38
  3.5 7.7 %all-to-all-start = ((bf16[8,56,640]{2,1,0:T(8,128)(2,1)}), bf16[8,56,640]{2,1,0:T(8,128)(2,1)S(1)}, u32[]{:S(2)}, u32[]{:S(2)}) async-start(bf16[8,56,640]{2,1,0:T(8,128)(2,1)} %shard_map.93), calls=%async_computation | async-start | bytes 1146880 | tf_op jit(solution)/shard_map/all_to_all | solution.py:335
  11.2 12.2 %all-gather = bf16[1,512,640]{2,1,0:T(8,128)(2,1)S(1)} all-gather(bf16[1,128,640]{2,1,0:T(8,128)(2,1)S(1)} %copy-done), channel_id=2, replica_groups=mesh['z'=8,'core'=2,'y'=8,'x'=4] {'x'}, dimensions={1}, use_global_device_ids=true | all-gather | bytes 819200 | tf_op jit(solution)/shard_map/all_gather | solution.py:339
  23.4 6.4 %collective-permute-start = (bf16[512,640]{1,0:T(8,128)(2,1)S(1)}, bf16[512,640]{1,0:T(8,128)(2,1)S(1)}, u32[]{:S(2)}, u32[]{:S(2)}) collective-permute-start(bf16[512,640]{1,0:T(8,128)(2,1)S(1)} %bitcast.7), channel_id=1, source_target_pairs={{0,32},{32,0},{1,33},{33,1},{2,34},{34,2},{3,35},{35,3},{4,36},{36... | collective-permute-start | bytes 1966088 | tf_op jit(solution)/shard_map/ppermute | solution.py:327
  29.7 1.7 %collective-permute-done.theirs = bf16[512,640]{1,0:T(8,128)(2,1)S(1)} collective-permute-done((bf16[512,640]{1,0:T(8,128)(2,1)S(1)}, bf16[512,640]{1,0:T(8,128)(2,1)S(1)}, u32[]{:S(2)}, u32[]{:S(2)}) %collective-permute-start) | collective-permute-done | bytes 655392 | tf_op jit(solution)/shard_map/ppermute | solution.py:327
  31.5 0.0 all-to-all-done.got
  31.5 2.1 %shard_map.94 = (bf16[8,400,128]{2,1,0:T(8,128)(2,1)}, bf16[240,640]{1,0:T(8,128)(2,1)S(1)}, bf16[80,640]{1,0:T(8,128)(2,1)S(1)}, bf16[8,128,640]{2,1,0:T(8,128)(2,1)S(1)}) custom-call(bf16[512,640]{1,0:T(8,128)(2,1)S(1)} %bitcast.8, bf16[512,640]{1,0:T(8,128)(2,1)S(1)} %collective-permute-done.theirs, bf16[8,56,640]{2,1,0:T(8,128)(2,1)S(1)} %all-to-all-done.got), custom_call_target="tpu_custom_call" | custom-call | tf_op jit(solution)/shard_map/pallas_call | solution.py:38
  33.6 1.1 copy-done.1
  34.6 4.0 %all-to-all-start.1 = ((bf16[8,400,128]{2,1,0:T(8,128)(2,1)}), bf16[8,400,128]{2,1,0:T(8,128)(2,1)S(1)}, u32[]{:S(2)}, u32[]{:S(2)}) async-start(bf16[8,400,128]{2,1,0:T(8,128)(2,1)} %get-tuple-element.46), calls=%async_computation.1 | async-start | bytes 1638400 | tf_op jit(solution)/shard_map/all_to_all | solution.py:335
  38.6 4.5 %collective-permute-start.3 = (bf16[80,640]{1,0:T(8,128)(2,1)S(1)}, bf16[80,640]{1,0:T(8,128)(2,1)S(1)}, u32[]{:S(2)}, u32[]{:S(2)}) collective-permute-start(bf16[80,640]{1,0:T(8,128)(2,1)S(1)} %get-tuple-element.47), channel_id=1, source_target_pairs={{0,3},{1,0},{2,1},{3,2},{4,7},{5,4},{6,5},{7,6},{8,11},{9,8},{10,9... | collective-permute-start | bytes 307208 | tf_op jit(solution)/shard_map/ppermute | solution.py:319
  43.1 2.5 %collective-permute-start.2 = (bf16[80,640]{1,0:T(8,128)(2,1)S(1)}, bf16[80,640]{1,0:T(8,128)(2,1)S(1)}, u32[]{:S(2)}, u32[]{:S(2)}) collective-permute-start(bf16[80,640]{1,0:T(8,128)(2,1)S(1)} %get-tuple-element.47), channel_id=1, source_target_pairs={{0,2},{1,3},{2,0},{3,1},{4,6},{5,7},{6,4},{7,5},{8,10},{9,11},{10,... | collective-permute-start | bytes 307208 | tf_op jit(solution)/shard_map/ppermute | solution.py:319
  45.6 2.5 %collective-permute-start.1 = (bf16[80,640]{1,0:T(8,128)(2,1)S(1)}, bf16[80,640]{1,0:T(8,128)(2,1)S(1)}, u32[]{:S(2)}, u32[]{:S(2)}) collective-permute-start(bf16[80,640]{1,0:T(8,128)(2,1)S(1)} %get-tuple-element.47), channel_id=1, source_target_pairs={{0,1},{1,2},{2,3},{3,0},{4,5},{5,6},{6,7},{7,4},{8,9},{9,10},{10,1... | collective-permute-start | bytes 307208 | tf_op jit(solution)/shard_map/ppermute | solution.py:319
  48.1 3.9 %collective-permute-done.3 = bf16[80,640]{1,0:T(8,128)(2,1)S(1)} collective-permute-done((bf16[80,640]{1,0:T(8,128)(2,1)S(1)}, bf16[80,640]{1,0:T(8,128)(2,1)S(1)}, u32[]{:S(2)}, u32[]{:S(2)}) %collective-permute-start.3) | collective-permute-done | bytes 102432 | tf_op jit(solution)/shard_map/ppermute | solution.py:319
  52.0 1.6 %collective-permute-done.2 = bf16[80,640]{1,0:T(8,128)(2,1)S(1)} collective-permute-done((bf16[80,640]{1,0:T(8,128)(2,1)S(1)}, bf16[80,640]{1,0:T(8,128)(2,1)S(1)}, u32[]{:S(2)}, u32[]{:S(2)}) %collective-permute-start.2) | collective-permute-done | bytes 102432 | tf_op jit(solution)/shard_map/ppermute | solution.py:319
  53.6 1.8 %collective-permute-done.1 = bf16[80,640]{1,0:T(8,128)(2,1)S(1)} collective-permute-done((bf16[80,640]{1,0:T(8,128)(2,1)S(1)}, bf16[80,640]{1,0:T(8,128)(2,1)S(1)}, u32[]{:S(2)}, u32[]{:S(2)}) %collective-permute-start.1) | collective-permute-done | bytes 102432 | tf_op jit(solution)/shard_map/ppermute | solution.py:319
  55.4 2.8 %collective-permute-start.4 = (bf16[320,640]{1,0:T(8,128)(2,1)S(1)}, bf16[320,640]{1,0:T(8,128)(2,1)S(1)}, u32[]{:S(2)}, u32[]{:S(2)}) collective-permute-start(bf16[320,640]{1,0:T(8,128)(2,1)S(1)} %constant_dynamic-update-slice_fusion.out_mine), channel_id=1, source_target_pairs={{0,32},{32,0},{1,33},{33,1},{2,34},{34,2},{3,35},{35,3},{4,36},{36... | collective-permute-start | bytes 1228808 | tf_op jit(solution)/shard_map/ppermute | solution.py:327
  58.2 2.3 %shard_map.95 = (bf16[1920,128]{1,0:T(8,128)(2,1)S(1)}, f32[8,128,128]{2,1,0:T(8,128)S(1)}, bf16[640,128]{1,0:T(8,128)(2,1)S(1)}, bf16[128,640]{1,0:T(8,128)(2,1)S(1)}) custom-call(s32[32]{0:T(128)S(1)} %copy-done.5, bf16[8,400,128]{2,1,0:T(8,128)(2,1)S(1)} %all-to-all-done.1.got), custom_call_target="tpu_custom_call" | custom-call | tf_op jit(solution)/shard_map/pallas_call | solution.py:38
  60.5 4.3 %shard_map.96 = (bf16[8,640,128]{2,1,0:T(8,128)(2,1)S(1)}, bf16[128,640]{1,0:T(8,128)(2,1)S(1)}) custom-call(s32[32]{0:T(128)S(1)} %copy-done.5, s32[32]{0:T(128)S(1)} %copy-done.4, bf16[8,400,128]{2,1,0:T(8,128)(2,1)S(1)} %all-to-all-done.1.got, bf16[1920,128]{1,0:T(8,128)(2,1)S(1)} %get-tuple-element.49.qkv_t, f32[8,128,128]{2,1,0:T(8,128)S(1)} %get-tuple-element.50.prob, ...), custom_call_target="tpu_custom_call" | custom-call | tf_op jit(solution)/shard_map/pallas_call | solution.py:38
  64.9 1.1 copy-done.3
  66.0 3.5 %all-to-all-start.2 = ((bf16[8,640,128]{2,1,0:T(8,128)(2,1)}), bf16[8,640,128]{2,1,0:T(8,128)(2,1)S(1)}, u32[]{:S(2)}, u32[]{:S(2)}) async-start(bf16[8,640,128]{2,1,0:T(8,128)(2,1)} %copy-done.3), calls=%async_computation.2 | async-start | bytes 2621440 | tf_op jit(solution)/shard_map/all_to_all | solution.py:335
  69.5 1.3 shard_map.97
  70.8 3.2 %collective-permute-start.5 = (bf16[32,640]{1,0:T(8,128)(2,1)S(1)}, bf16[32,640]{1,0:T(8,128)(2,1)S(1)}, u32[]{:S(2)}, u32[]{:S(2)}) collective-permute-start(bf16[32,640]{1,0:T(8,128)(2,1)S(1)} %get-tuple-element.60), channel_id=1, source_target_pairs={{0,1},{1,2},{2,3},{3,0},{4,5},{5,6},{6,7},{7,4},{8,9},{9,10},{10,1... | collective-permute-start | bytes 122888 | tf_op jit(solution)/shard_map/ppermute | solution.py:319
  74.0 4.3 %collective-permute-start.6 = (bf16[32,640]{1,0:T(8,128)(2,1)S(1)}, bf16[32,640]{1,0:T(8,128)(2,1)S(1)}, u32[]{:S(2)}, u32[]{:S(2)}) collective-permute-start(bf16[32,640]{1,0:T(8,128)(2,1)S(1)} %get-tuple-element.61), channel_id=1, source_target_pairs={{0,2},{1,3},{2,0},{3,1},{4,6},{5,7},{6,4},{7,5},{8,10},{9,11},{10,... | collective-permute-start | bytes 122888 | tf_op jit(solution)/shard_map/ppermute | solution.py:319
  78.4 3.1 %collective-permute-start.7 = (bf16[32,640]{1,0:T(8,128)(2,1)S(1)}, bf16[32,640]{1,0:T(8,128)(2,1)S(1)}, u32[]{:S(2)}, u32[]{:S(2)}) collective-permute-start(bf16[32,640]{1,0:T(8,128)(2,1)S(1)} %get-tuple-element.62), channel_id=1, source_target_pairs={{0,3},{1,0},{2,1},{3,2},{4,7},{5,4},{6,5},{7,6},{8,11},{9,8},{10,9... | collective-permute-start | bytes 122888 | tf_op jit(solution)/shard_map/ppermute | solution.py:319
  81.5 6.6 %collective-permute-done.5.refs_1_ = bf16[32,640]{1,0:T(8,128)(2,1)S(1)} collective-permute-done((bf16[32,640]{1,0:T(8,128)(2,1)S(1)}, bf16[32,640]{1,0:T(8,128)(2,1)S(1)}, u32[]{:S(2)}, u32[]{:S(2)}) %collective-permute-start.5) | collective-permute-done | bytes 40992 | tf_op jit(solution)/shard_map/ppermute | solution.py:319
  88.1 0.8 collective-permute-done.6.refs_2_
  88.9 1.3 copy-done.2
  90.2 1.9 %shard_map.98 = bf16[8,56,640]{2,1,0:T(8,128)(2,1)} custom-call(bf16[8,640,128]{2,1,0:T(8,128)(2,1)S(1)} %all-to-all-done.2.got, bf16[8,128,640]{2,1,0:T(8,128)(2,1)S(1)} %copy-done.2, bf16[32,640]{1,0:T(8,128)(2,1)S(1)} %get-tuple-element.65.refs_0_, bf16[32,640]{1,0:T(8,128)(2,1)S(1)} %collective-permute-done.5.refs_1_, ...), custom_call_target="tpu_custom_call" | custom-call | tf_op jit(solution)/shard_map/pallas_call | solution.py:38
  92.0 6.8 %all-to-all-start.3 = ((bf16[8,56,640]{2,1,0:T(8,128)(2,1)}), bf16[8,56,640]{2,1,0:T(8,128)(2,1)S(1)}, u32[]{:S(2)}, u32[]{:S(2)}) async-start(bf16[8,56,640]{2,1,0:T(8,128)(2,1)} %shard_map.98), calls=%async_computation.3 | async-start | bytes 1146880 | tf_op jit(solution)/shard_map/all_to_all | solution.py:335
  98.8 0.6 shard_map.99
  99.5 3.4 %collective-permute-start.8 = (bf16[4,128,640]{2,1,0:T(8,128)(2,1)S(1)}, bf16[4,128,640]{2,1,0:T(8,128)(2,1)S(1)}, u32[]{:S(2)}, u32[]{:S(2)}) collective-permute-start(bf16[4,128,640]{2,1,0:T(8,128)(2,1)S(1)} %get-tuple-element.73), channel_id=1, source_target_pairs={{0,32},{32,0},{1,33},{33,1},{2,34},{34,2},{3,35},{35,3},{4,36},{36... | collective-permute-start | bytes 1966088 | tf_op jit(solution)/shard_map/ppermute | solution.py:327
  102.8 1.7 %collective-permute-done.8.theirs = bf16[4,128,640]{2,1,0:T(8,128)(2,1)S(1)} collective-permute-done((bf16[4,128,640]{2,1,0:T(8,128)(2,1)S(1)}, bf16[4,128,640]{2,1,0:T(8,128)(2,1)S(1)}, u32[]{:S(2)}, u32[]{:S(2)}) %collective-permute-start.8) | collective-permute-done | bytes 655392 | tf_op jit(solution)/shard_map/ppermute | solution.py:327
  104.5 0.2 shard_map.100
  104.7 2.1 %collective-permute-start.9 = (bf16[128,640]{1,0:T(8,128)(2,1)S(1)}, bf16[128,640]{1,0:T(8,128)(2,1)S(1)}, u32[]{:S(2)}, u32[]{:S(2)}) collective-permute-start(bf16[128,640]{1,0:T(8,128)(2,1)S(1)} %get-tuple-element.74), channel_id=1, source_target_pairs={{0,1},{1,2},{2,3},{3,0},{4,5},{5,6},{6,7},{7,4},{8,9},{9,10},{10,1... | collective-permute-start | bytes 491528 | tf_op jit(solution)/shard_map/ppermute | solution.py:319
  106.8 6.4 %collective-permute-done.9.refs_1_ = bf16[128,640]{1,0:T(8,128)(2,1)S(1)} collective-permute-done((bf16[128,640]{1,0:T(8,128)(2,1)S(1)}, bf16[128,640]{1,0:T(8,128)(2,1)S(1)}, u32[]{:S(2)}, u32[]{:S(2)}) %collective-permute-start.9) | collective-permute-done | bytes 163872 | tf_op jit(solution)/shard_map/ppermute | solution.py:319
  113.2 3.4 %all-to-all-done.3.came = bf16[8,56,640]{2,1,0:T(8,128)(2,1)S(1)} async-done(((bf16[8,56,640]{2,1,0:T(8,128)(2,1)}), bf16[8,56,640]{2,1,0:T(8,128)(2,1)S(1)}, u32[]{:S(2)}, u32[]{:S(2)}) %all-to-all-start.3) | async-done | bytes 573472 | tf_op jit(solution)/shard_map/all_to_all | solution.py:335
  116.6 0.1 slice_reduce_fusion
  116.6 0.8 broadcast_in_dim.2
  117.4 8.9 %all-to-all-start.4 = ((bf16[8,40,640]{2,1,0:T(8,128)(2,1)}), bf16[8,40,640]{2,1,0:T(8,128)(2,1)S(1)}, u32[]{:S(2)}, u32[]{:S(2)}) async-start(bf16[8,40,640]{2,1,0:T(8,128)(2,1)} %broadcast_in_dim.2), calls=%async_computation.4 | async-start | bytes 819200 | tf_op jit(solution)/shard_map/all_to_all | solution.py:335
  126.3 2.8 %collective-permute-start.10 = (bf16[128,640]{1,0:T(8,128)(2,1)S(1)}, bf16[128,640]{1,0:T(8,128)(2,1)S(1)}, u32[]{:S(2)}, u32[]{:S(2)}) collective-permute-start(bf16[128,640]{1,0:T(8,128)(2,1)S(1)} %get-tuple-element.81), channel_id=1, source_target_pairs={{0,2},{1,3},{2,0},{3,1},{4,6},{5,7},{6,4},{7,5},{8,10},{9,11},{10,... | collective-permute-start | bytes 491528 | tf_op jit(solution)/shard_map/ppermute | solution.py:319
  129.1 5.6 %collective-permute-start.11 = (bf16[128,640]{1,0:T(8,128)(2,1)S(1)}, bf16[128,640]{1,0:T(8,128)(2,1)S(1)}, u32[]{:S(2)}, u32[]{:S(2)}) collective-permute-start(bf16[128,640]{1,0:T(8,128)(2,1)S(1)} %get-tuple-element.82), channel_id=1, source_target_pairs={{0,3},{1,0},{2,1},{3,2},{4,7},{5,4},{6,5},{7,6},{8,11},{9,8},{10,9... | collective-permute-start | bytes 491528 | tf_op jit(solution)/shard_map/ppermute | solution.py:319
  134.7 1.5 %shard_map.102 = bf16[256,640]{1,0:T(8,128)(2,1)} custom-call(s32[32]{0:T(128)S(1)} %copy-done.4, bf16[8,56,640]{2,1,0:T(8,128)(2,1)S(1)} %all-to-all-done.3.came), custom_call_target="tpu_custom_call" | custom-call | tf_op jit(solution)/shard_map/pallas_call | solution.py:38
  136.2 2.3 %collective-permute-done.11.refs_3_ = bf16[128,640]{1,0:T(8,128)(2,1)S(1)} collective-permute-done((bf16[128,640]{1,0:T(8,128)(2,1)S(1)}, bf16[128,640]{1,0:T(8,128)(2,1)S(1)}, u32[]{:S(2)}, u32[]{:S(2)}) %collective-permute-start.11) | collective-permute-done | bytes 163872 | tf_op jit(solution)/shard_map/ppermute | solution.py:319
  138.5 0.9 shard_map.101
  139.4 0.1 convert_reduce_fusion
  139.5 4.8 %collective-permute-start.12 = (f32[40,640]{1,0:T(8,128)S(1)}, f32[40,640]{1,0:T(8,128)S(1)}, u32[]{:S(2)}, u32[]{:S(2)}) collective-permute-start(f32[40,640]{1,0:T(8,128)S(1)} %broadcast_multiply_fusion.own), channel_id=1, source_target_pairs={{0,32},{32,0},{1,33},{33,1},{2,34},{34,2},{3,35},{35,3},{4,36},{36... | collective-permute-start | bytes 307208 | tf_op jit(solution)/shard_map/ppermute | solution.py:327
  144.3 0.9 collective-permute-done.12.other
  145.2 0.7 shard_map.103
  (20 shorter events, 0.1 us)
Async XLA Ops:
  0.6 10.5 %copy-start = (bf16[1,128,640]{2,1,0:T(8,128)(2,1)S(1)}, bf16[1,128,640]{2,1,0:T(8,128)(2,1)}, u32[]{:S(2)}) copy-start(bf16[1,128,640]{2,1,0:T(8,128)(2,1)} %param.6) | copy-start | bytes 491524
  3.5 27.9 %all-to-all-start = ((bf16[8,56,640]{2,1,0:T(8,128)(2,1)}), bf16[8,56,640]{2,1,0:T(8,128)(2,1)S(1)}, u32[]{:S(2)}, u32[]{:S(2)}) async-start(bf16[8,56,640]{2,1,0:T(8,128)(2,1)} %shard_map.93), calls=%async_computation | async-start | bytes 1146880 | tf_op jit(solution)/shard_map/all_to_all | solution.py:335
  23.4 8.1 %collective-permute-start = (bf16[512,640]{1,0:T(8,128)(2,1)S(1)}, bf16[512,640]{1,0:T(8,128)(2,1)S(1)}, u32[]{:S(2)}, u32[]{:S(2)}) collective-permute-start(bf16[512,640]{1,0:T(8,128)(2,1)S(1)} %bitcast.7), channel_id=1, source_target_pairs={{0,32},{32,0},{1,33},{33,1},{2,34},{34,2},{3,35},{35,3},{4,36},{36... | collective-permute-start | bytes 1966088 | tf_op jit(solution)/shard_map/ppermute | solution.py:327
  33.6 1.1 copy-start.1
  34.6 23.6 %copy-start.5 = (s32[32]{0:T(128)S(1)}, s32[32]{0:T(128)}, u32[]{:S(2)}) copy-start(s32[32]{0:T(128)} %lengths.5) | copy-start | bytes 388
  34.6 25.9 %copy-start.4 = (s32[32]{0:T(128)S(1)}, s32[32]{0:T(128)}, u32[]{:S(2)}) copy-start(s32[32]{0:T(128)} %offsets.7) | copy-start | bytes 388
  34.6 20.7 %all-to-all-start.1 = ((bf16[8,400,128]{2,1,0:T(8,128)(2,1)}), bf16[8,400,128]{2,1,0:T(8,128)(2,1)S(1)}, u32[]{:S(2)}, u32[]{:S(2)}) async-start(bf16[8,400,128]{2,1,0:T(8,128)(2,1)} %get-tuple-element.46), calls=%async_computation.1 | async-start | bytes 1638400 | tf_op jit(solution)/shard_map/all_to_all | solution.py:335
  38.6 13.4 %collective-permute-start.3 = (bf16[80,640]{1,0:T(8,128)(2,1)S(1)}, bf16[80,640]{1,0:T(8,128)(2,1)S(1)}, u32[]{:S(2)}, u32[]{:S(2)}) collective-permute-start(bf16[80,640]{1,0:T(8,128)(2,1)S(1)} %get-tuple-element.47), channel_id=1, source_target_pairs={{0,3},{1,0},{2,1},{3,2},{4,7},{5,4},{6,5},{7,6},{8,11},{9,8},{10,9... | collective-permute-start | bytes 307208 | tf_op jit(solution)/shard_map/ppermute | solution.py:319
  43.1 10.4 %collective-permute-start.2 = (bf16[80,640]{1,0:T(8,128)(2,1)S(1)}, bf16[80,640]{1,0:T(8,128)(2,1)S(1)}, u32[]{:S(2)}, u32[]{:S(2)}) collective-permute-start(bf16[80,640]{1,0:T(8,128)(2,1)S(1)} %get-tuple-element.47), channel_id=1, source_target_pairs={{0,2},{1,3},{2,0},{3,1},{4,6},{5,7},{6,4},{7,5},{8,10},{9,11},{10,... | collective-permute-start | bytes 307208 | tf_op jit(solution)/shard_map/ppermute | solution.py:319
  45.6 9.8 %collective-permute-start.1 = (bf16[80,640]{1,0:T(8,128)(2,1)S(1)}, bf16[80,640]{1,0:T(8,128)(2,1)S(1)}, u32[]{:S(2)}, u32[]{:S(2)}) collective-permute-start(bf16[80,640]{1,0:T(8,128)(2,1)S(1)} %get-tuple-element.47), channel_id=1, source_target_pairs={{0,1},{1,2},{2,3},{3,0},{4,5},{5,6},{6,7},{7,4},{8,9},{9,10},{10,1... | collective-permute-start | bytes 307208 | tf_op jit(solution)/shard_map/ppermute | solution.py:319
  55.4 5.1 %collective-permute-start.4 = (bf16[320,640]{1,0:T(8,128)(2,1)S(1)}, bf16[320,640]{1,0:T(8,128)(2,1)S(1)}, u32[]{:S(2)}, u32[]{:S(2)}) collective-permute-start(bf16[320,640]{1,0:T(8,128)(2,1)S(1)} %constant_dynamic-update-slice_fusion.out_mine), channel_id=1, source_target_pairs={{0,32},{32,0},{1,33},{33,1},{2,34},{34,2},{3,35},{35,3},{4,36},{36... | collective-permute-start | bytes 1228808 | tf_op jit(solution)/shard_map/ppermute | solution.py:327
  64.9 1.1 copy-start.3
  66.0 22.9 %all-to-all-start.2 = ((bf16[8,640,128]{2,1,0:T(8,128)(2,1)}), bf16[8,640,128]{2,1,0:T(8,128)(2,1)S(1)}, u32[]{:S(2)}, u32[]{:S(2)}) async-start(bf16[8,640,128]{2,1,0:T(8,128)(2,1)} %copy-done.3), calls=%async_computation.2 | async-start | bytes 2621440 | tf_op jit(solution)/shard_map/all_to_all | solution.py:335
  70.8 17.3 %collective-permute-start.5 = (bf16[32,640]{1,0:T(8,128)(2,1)S(1)}, bf16[32,640]{1,0:T(8,128)(2,1)S(1)}, u32[]{:S(2)}, u32[]{:S(2)}) collective-permute-start(bf16[32,640]{1,0:T(8,128)(2,1)S(1)} %get-tuple-element.60), channel_id=1, source_target_pairs={{0,1},{1,2},{2,3},{3,0},{4,5},{5,6},{6,7},{7,4},{8,9},{9,10},{10,1... | collective-permute-start | bytes 122888 | tf_op jit(solution)/shard_map/ppermute | solution.py:319
  74.0 14.8 %collective-permute-start.6 = (bf16[32,640]{1,0:T(8,128)(2,1)S(1)}, bf16[32,640]{1,0:T(8,128)(2,1)S(1)}, u32[]{:S(2)}, u32[]{:S(2)}) collective-permute-start(bf16[32,640]{1,0:T(8,128)(2,1)S(1)} %get-tuple-element.61), channel_id=1, source_target_pairs={{0,2},{1,3},{2,0},{3,1},{4,6},{5,7},{6,4},{7,5},{8,10},{9,11},{10,... | collective-permute-start | bytes 122888 | tf_op jit(solution)/shard_map/ppermute | solution.py:319
  78.4 10.5 %collective-permute-start.7 = (bf16[32,640]{1,0:T(8,128)(2,1)S(1)}, bf16[32,640]{1,0:T(8,128)(2,1)S(1)}, u32[]{:S(2)}, u32[]{:S(2)}) collective-permute-start(bf16[32,640]{1,0:T(8,128)(2,1)S(1)} %get-tuple-element.62), channel_id=1, source_target_pairs={{0,3},{1,0},{2,1},{3,2},{4,7},{5,4},{6,5},{7,6},{8,11},{9,8},{10,9... | collective-permute-start | bytes 122888 | tf_op jit(solution)/shard_map/ppermute | solution.py:319
  88.9 1.3 copy-start.2
  92.0 24.5 %all-to-all-start.3 = ((bf16[8,56,640]{2,1,0:T(8,128)(2,1)}), bf16[8,56,640]{2,1,0:T(8,128)(2,1)S(1)}, u32[]{:S(2)}, u32[]{:S(2)}) async-start(bf16[8,56,640]{2,1,0:T(8,128)(2,1)} %shard_map.98), calls=%async_computation.3 | async-start | bytes 1146880 | tf_op jit(solution)/shard_map/all_to_all | solution.py:335
  99.5 5.1 %collective-permute-start.8 = (bf16[4,128,640]{2,1,0:T(8,128)(2,1)S(1)}, bf16[4,128,640]{2,1,0:T(8,128)(2,1)S(1)}, u32[]{:S(2)}, u32[]{:S(2)}) collective-permute-start(bf16[4,128,640]{2,1,0:T(8,128)(2,1)S(1)} %get-tuple-element.73), channel_id=1, source_target_pairs={{0,32},{32,0},{1,33},{33,1},{2,34},{34,2},{3,35},{35,3},{4,36},{36... | collective-permute-start | bytes 1966088 | tf_op jit(solution)/shard_map/ppermute | solution.py:327
  104.7 8.5 %collective-permute-start.9 = (bf16[128,640]{1,0:T(8,128)(2,1)S(1)}, bf16[128,640]{1,0:T(8,128)(2,1)S(1)}, u32[]{:S(2)}, u32[]{:S(2)}) collective-permute-start(bf16[128,640]{1,0:T(8,128)(2,1)S(1)} %get-tuple-element.74), channel_id=1, source_target_pairs={{0,1},{1,2},{2,3},{3,0},{4,5},{5,6},{6,7},{7,4},{8,9},{9,10},{10,1... | collective-permute-start | bytes 491528 | tf_op jit(solution)/shard_map/ppermute | solution.py:319
  117.4 22.0 %all-to-all-start.4 = ((bf16[8,40,640]{2,1,0:T(8,128)(2,1)}), bf16[8,40,640]{2,1,0:T(8,128)(2,1)S(1)}, u32[]{:S(2)}, u32[]{:S(2)}) async-start(bf16[8,40,640]{2,1,0:T(8,128)(2,1)} %broadcast_in_dim.2), calls=%async_computation.4 | async-start | bytes 819200 | tf_op jit(solution)/shard_map/all_to_all | solution.py:335
  126.3 9.9 %collective-permute-start.10 = (bf16[128,640]{1,0:T(8,128)(2,1)S(1)}, bf16[128,640]{1,0:T(8,128)(2,1)S(1)}, u32[]{:S(2)}, u32[]{:S(2)}) collective-permute-start(bf16[128,640]{1,0:T(8,128)(2,1)S(1)} %get-tuple-element.81), channel_id=1, source_target_pairs={{0,2},{1,3},{2,0},{3,1},{4,6},{5,7},{6,4},{7,5},{8,10},{9,11},{10,... | collective-permute-start | bytes 491528 | tf_op jit(solution)/shard_map/ppermute | solution.py:319
  129.1 9.4 %collective-permute-start.11 = (bf16[128,640]{1,0:T(8,128)(2,1)S(1)}, bf16[128,640]{1,0:T(8,128)(2,1)S(1)}, u32[]{:S(2)}, u32[]{:S(2)}) collective-permute-start(bf16[128,640]{1,0:T(8,128)(2,1)S(1)} %get-tuple-element.82), channel_id=1, source_target_pairs={{0,3},{1,0},{2,1},{3,2},{4,7},{5,4},{6,5},{7,6},{8,11},{9,8},{10,9... | collective-permute-start | bytes 491528 | tf_op jit(solution)/shard_map/ppermute | solution.py:319
  139.5 5.7 %collective-permute-start.12 = (f32[40,640]{1,0:T(8,128)S(1)}, f32[40,640]{1,0:T(8,128)S(1)}, u32[]{:S(2)}, u32[]{:S(2)}) collective-permute-start(f32[40,640]{1,0:T(8,128)S(1)} %broadcast_multiply_fusion.own), channel_id=1, source_target_pairs={{0,32},{32,0},{1,33},{33,1},{2,34},{34,2},{3,35},{35,3},{4,36},{36... | collective-permute-start | bytes 307208 | tf_op jit(solution)/shard_map/ppermute | solution.py:327

commit v4 on v3

--- a/solution.py
+++ b/solution.py
@@ -31,9 +31,9 @@
     return lax.dot_general(a, b, (((ca,), (cb,)), ((), ())), preferred_element_type=F32)
 
 
-def call(kernel, out_shape, scratch, *args, smem=1, space=pltpu.VMEM, limit=VMEM_LIMIT):
+def call(kernel, out_shape, scratch, *args, smem=1, limit=VMEM_LIMIT):
     specs = [pl.BlockSpec(memory_space=pltpu.SMEM)] * smem + [
-        pl.BlockSpec(memory_space=space)
+        pl.BlockSpec(memory_space=pltpu.VMEM)
     ] * (len(args) - smem)
     return pl.pallas_call(
         kernel,
@@ -99,21 +99,10 @@
                 yield core * NX + x, y, 2 * (NX * y + x) + core
 
 
-def pre_kernel(offsets, *refs):
-    sources, send, targets, sems, fq, fo = refs[:3], refs[3], refs[4:7], refs[7], *refs[8:]
-    copies = [
-        pltpu.make_async_copy(source, target, sems.at[n])
-        for n, (source, target) in enumerate(zip(sources, targets, strict=True))
-    ]
-    for copy in copies:
-        copy.start()
-    d_embeds, wq, wo = targets
+def pre_kernel(offsets, d_embeds, wq, wo, send, fq, fo):
     first = here()[0] == 0
-    seq_rows = d_embeds.shape[0]
-    row = lax.broadcasted_iota(jnp.int32, (seq_rows, CAP), 0)
+    row = lax.broadcasted_iota(jnp.int32, (d_embeds.shape[0], CAP), 0)
     pick = one_hot(row == target_rows(offsets))
-    for copy in copies:
-        copy.wait()
     fetched = dot(pick, d_embeds[...], 0, 0).astype(BF)
     fq[...] = wq[...].astype(F32)
     fo[...] = wo[...].astype(F32)
@@ -348,15 +337,8 @@
     send = call(
         pre_kernel,
         sds((NY, EY + PIECE, D)),
-        [
-            scratch(d_embeds.shape, BF),
-            scratch((2 * QP, D), BF),
-            scratch((2 * OP, D), BF),
-            pltpu.SemaphoreType.DMA((3,)),
-            scratch((2 * QP, D), F32),
-            scratch((2 * OP, D), F32),
-        ],
-        offsets, d_embeds, w_qkv.T, w_out.T, space=pltpu.HBM, limit=None,
+        [scratch((2 * QP, D), F32), scratch((2 * OP, D), F32)],
+        offsets, d_embeds, w_qkv.T, w_out.T, limit=56 * 1024 * 1024,
     )
     got = exchange(send, "y")
     mine = gather(tokens, "x")

time: 147 us -> 146 us (level)
  no operation moved by 1% of the time
where the time goes in v4:
time: 146 us; the launch traced here: 145 us
  starting transfers between devices  78.7 us (54%)
  waiting for transfers between devices  31.1 us (21%)
  Pallas kernels  17.9 us (12%)
  blocking collectives  12.2 us (8%)
  local copies, waits for them, and re-layouts  4.33 us (3%)
    all_to_all x5, starting transfers between devices, exchange(): return lax.all_to_all(a, axis, split_axis=0, concat_axis=0, tiled=True)  30.8 us
    ppermute x9, starting transfers between devices, along_x(): return lax.ppermute(a, 'x', [(x, target(x)) for x in range(NX)])  30.6 us
    ppermute x9, waiting for transfers between devices, along_x(): return lax.ppermute(a, 'x', [(x, target(x)) for x in range(NX)])  23.3 us
    pallas_call x11, Pallas kernels, call(): pl.pallas_call(kernel, out_shape=out_shape, in_specs=specs, out_specs=jax...  17.9 us
    ppermute x4, starting transfers between devices, swap(): return lax.ppermute(a, 'core', [(0, 1), (1, 0)])  17.3 us
    all_gather x1, blocking collectives, gather(): return lax.all_gather(a, axis, axis=0, tiled=True)  12.2 us
    ppermute x4, waiting for transfers between devices, swap(): return lax.ppermute(a, 'core', [(0, 1), (1, 0)])  4.33 us
    unnamed x15, local copies, waits for them, and re-layouts  3.52 us
  transfers between devices with their start and end apart: 18, of which 11 were waited for; matrix products, arithmetic and copies ran while one was open for 0% of the time, Pallas kernels for 5%

profile of v4, /device:TPU:1, one launch (start us, length us, event | category | flops | bytes accessed | tf_op | source)
XLA Modules:
  0.0 145.2 jit_solution(8868706309934853484)
XLA Ops:
  0.6 2.2 %shard_map.93 = bf16[8,56,640]{2,1,0:T(8,128)(2,1)} custom-call(s32[32]{0:T(128)} %offsets.7, bf16[256,640]{1,0:T(8,128)(2,1)} %d_embeds.1, bf16[60,640]{1,0:T(8,128)(2,1)} %bitcast.12, bf16[20,640]{1,0:T(8,128)(2,1)} %bitcast.13), custom_call_target="tpu_custom_call" | custom-call | tf_op jit(solution)/shard_map/pallas_call | solution.py:38
  2.8 7.7 %all-to-all-start = ((bf16[8,56,640]{2,1,0:T(8,128)(2,1)}), bf16[8,56,640]{2,1,0:T(8,128)(2,1)S(1)}, u32[]{:S(2)}, u32[]{:S(2)}) async-start(bf16[8,56,640]{2,1,0:T(8,128)(2,1)} %shard_map.93), calls=%async_computation | async-start | bytes 1146880 | tf_op jit(solution)/shard_map/all_to_all | solution.py:324
  10.5 12.2 %all-gather = bf16[1,512,640]{2,1,0:T(8,128)(2,1)S(1)} all-gather(bf16[1,128,640]{2,1,0:T(8,128)(2,1)S(1)} %copy-done), channel_id=2, replica_groups=mesh['z'=8,'core'=2,'y'=8,'x'=4] {'x'}, dimensions={1}, use_global_device_ids=true | all-gather | bytes 819200 | tf_op jit(solution)/shard_map/all_gather | solution.py:328
  22.7 6.4 %collective-permute-start = (bf16[512,640]{1,0:T(8,128)(2,1)S(1)}, bf16[512,640]{1,0:T(8,128)(2,1)S(1)}, u32[]{:S(2)}, u32[]{:S(2)}) collective-permute-start(bf16[512,640]{1,0:T(8,128)(2,1)S(1)} %bitcast.7), channel_id=1, source_target_pairs={{0,32},{32,0},{1,33},{33,1},{2,34},{34,2},{3,35},{35,3},{4,36},{36... | collective-permute-start | bytes 1966088 | tf_op jit(solution)/shard_map/ppermute | solution.py:316
  29.0 1.7 %collective-permute-done.theirs = bf16[512,640]{1,0:T(8,128)(2,1)S(1)} collective-permute-done((bf16[512,640]{1,0:T(8,128)(2,1)S(1)}, bf16[512,640]{1,0:T(8,128)(2,1)S(1)}, u32[]{:S(2)}, u32[]{:S(2)}) %collective-permute-start) | collective-permute-done | bytes 655392 | tf_op jit(solution)/shard_map/ppermute | solution.py:316
  30.8 0.0 all-to-all-done.got
  30.8 2.1 %shard_map.94 = (bf16[8,400,128]{2,1,0:T(8,128)(2,1)}, bf16[240,640]{1,0:T(8,128)(2,1)S(1)}, bf16[80,640]{1,0:T(8,128)(2,1)S(1)}, bf16[8,128,640]{2,1,0:T(8,128)(2,1)S(1)}) custom-call(bf16[512,640]{1,0:T(8,128)(2,1)S(1)} %bitcast.8, bf16[512,640]{1,0:T(8,128)(2,1)S(1)} %collective-permute-done.theirs, bf16[8,56,640]{2,1,0:T(8,128)(2,1)S(1)} %all-to-all-done.got), custom_call_target="tpu_custom_call" | custom-call | tf_op jit(solution)/shard_map/pallas_call | solution.py:38
  32.9 1.1 copy-done.1
  33.9 4.0 %all-to-all-start.1 = ((bf16[8,400,128]{2,1,0:T(8,128)(2,1)}), bf16[8,400,128]{2,1,0:T(8,128)(2,1)S(1)}, u32[]{:S(2)}, u32[]{:S(2)}) async-start(bf16[8,400,128]{2,1,0:T(8,128)(2,1)} %get-tuple-element.46), calls=%async_computation.1 | async-start | bytes 1638400 | tf_op jit(solution)/shard_map/all_to_all | solution.py:324
  37.9 4.5 %collective-permute-start.3 = (bf16[80,640]{1,0:T(8,128)(2,1)S(1)}, bf16[80,640]{1,0:T(8,128)(2,1)S(1)}, u32[]{:S(2)}, u32[]{:S(2)}) collective-permute-start(bf16[80,640]{1,0:T(8,128)(2,1)S(1)} %get-tuple-element.47), channel_id=1, source_target_pairs={{0,3},{1,0},{2,1},{3,2},{4,7},{5,4},{6,5},{7,6},{8,11},{9,8},{10,9... | collective-permute-start | bytes 307208 | tf_op jit(solution)/shard_map/ppermute | solution.py:308
  42.4 2.5 %collective-permute-start.2 = (bf16[80,640]{1,0:T(8,128)(2,1)S(1)}, bf16[80,640]{1,0:T(8,128)(2,1)S(1)}, u32[]{:S(2)}, u32[]{:S(2)}) collective-permute-start(bf16[80,640]{1,0:T(8,128)(2,1)S(1)} %get-tuple-element.47), channel_id=1, source_target_pairs={{0,2},{1,3},{2,0},{3,1},{4,6},{5,7},{6,4},{7,5},{8,10},{9,11},{10,... | collective-permute-start | bytes 307208 | tf_op jit(solution)/shard_map/ppermute | solution.py:308
  44.9 2.5 %collective-permute-start.1 = (bf16[80,640]{1,0:T(8,128)(2,1)S(1)}, bf16[80,640]{1,0:T(8,128)(2,1)S(1)}, u32[]{:S(2)}, u32[]{:S(2)}) collective-permute-start(bf16[80,640]{1,0:T(8,128)(2,1)S(1)} %get-tuple-element.47), channel_id=1, source_target_pairs={{0,1},{1,2},{2,3},{3,0},{4,5},{5,6},{6,7},{7,4},{8,9},{9,10},{10,1... | collective-permute-start | bytes 307208 | tf_op jit(solution)/shard_map/ppermute | solution.py:308
  47.4 3.9 %collective-permute-done.3 = bf16[80,640]{1,0:T(8,128)(2,1)S(1)} collective-permute-done((bf16[80,640]{1,0:T(8,128)(2,1)S(1)}, bf16[80,640]{1,0:T(8,128)(2,1)S(1)}, u32[]{:S(2)}, u32[]{:S(2)}) %collective-permute-start.3) | collective-permute-done | bytes 102432 | tf_op jit(solution)/shard_map/ppermute | solution.py:308
  51.3 1.6 %collective-permute-done.2 = bf16[80,640]{1,0:T(8,128)(2,1)S(1)} collective-permute-done((bf16[80,640]{1,0:T(8,128)(2,1)S(1)}, bf16[80,640]{1,0:T(8,128)(2,1)S(1)}, u32[]{:S(2)}, u32[]{:S(2)}) %collective-permute-start.2) | collective-permute-done | bytes 102432 | tf_op jit(solution)/shard_map/ppermute | solution.py:308
  52.8 1.8 %collective-permute-done.1 = bf16[80,640]{1,0:T(8,128)(2,1)S(1)} collective-permute-done((bf16[80,640]{1,0:T(8,128)(2,1)S(1)}, bf16[80,640]{1,0:T(8,128)(2,1)S(1)}, u32[]{:S(2)}, u32[]{:S(2)}) %collective-permute-start.1) | collective-permute-done | bytes 102432 | tf_op jit(solution)/shard_map/ppermute | solution.py:308
  54.7 2.8 %collective-permute-start.4 = (bf16[320,640]{1,0:T(8,128)(2,1)S(1)}, bf16[320,640]{1,0:T(8,128)(2,1)S(1)}, u32[]{:S(2)}, u32[]{:S(2)}) collective-permute-start(bf16[320,640]{1,0:T(8,128)(2,1)S(1)} %constant_dynamic-update-slice_fusion.out_mine), channel_id=1, source_target_pairs={{0,32},{32,0},{1,33},{33,1},{2,34},{34,2},{3,35},{35,3},{4,36},{36... | collective-permute-start | bytes 1228808 | tf_op jit(solution)/shard_map/ppermute | solution.py:316
  57.5 2.3 %shard_map.95 = (bf16[1920,128]{1,0:T(8,128)(2,1)S(1)}, f32[8,128,128]{2,1,0:T(8,128)S(1)}, bf16[640,128]{1,0:T(8,128)(2,1)S(1)}, bf16[128,640]{1,0:T(8,128)(2,1)S(1)}) custom-call(s32[32]{0:T(128)S(1)} %copy-done.5, bf16[8,400,128]{2,1,0:T(8,128)(2,1)S(1)} %all-to-all-done.1.got), custom_call_target="tpu_custom_call" | custom-call | tf_op jit(solution)/shard_map/pallas_call | solution.py:38
  59.8 4.3 %shard_map.96 = (bf16[8,640,128]{2,1,0:T(8,128)(2,1)S(1)}, bf16[128,640]{1,0:T(8,128)(2,1)S(1)}) custom-call(s32[32]{0:T(128)S(1)} %copy-done.5, s32[32]{0:T(128)S(1)} %copy-done.4, bf16[8,400,128]{2,1,0:T(8,128)(2,1)S(1)} %all-to-all-done.1.got, bf16[1920,128]{1,0:T(8,128)(2,1)S(1)} %get-tuple-element.49.qkv_t, f32[8,128,128]{2,1,0:T(8,128)S(1)} %get-tuple-element.50.prob, ...), custom_call_target="tpu_custom_call" | custom-call | tf_op jit(solution)/shard_map/pallas_call | solution.py:38
  64.2 1.1 copy-done.3
  65.3 3.5 %all-to-all-start.2 = ((bf16[8,640,128]{2,1,0:T(8,128)(2,1)}), bf16[8,640,128]{2,1,0:T(8,128)(2,1)S(1)}, u32[]{:S(2)}, u32[]{:S(2)}) async-start(bf16[8,640,128]{2,1,0:T(8,128)(2,1)} %copy-done.3), calls=%async_computation.2 | async-start | bytes 2621440 | tf_op jit(solution)/shard_map/all_to_all | solution.py:324
  68.8 1.3 shard_map.97
  70.1 3.2 %collective-permute-start.5 = (bf16[32,640]{1,0:T(8,128)(2,1)S(1)}, bf16[32,640]{1,0:T(8,128)(2,1)S(1)}, u32[]{:S(2)}, u32[]{:S(2)}) collective-permute-start(bf16[32,640]{1,0:T(8,128)(2,1)S(1)} %get-tuple-element.60), channel_id=1, source_target_pairs={{0,1},{1,2},{2,3},{3,0},{4,5},{5,6},{6,7},{7,4},{8,9},{9,10},{10,1... | collective-permute-start | bytes 122888 | tf_op jit(solution)/shard_map/ppermute | solution.py:308
  73.3 4.3 %collective-permute-start.6 = (bf16[32,640]{1,0:T(8,128)(2,1)S(1)}, bf16[32,640]{1,0:T(8,128)(2,1)S(1)}, u32[]{:S(2)}, u32[]{:S(2)}) collective-permute-start(bf16[32,640]{1,0:T(8,128)(2,1)S(1)} %get-tuple-element.61), channel_id=1, source_target_pairs={{0,2},{1,3},{2,0},{3,1},{4,6},{5,7},{6,4},{7,5},{8,10},{9,11},{10,... | collective-permute-start | bytes 122888 | tf_op jit(solution)/shard_map/ppermute | solution.py:308
  77.7 3.1 %collective-permute-start.7 = (bf16[32,640]{1,0:T(8,128)(2,1)S(1)}, bf16[32,640]{1,0:T(8,128)(2,1)S(1)}, u32[]{:S(2)}, u32[]{:S(2)}) collective-permute-start(bf16[32,640]{1,0:T(8,128)(2,1)S(1)} %get-tuple-element.62), channel_id=1, source_target_pairs={{0,3},{1,0},{2,1},{3,2},{4,7},{5,4},{6,5},{7,6},{8,11},{9,8},{10,9... | collective-permute-start | bytes 122888 | tf_op jit(solution)/shard_map/ppermute | solution.py:308
  80.8 6.6 %collective-permute-done.5.refs_1_ = bf16[32,640]{1,0:T(8,128)(2,1)S(1)} collective-permute-done((bf16[32,640]{1,0:T(8,128)(2,1)S(1)}, bf16[32,640]{1,0:T(8,128)(2,1)S(1)}, u32[]{:S(2)}, u32[]{:S(2)}) %collective-permute-start.5) | collective-permute-done | bytes 40992 | tf_op jit(solution)/shard_map/ppermute | solution.py:308
  87.4 0.8 collective-permute-done.6.refs_2_
  88.2 1.3 copy-done.2
  89.5 1.9 %shard_map.98 = bf16[8,56,640]{2,1,0:T(8,128)(2,1)} custom-call(bf16[8,640,128]{2,1,0:T(8,128)(2,1)S(1)} %all-to-all-done.2.got, bf16[8,128,640]{2,1,0:T(8,128)(2,1)S(1)} %copy-done.2, bf16[32,640]{1,0:T(8,128)(2,1)S(1)} %get-tuple-element.65.refs_0_, bf16[32,640]{1,0:T(8,128)(2,1)S(1)} %collective-permute-done.5.refs_1_, ...), custom_call_target="tpu_custom_call" | custom-call | tf_op jit(solution)/shard_map/pallas_call | solution.py:38
  91.3 6.8 %all-to-all-start.3 = ((bf16[8,56,640]{2,1,0:T(8,128)(2,1)}), bf16[8,56,640]{2,1,0:T(8,128)(2,1)S(1)}, u32[]{:S(2)}, u32[]{:S(2)}) async-start(bf16[8,56,640]{2,1,0:T(8,128)(2,1)} %shard_map.98), calls=%async_computation.3 | async-start | bytes 1146880 | tf_op jit(solution)/shard_map/all_to_all | solution.py:324
  98.1 0.6 shard_map.99
  98.8 3.4 %collective-permute-start.8 = (bf16[4,128,640]{2,1,0:T(8,128)(2,1)S(1)}, bf16[4,128,640]{2,1,0:T(8,128)(2,1)S(1)}, u32[]{:S(2)}, u32[]{:S(2)}) collective-permute-start(bf16[4,128,640]{2,1,0:T(8,128)(2,1)S(1)} %get-tuple-element.73), channel_id=1, source_target_pairs={{0,32},{32,0},{1,33},{33,1},{2,34},{34,2},{3,35},{35,3},{4,36},{36... | collective-permute-start | bytes 1966088 | tf_op jit(solution)/shard_map/ppermute | solution.py:316
  102.1 1.7 %collective-permute-done.8.theirs = bf16[4,128,640]{2,1,0:T(8,128)(2,1)S(1)} collective-permute-done((bf16[4,128,640]{2,1,0:T(8,128)(2,1)S(1)}, bf16[4,128,640]{2,1,0:T(8,128)(2,1)S(1)}, u32[]{:S(2)}, u32[]{:S(2)}) %collective-permute-start.8) | collective-permute-done | bytes 655392 | tf_op jit(solution)/shard_map/ppermute | solution.py:316
  103.8 0.2 shard_map.100
  104.0 2.1 %collective-permute-start.9 = (bf16[128,640]{1,0:T(8,128)(2,1)S(1)}, bf16[128,640]{1,0:T(8,128)(2,1)S(1)}, u32[]{:S(2)}, u32[]{:S(2)}) collective-permute-start(bf16[128,640]{1,0:T(8,128)(2,1)S(1)} %get-tuple-element.74), channel_id=1, source_target_pairs={{0,1},{1,2},{2,3},{3,0},{4,5},{5,6},{6,7},{7,4},{8,9},{9,10},{10,1... | collective-permute-start | bytes 491528 | tf_op jit(solution)/shard_map/ppermute | solution.py:308
  106.1 6.4 %collective-permute-done.9.refs_1_ = bf16[128,640]{1,0:T(8,128)(2,1)S(1)} collective-permute-done((bf16[128,640]{1,0:T(8,128)(2,1)S(1)}, bf16[128,640]{1,0:T(8,128)(2,1)S(1)}, u32[]{:S(2)}, u32[]{:S(2)}) %collective-permute-start.9) | collective-permute-done | bytes 163872 | tf_op jit(solution)/shard_map/ppermute | solution.py:308
  112.5 3.4 %all-to-all-done.3.came = bf16[8,56,640]{2,1,0:T(8,128)(2,1)S(1)} async-done(((bf16[8,56,640]{2,1,0:T(8,128)(2,1)}), bf16[8,56,640]{2,1,0:T(8,128)(2,1)S(1)}, u32[]{:S(2)}, u32[]{:S(2)}) %all-to-all-start.3) | async-done | bytes 573472 | tf_op jit(solution)/shard_map/all_to_all | solution.py:324
  115.9 0.1 slice_reduce_fusion
  115.9 0.8 broadcast_in_dim.2
  116.7 8.9 %all-to-all-start.4 = ((bf16[8,40,640]{2,1,0:T(8,128)(2,1)}), bf16[8,40,640]{2,1,0:T(8,128)(2,1)S(1)}, u32[]{:S(2)}, u32[]{:S(2)}) async-start(bf16[8,40,640]{2,1,0:T(8,128)(2,1)} %broadcast_in_dim.2), calls=%async_computation.4 | async-start | bytes 819200 | tf_op jit(solution)/shard_map/all_to_all | solution.py:324
  125.6 2.8 %collective-permute-start.10 = (bf16[128,640]{1,0:T(8,128)(2,1)S(1)}, bf16[128,640]{1,0:T(8,128)(2,1)S(1)}, u32[]{:S(2)}, u32[]{:S(2)}) collective-permute-start(bf16[128,640]{1,0:T(8,128)(2,1)S(1)} %get-tuple-element.81), channel_id=1, source_target_pairs={{0,2},{1,3},{2,0},{3,1},{4,6},{5,7},{6,4},{7,5},{8,10},{9,11},{10,... | collective-permute-start | bytes 491528 | tf_op jit(solution)/shard_map/ppermute | solution.py:308
  128.4 5.6 %collective-permute-start.11 = (bf16[128,640]{1,0:T(8,128)(2,1)S(1)}, bf16[128,640]{1,0:T(8,128)(2,1)S(1)}, u32[]{:S(2)}, u32[]{:S(2)}) collective-permute-start(bf16[128,640]{1,0:T(8,128)(2,1)S(1)} %get-tuple-element.82), channel_id=1, source_target_pairs={{0,3},{1,0},{2,1},{3,2},{4,7},{5,4},{6,5},{7,6},{8,11},{9,8},{10,9... | collective-permute-start | bytes 491528 | tf_op jit(solution)/shard_map/ppermute | solution.py:308
  134.0 1.5 %shard_map.102 = bf16[256,640]{1,0:T(8,128)(2,1)} custom-call(s32[32]{0:T(128)S(1)} %copy-done.4, bf16[8,56,640]{2,1,0:T(8,128)(2,1)S(1)} %all-to-all-done.3.came), custom_call_target="tpu_custom_call" | custom-call | tf_op jit(solution)/shard_map/pallas_call | solution.py:38
  135.5 2.3 %collective-permute-done.11.refs_3_ = bf16[128,640]{1,0:T(8,128)(2,1)S(1)} collective-permute-done((bf16[128,640]{1,0:T(8,128)(2,1)S(1)}, bf16[128,640]{1,0:T(8,128)(2,1)S(1)}, u32[]{:S(2)}, u32[]{:S(2)}) %collective-permute-start.11) | collective-permute-done | bytes 163872 | tf_op jit(solution)/shard_map/ppermute | solution.py:308
  137.8 0.9 shard_map.101
  138.7 0.1 convert_reduce_fusion
  138.8 4.8 %collective-permute-start.12 = (f32[40,640]{1,0:T(8,128)S(1)}, f32[40,640]{1,0:T(8,128)S(1)}, u32[]{:S(2)}, u32[]{:S(2)}) collective-permute-start(f32[40,640]{1,0:T(8,128)S(1)} %broadcast_multiply_fusion.own), channel_id=1, source_target_pairs={{0,32},{32,0},{1,33},{33,1},{2,34},{34,2},{3,35},{35,3},{4,36},{36... | collective-permute-start | bytes 307208 | tf_op jit(solution)/shard_map/ppermute | solution.py:316
  143.6 0.9 collective-permute-done.12.other
  144.5 0.7 shard_map.103
  (20 shorter events, 0.1 us)
Async XLA Ops:
  0.6 9.8 %copy-start = (bf16[1,128,640]{2,1,0:T(8,128)(2,1)S(1)}, bf16[1,128,640]{2,1,0:T(8,128)(2,1)}, u32[]{:S(2)}) copy-start(bf16[1,128,640]{2,1,0:T(8,128)(2,1)} %param.6) | copy-start | bytes 491524
  2.8 27.9 %all-to-all-start = ((bf16[8,56,640]{2,1,0:T(8,128)(2,1)}), bf16[8,56,640]{2,1,0:T(8,128)(2,1)S(1)}, u32[]{:S(2)}, u32[]{:S(2)}) async-start(bf16[8,56,640]{2,1,0:T(8,128)(2,1)} %shard_map.93), calls=%async_computation | async-start | bytes 1146880 | tf_op jit(solution)/shard_map/all_to_all | solution.py:324
  22.7 8.1 %collective-permute-start = (bf16[512,640]{1,0:T(8,128)(2,1)S(1)}, bf16[512,640]{1,0:T(8,128)(2,1)S(1)}, u32[]{:S(2)}, u32[]{:S(2)}) collective-permute-start(bf16[512,640]{1,0:T(8,128)(2,1)S(1)} %bitcast.7), channel_id=1, source_target_pairs={{0,32},{32,0},{1,33},{33,1},{2,34},{34,2},{3,35},{35,3},{4,36},{36... | collective-permute-start | bytes 1966088 | tf_op jit(solution)/shard_map/ppermute | solution.py:316
  32.9 1.1 copy-start.1
  33.9 23.6 %copy-start.5 = (s32[32]{0:T(128)S(1)}, s32[32]{0:T(128)}, u32[]{:S(2)}) copy-start(s32[32]{0:T(128)} %lengths.5) | copy-start | bytes 388
  33.9 25.9 %copy-start.4 = (s32[32]{0:T(128)S(1)}, s32[32]{0:T(128)}, u32[]{:S(2)}) copy-start(s32[32]{0:T(128)} %offsets.7) | copy-start | bytes 388
  33.9 20.7 %all-to-all-start.1 = ((bf16[8,400,128]{2,1,0:T(8,128)(2,1)}), bf16[8,400,128]{2,1,0:T(8,128)(2,1)S(1)}, u32[]{:S(2)}, u32[]{:S(2)}) async-start(bf16[8,400,128]{2,1,0:T(8,128)(2,1)} %get-tuple-element.46), calls=%async_computation.1 | async-start | bytes 1638400 | tf_op jit(solution)/shard_map/all_to_all | solution.py:324
  37.9 13.4 %collective-permute-start.3 = (bf16[80,640]{1,0:T(8,128)(2,1)S(1)}, bf16[80,640]{1,0:T(8,128)(2,1)S(1)}, u32[]{:S(2)}, u32[]{:S(2)}) collective-permute-start(bf16[80,640]{1,0:T(8,128)(2,1)S(1)} %get-tuple-element.47), channel_id=1, source_target_pairs={{0,3},{1,0},{2,1},{3,2},{4,7},{5,4},{6,5},{7,6},{8,11},{9,8},{10,9... | collective-permute-start | bytes 307208 | tf_op jit(solution)/shard_map/ppermute | solution.py:308
  42.4 10.4 %collective-permute-start.2 = (bf16[80,640]{1,0:T(8,128)(2,1)S(1)}, bf16[80,640]{1,0:T(8,128)(2,1)S(1)}, u32[]{:S(2)}, u32[]{:S(2)}) collective-permute-start(bf16[80,640]{1,0:T(8,128)(2,1)S(1)} %get-tuple-element.47), channel_id=1, source_target_pairs={{0,2},{1,3},{2,0},{3,1},{4,6},{5,7},{6,4},{7,5},{8,10},{9,11},{10,... | collective-permute-start | bytes 307208 | tf_op jit(solution)/shard_map/ppermute | solution.py:308
  44.9 9.8 %collective-permute-start.1 = (bf16[80,640]{1,0:T(8,128)(2,1)S(1)}, bf16[80,640]{1,0:T(8,128)(2,1)S(1)}, u32[]{:S(2)}, u32[]{:S(2)}) collective-permute-start(bf16[80,640]{1,0:T(8,128)(2,1)S(1)} %get-tuple-element.47), channel_id=1, source_target_pairs={{0,1},{1,2},{2,3},{3,0},{4,5},{5,6},{6,7},{7,4},{8,9},{9,10},{10,1... | collective-permute-start | bytes 307208 | tf_op jit(solution)/shard_map/ppermute | solution.py:308
  54.7 5.1 %collective-permute-start.4 = (bf16[320,640]{1,0:T(8,128)(2,1)S(1)}, bf16[320,640]{1,0:T(8,128)(2,1)S(1)}, u32[]{:S(2)}, u32[]{:S(2)}) collective-permute-start(bf16[320,640]{1,0:T(8,128)(2,1)S(1)} %constant_dynamic-update-slice_fusion.out_mine), channel_id=1, source_target_pairs={{0,32},{32,0},{1,33},{33,1},{2,34},{34,2},{3,35},{35,3},{4,36},{36... | collective-permute-start | bytes 1228808 | tf_op jit(solution)/shard_map/ppermute | solution.py:316
  64.2 1.1 copy-start.3
  65.3 22.9 %all-to-all-start.2 = ((bf16[8,640,128]{2,1,0:T(8,128)(2,1)}), bf16[8,640,128]{2,1,0:T(8,128)(2,1)S(1)}, u32[]{:S(2)}, u32[]{:S(2)}) async-start(bf16[8,640,128]{2,1,0:T(8,128)(2,1)} %copy-done.3), calls=%async_computation.2 | async-start | bytes 2621440 | tf_op jit(solution)/shard_map/all_to_all | solution.py:324
  70.1 17.3 %collective-permute-start.5 = (bf16[32,640]{1,0:T(8,128)(2,1)S(1)}, bf16[32,640]{1,0:T(8,128)(2,1)S(1)}, u32[]{:S(2)}, u32[]{:S(2)}) collective-permute-start(bf16[32,640]{1,0:T(8,128)(2,1)S(1)} %get-tuple-element.60), channel_id=1, source_target_pairs={{0,1},{1,2},{2,3},{3,0},{4,5},{5,6},{6,7},{7,4},{8,9},{9,10},{10,1... | collective-permute-start | bytes 122888 | tf_op jit(solution)/shard_map/ppermute | solution.py:308
  73.3 14.8 %collective-permute-start.6 = (bf16[32,640]{1,0:T(8,128)(2,1)S(1)}, bf16[32,640]{1,0:T(8,128)(2,1)S(1)}, u32[]{:S(2)}, u32[]{:S(2)}) collective-permute-start(bf16[32,640]{1,0:T(8,128)(2,1)S(1)} %get-tuple-element.61), channel_id=1, source_target_pairs={{0,2},{1,3},{2,0},{3,1},{4,6},{5,7},{6,4},{7,5},{8,10},{9,11},{10,... | collective-permute-start | bytes 122888 | tf_op jit(solution)/shard_map/ppermute | solution.py:308
  77.7 10.5 %collective-permute-start.7 = (bf16[32,640]{1,0:T(8,128)(2,1)S(1)}, bf16[32,640]{1,0:T(8,128)(2,1)S(1)}, u32[]{:S(2)}, u32[]{:S(2)}) collective-permute-start(bf16[32,640]{1,0:T(8,128)(2,1)S(1)} %get-tuple-element.62), channel_id=1, source_target_pairs={{0,3},{1,0},{2,1},{3,2},{4,7},{5,4},{6,5},{7,6},{8,11},{9,8},{10,9... | collective-permute-start | bytes 122888 | tf_op jit(solution)/shard_map/ppermute | solution.py:308
  88.2 1.3 copy-start.2
  91.3 24.5 %all-to-all-start.3 = ((bf16[8,56,640]{2,1,0:T(8,128)(2,1)}), bf16[8,56,640]{2,1,0:T(8,128)(2,1)S(1)}, u32[]{:S(2)}, u32[]{:S(2)}) async-start(bf16[8,56,640]{2,1,0:T(8,128)(2,1)} %shard_map.98), calls=%async_computation.3 | async-start | bytes 1146880 | tf_op jit(solution)/shard_map/all_to_all | solution.py:324
  98.8 5.1 %collective-permute-start.8 = (bf16[4,128,640]{2,1,0:T(8,128)(2,1)S(1)}, bf16[4,128,640]{2,1,0:T(8,128)(2,1)S(1)}, u32[]{:S(2)}, u32[]{:S(2)}) collective-permute-start(bf16[4,128,640]{2,1,0:T(8,128)(2,1)S(1)} %get-tuple-element.73), channel_id=1, source_target_pairs={{0,32},{32,0},{1,33},{33,1},{2,34},{34,2},{3,35},{35,3},{4,36},{36... | collective-permute-start | bytes 1966088 | tf_op jit(solution)/shard_map/ppermute | solution.py:316
  104.0 8.5 %collective-permute-start.9 = (bf16[128,640]{1,0:T(8,128)(2,1)S(1)}, bf16[128,640]{1,0:T(8,128)(2,1)S(1)}, u32[]{:S(2)}, u32[]{:S(2)}) collective-permute-start(bf16[128,640]{1,0:T(8,128)(2,1)S(1)} %get-tuple-element.74), channel_id=1, source_target_pairs={{0,1},{1,2},{2,3},{3,0},{4,5},{5,6},{6,7},{7,4},{8,9},{9,10},{10,1... | collective-permute-start | bytes 491528 | tf_op jit(solution)/shard_map/ppermute | solution.py:308
  116.7 22.0 %all-to-all-start.4 = ((bf16[8,40,640]{2,1,0:T(8,128)(2,1)}), bf16[8,40,640]{2,1,0:T(8,128)(2,1)S(1)}, u32[]{:S(2)}, u32[]{:S(2)}) async-start(bf16[8,40,640]{2,1,0:T(8,128)(2,1)} %broadcast_in_dim.2), calls=%async_computation.4 | async-start | bytes 819200 | tf_op jit(solution)/shard_map/all_to_all | solution.py:324
  125.6 9.9 %collective-permute-start.10 = (bf16[128,640]{1,0:T(8,128)(2,1)S(1)}, bf16[128,640]{1,0:T(8,128)(2,1)S(1)}, u32[]{:S(2)}, u32[]{:S(2)}) collective-permute-start(bf16[128,640]{1,0:T(8,128)(2,1)S(1)} %get-tuple-element.81), channel_id=1, source_target_pairs={{0,2},{1,3},{2,0},{3,1},{4,6},{5,7},{6,4},{7,5},{8,10},{9,11},{10,... | collective-permute-start | bytes 491528 | tf_op jit(solution)/shard_map/ppermute | solution.py:308
  128.4 9.4 %collective-permute-start.11 = (bf16[128,640]{1,0:T(8,128)(2,1)S(1)}, bf16[128,640]{1,0:T(8,128)(2,1)S(1)}, u32[]{:S(2)}, u32[]{:S(2)}) collective-permute-start(bf16[128,640]{1,0:T(8,128)(2,1)S(1)} %get-tuple-element.82), channel_id=1, source_target_pairs={{0,3},{1,0},{2,1},{3,2},{4,7},{5,4},{6,5},{7,6},{8,11},{9,8},{10,9... | collective-permute-start | bytes 491528 | tf_op jit(solution)/shard_map/ppermute | solution.py:308
  138.8 5.7 %collective-permute-start.12 = (f32[40,640]{1,0:T(8,128)S(1)}, f32[40,640]{1,0:T(8,128)S(1)}, u32[]{:S(2)}, u32[]{:S(2)}) collective-permute-start(f32[40,640]{1,0:T(8,128)S(1)} %broadcast_multiply_fusion.own), channel_id=1, source_target_pairs={{0,32},{32,0},{1,33},{33,1},{2,34},{34,2},{3,35},{35,3},{4,36},{36... | collective-permute-start | bytes 307208 | tf_op jit(solution)/shard_map/ppermute | solution.py:316

commit v5 on v4

--- a/solution.py
+++ b/solution.py
@@ -173,7 +173,7 @@
 
 def bwd_kernel(
     lengths, offsets, got, qkv_t, prob, context, out_mine, out_theirs, send,
-    grad, gt, gp, dq, dp,
+    grad, gt, gp, go, dq, dp,
 ):
     core, me = here()
     x_here = lax.axis_index("x")
@@ -188,10 +188,11 @@
     gt[...] = grad_f.T
     for member, y, half in blocks():
         gp[member, y * OP : (y + 1) * OP] = gt[half * OP : (half + 1) * OP]
-    d_ctx = None
-    for member, rows in out_blocks(core, x_here, out_mine, out_theirs):
-        term = dot(gp[member].T.astype(BF), rows, 1, 0)
-        d_ctx = term if d_ctx is None else d_ctx + term
+    for n, (member, _) in enumerate(out_blocks(core, x_here, out_mine, out_theirs)):
+        go[n] = gp[member]
+    left = go[...].reshape(TEAM * OB, CAP).T.astype(BF)
+    rows = jnp.concatenate([out_mine[...], out_theirs[...]], axis=0)
+    d_ctx = dot(left, rows, 1, 0)
     d_ctx_t = d_ctx.astype(BF).astype(F32).T.astype(BF)
     for h in range(HEADS):
         at = [slice(part * D + h * HEAD_DIM, part * D + (h + 1) * HEAD_DIM) for part in range(3)]
@@ -207,10 +208,10 @@
     for member, y, half in blocks():
         low = member * QB + y * QP
         dp[low : low + QP] = dq[half * QP : (half + 1) * QP]
+    parts = dot(gp[...].reshape(TEAM * OB, CAP).astype(BF), context[...], 1, 0).astype(BF)
     for member in range(TEAM):
         send[member, 0:QB] = dp[member * QB : (member + 1) * QB].astype(BF)
-        rows = gp[member].astype(BF)
-        part = dot(rows, context[...], 1, 0).astype(BF)
+        part = parts[member * OB : (member + 1) * OB]
         for lane in range(LB):
             low = QB + lane * OB
             send[member, low : low + OB] = part[:, lane * CAP : (lane + 1) * CAP]
@@ -241,11 +242,8 @@
 def grads_kernel(got, normed, *refs):
     near, (send, fq, fo, tmp, rows_x) = refs[:NX], refs[NX:]
     x_here = lax.axis_index("x")
-    total = None
-    for member in range(TEAM):
-        term = dot(got[member, 0:QB], normed[member], 1, 0)
-        total = term if total is None else total + term
-    fq[...] = total
+    left = jnp.concatenate([got[member, 0:QB] for member in range(TEAM)], axis=1)
+    fq[...] = dot(left, normed[...].reshape(TEAM * CAP, D), 1, 0)
     for lane in range(LB):
         low = QB + lane * OB
         total = got[0, low : low + OB].astype(F32)
@@ -365,6 +363,7 @@
         (sds((TEAM, QB + LB * OB, CAP)), sds((CAP, D))),
         [
             scratch((D, CAP), F32),
+            scratch((TEAM, OB, CAP), F32),
             scratch((TEAM, OB, CAP), F32),
             scratch((3 * D, CAP), F32),
             scratch((3 * D, CAP), F32),

time: 146 us -> 146 us (level)
  no operation moved by 1% of the time
where the time goes in v5:
time: 146 us; the launch traced here: 145 us
  starting transfers between devices  78.7 us (54%)
  waiting for transfers between devices  31.1 us (21%)
  Pallas kernels  17.3 us (12%)
  blocking collectives  12.2 us (8%)
  local copies, waits for them, and re-layouts  4.33 us (3%)
    all_to_all x5, starting transfers between devices, exchange(): return lax.all_to_all(a, axis, split_axis=0, concat_axis=0, tiled=True)  30.8 us
    ppermute x9, starting transfers between devices, along_x(): return lax.ppermute(a, 'x', [(x, target(x)) for x in range(NX)])  30.6 us
    ppermute x9, waiting for transfers between devices, along_x(): return lax.ppermute(a, 'x', [(x, target(x)) for x in range(NX)])  23.3 us
    ppermute x4, starting transfers between devices, swap(): return lax.ppermute(a, 'core', [(0, 1), (1, 0)])  17.3 us
    pallas_call x11, Pallas kernels, call(): pl.pallas_call(kernel, out_shape=out_shape, in_specs=specs, out_specs=jax...  17.3 us
    all_gather x1, blocking collectives, gather(): return lax.all_gather(a, axis, axis=0, tiled=True)  12.2 us
    ppermute x4, waiting for transfers between devices, swap(): return lax.ppermute(a, 'core', [(0, 1), (1, 0)])  4.33 us
    unnamed x15, local copies, waits for them, and re-layouts  3.52 us
  transfers between devices with their start and end apart: 18, of which 11 were waited for; matrix products, arithmetic and copies ran while one was open for 0% of the time, Pallas kernels for 5%

profile of v5, /device:TPU:1, one launch (start us, length us, event | category | flops | bytes accessed | tf_op | source)
XLA Modules:
  0.0 144.6 jit_solution(896222176971161441)
XLA Ops:
  0.6 2.2 %shard_map.93 = bf16[8,56,640]{2,1,0:T(8,128)(2,1)} custom-call(s32[32]{0:T(128)} %offsets.7, bf16[256,640]{1,0:T(8,128)(2,1)} %d_embeds.1, bf16[60,640]{1,0:T(8,128)(2,1)} %bitcast.12, bf16[20,640]{1,0:T(8,128)(2,1)} %bitcast.13), custom_call_target="tpu_custom_call" | custom-call | tf_op jit(solution)/shard_map/pallas_call | solution.py:38
  2.8 7.7 %all-to-all-start = ((bf16[8,56,640]{2,1,0:T(8,128)(2,1)}), bf16[8,56,640]{2,1,0:T(8,128)(2,1)S(1)}, u32[]{:S(2)}, u32[]{:S(2)}) async-start(bf16[8,56,640]{2,1,0:T(8,128)(2,1)} %shard_map.93), calls=%async_computation | async-start | bytes 1146880 | tf_op jit(solution)/shard_map/all_to_all | solution.py:322
  10.5 12.2 %all-gather = bf16[1,512,640]{2,1,0:T(8,128)(2,1)S(1)} all-gather(bf16[1,128,640]{2,1,0:T(8,128)(2,1)S(1)} %copy-done), channel_id=2, replica_groups=mesh['z'=8,'core'=2,'y'=8,'x'=4] {'x'}, dimensions={1}, use_global_device_ids=true | all-gather | bytes 819200 | tf_op jit(solution)/shard_map/all_gather | solution.py:326
  22.7 6.4 %collective-permute-start = (bf16[512,640]{1,0:T(8,128)(2,1)S(1)}, bf16[512,640]{1,0:T(8,128)(2,1)S(1)}, u32[]{:S(2)}, u32[]{:S(2)}) collective-permute-start(bf16[512,640]{1,0:T(8,128)(2,1)S(1)} %bitcast.7), channel_id=1, source_target_pairs={{0,32},{32,0},{1,33},{33,1},{2,34},{34,2},{3,35},{35,3},{4,36},{36... | collective-permute-start | bytes 1966088 | tf_op jit(solution)/shard_map/ppermute | solution.py:314
  29.0 1.7 %collective-permute-done.theirs = bf16[512,640]{1,0:T(8,128)(2,1)S(1)} collective-permute-done((bf16[512,640]{1,0:T(8,128)(2,1)S(1)}, bf16[512,640]{1,0:T(8,128)(2,1)S(1)}, u32[]{:S(2)}, u32[]{:S(2)}) %collective-permute-start) | collective-permute-done | bytes 655392 | tf_op jit(solution)/shard_map/ppermute | solution.py:314
  30.8 2.1 %shard_map.94 = (bf16[8,400,128]{2,1,0:T(8,128)(2,1)}, bf16[240,640]{1,0:T(8,128)(2,1)S(1)}, bf16[80,640]{1,0:T(8,128)(2,1)S(1)}, bf16[8,128,640]{2,1,0:T(8,128)(2,1)S(1)}) custom-call(bf16[512,640]{1,0:T(8,128)(2,1)S(1)} %bitcast.8, bf16[512,640]{1,0:T(8,128)(2,1)S(1)} %collective-permute-done.theirs, bf16[8,56,640]{2,1,0:T(8,128)(2,1)S(1)} %all-to-all-done.got), custom_call_target="tpu_custom_call" | custom-call | tf_op jit(solution)/shard_map/pallas_call | solution.py:38
  32.9 1.1 copy-done.1
  33.9 4.0 %all-to-all-start.1 = ((bf16[8,400,128]{2,1,0:T(8,128)(2,1)}), bf16[8,400,128]{2,1,0:T(8,128)(2,1)S(1)}, u32[]{:S(2)}, u32[]{:S(2)}) async-start(bf16[8,400,128]{2,1,0:T(8,128)(2,1)} %get-tuple-element.46), calls=%async_computation.1 | async-start | bytes 1638400 | tf_op jit(solution)/shard_map/all_to_all | solution.py:322
  37.9 4.5 %collective-permute-start.3 = (bf16[80,640]{1,0:T(8,128)(2,1)S(1)}, bf16[80,640]{1,0:T(8,128)(2,1)S(1)}, u32[]{:S(2)}, u32[]{:S(2)}) collective-permute-start(bf16[80,640]{1,0:T(8,128)(2,1)S(1)} %get-tuple-element.47), channel_id=1, source_target_pairs={{0,3},{1,0},{2,1},{3,2},{4,7},{5,4},{6,5},{7,6},{8,11},{9,8},{10,9... | collective-permute-start | bytes 307208 | tf_op jit(solution)/shard_map/ppermute | solution.py:306
  42.4 2.5 %collective-permute-start.2 = (bf16[80,640]{1,0:T(8,128)(2,1)S(1)}, bf16[80,640]{1,0:T(8,128)(2,1)S(1)}, u32[]{:S(2)}, u32[]{:S(2)}) collective-permute-start(bf16[80,640]{1,0:T(8,128)(2,1)S(1)} %get-tuple-element.47), channel_id=1, source_target_pairs={{0,2},{1,3},{2,0},{3,1},{4,6},{5,7},{6,4},{7,5},{8,10},{9,11},{10,... | collective-permute-start | bytes 307208 | tf_op jit(solution)/shard_map/ppermute | solution.py:306
  44.9 2.5 %collective-permute-start.1 = (bf16[80,640]{1,0:T(8,128)(2,1)S(1)}, bf16[80,640]{1,0:T(8,128)(2,1)S(1)}, u32[]{:S(2)}, u32[]{:S(2)}) collective-permute-start(bf16[80,640]{1,0:T(8,128)(2,1)S(1)} %get-tuple-element.47), channel_id=1, source_target_pairs={{0,1},{1,2},{2,3},{3,0},{4,5},{5,6},{6,7},{7,4},{8,9},{9,10},{10,1... | collective-permute-start | bytes 307208 | tf_op jit(solution)/shard_map/ppermute | solution.py:306
  47.4 3.9 %collective-permute-done.3 = bf16[80,640]{1,0:T(8,128)(2,1)S(1)} collective-permute-done((bf16[80,640]{1,0:T(8,128)(2,1)S(1)}, bf16[80,640]{1,0:T(8,128)(2,1)S(1)}, u32[]{:S(2)}, u32[]{:S(2)}) %collective-permute-start.3) | collective-permute-done | bytes 102432 | tf_op jit(solution)/shard_map/ppermute | solution.py:306
  51.3 1.6 %collective-permute-done.2 = bf16[80,640]{1,0:T(8,128)(2,1)S(1)} collective-permute-done((bf16[80,640]{1,0:T(8,128)(2,1)S(1)}, bf16[80,640]{1,0:T(8,128)(2,1)S(1)}, u32[]{:S(2)}, u32[]{:S(2)}) %collective-permute-start.2) | collective-permute-done | bytes 102432 | tf_op jit(solution)/shard_map/ppermute | solution.py:306
  52.8 1.8 %collective-permute-done.1 = bf16[80,640]{1,0:T(8,128)(2,1)S(1)} collective-permute-done((bf16[80,640]{1,0:T(8,128)(2,1)S(1)}, bf16[80,640]{1,0:T(8,128)(2,1)S(1)}, u32[]{:S(2)}, u32[]{:S(2)}) %collective-permute-start.1) | collective-permute-done | bytes 102432 | tf_op jit(solution)/shard_map/ppermute | solution.py:306
  54.7 0.0 all-to-all-done.1.got
  54.7 2.8 %collective-permute-start.4 = (bf16[320,640]{1,0:T(8,128)(2,1)S(1)}, bf16[320,640]{1,0:T(8,128)(2,1)S(1)}, u32[]{:S(2)}, u32[]{:S(2)}) collective-permute-start(bf16[320,640]{1,0:T(8,128)(2,1)S(1)} %constant_dynamic-update-slice_fusion.out_mine), channel_id=1, source_target_pairs={{0,32},{32,0},{1,33},{33,1},{2,34},{34,2},{3,35},{35,3},{4,36},{36... | collective-permute-start | bytes 1228808 | tf_op jit(solution)/shard_map/ppermute | solution.py:314
  57.5 2.3 %shard_map.95 = (bf16[1920,128]{1,0:T(8,128)(2,1)S(1)}, f32[8,128,128]{2,1,0:T(8,128)S(1)}, bf16[640,128]{1,0:T(8,128)(2,1)S(1)}, bf16[128,640]{1,0:T(8,128)(2,1)S(1)}) custom-call(s32[32]{0:T(128)S(1)} %copy-done.5, bf16[8,400,128]{2,1,0:T(8,128)(2,1)S(1)} %all-to-all-done.1.got), custom_call_target="tpu_custom_call" | custom-call | tf_op jit(solution)/shard_map/pallas_call | solution.py:38
  59.8 4.0 %shard_map.96 = (bf16[8,640,128]{2,1,0:T(8,128)(2,1)S(1)}, bf16[128,640]{1,0:T(8,128)(2,1)S(1)}) custom-call(s32[32]{0:T(128)S(1)} %copy-done.5, s32[32]{0:T(128)S(1)} %copy-done.4, bf16[8,400,128]{2,1,0:T(8,128)(2,1)S(1)} %all-to-all-done.1.got, bf16[1920,128]{1,0:T(8,128)(2,1)S(1)} %get-tuple-element.49.qkv_t, f32[8,128,128]{2,1,0:T(8,128)S(1)} %get-tuple-element.50.prob, ...), custom_call_target="tpu_custom_call" | custom-call | tf_op jit(solution)/shard_map/pallas_call | solution.py:38
  63.9 1.1 copy-done.3
  65.0 3.5 %all-to-all-start.2 = ((bf16[8,640,128]{2,1,0:T(8,128)(2,1)}), bf16[8,640,128]{2,1,0:T(8,128)(2,1)S(1)}, u32[]{:S(2)}, u32[]{:S(2)}) async-start(bf16[8,640,128]{2,1,0:T(8,128)(2,1)} %copy-done.3), calls=%async_computation.2 | async-start | bytes 2621440 | tf_op jit(solution)/shard_map/all_to_all | solution.py:322
  68.5 1.3 shard_map.97
  69.8 3.3 %collective-permute-start.5 = (bf16[32,640]{1,0:T(8,128)(2,1)S(1)}, bf16[32,640]{1,0:T(8,128)(2,1)S(1)}, u32[]{:S(2)}, u32[]{:S(2)}) collective-permute-start(bf16[32,640]{1,0:T(8,128)(2,1)S(1)} %get-tuple-element.60), channel_id=1, source_target_pairs={{0,1},{1,2},{2,3},{3,0},{4,5},{5,6},{6,7},{7,4},{8,9},{9,10},{10,1... | collective-permute-start | bytes 122888 | tf_op jit(solution)/shard_map/ppermute | solution.py:306
  73.1 4.3 %collective-permute-start.6 = (bf16[32,640]{1,0:T(8,128)(2,1)S(1)}, bf16[32,640]{1,0:T(8,128)(2,1)S(1)}, u32[]{:S(2)}, u32[]{:S(2)}) collective-permute-start(bf16[32,640]{1,0:T(8,128)(2,1)S(1)} %get-tuple-element.61), channel_id=1, source_target_pairs={{0,2},{1,3},{2,0},{3,1},{4,6},{5,7},{6,4},{7,5},{8,10},{9,11},{10,... | collective-permute-start | bytes 122888 | tf_op jit(solution)/shard_map/ppermute | solution.py:306
  77.4 3.1 %collective-permute-start.7 = (bf16[32,640]{1,0:T(8,128)(2,1)S(1)}, bf16[32,640]{1,0:T(8,128)(2,1)S(1)}, u32[]{:S(2)}, u32[]{:S(2)}) collective-permute-start(bf16[32,640]{1,0:T(8,128)(2,1)S(1)} %get-tuple-element.62), channel_id=1, source_target_pairs={{0,3},{1,0},{2,1},{3,2},{4,7},{5,4},{6,5},{7,6},{8,11},{9,8},{10,9... | collective-permute-start | bytes 122888 | tf_op jit(solution)/shard_map/ppermute | solution.py:306
  80.5 6.6 %collective-permute-done.5.refs_1_ = bf16[32,640]{1,0:T(8,128)(2,1)S(1)} collective-permute-done((bf16[32,640]{1,0:T(8,128)(2,1)S(1)}, bf16[32,640]{1,0:T(8,128)(2,1)S(1)}, u32[]{:S(2)}, u32[]{:S(2)}) %collective-permute-start.5) | collective-permute-done | bytes 40992 | tf_op jit(solution)/shard_map/ppermute | solution.py:306
  87.1 0.8 collective-permute-done.6.refs_2_
  87.9 1.3 copy-done.2
  89.2 1.5 %shard_map.98 = bf16[8,56,640]{2,1,0:T(8,128)(2,1)} custom-call(bf16[8,640,128]{2,1,0:T(8,128)(2,1)S(1)} %all-to-all-done.2.got, bf16[8,128,640]{2,1,0:T(8,128)(2,1)S(1)} %copy-done.2, bf16[32,640]{1,0:T(8,128)(2,1)S(1)} %get-tuple-element.65.refs_0_, bf16[32,640]{1,0:T(8,128)(2,1)S(1)} %collective-permute-done.5.refs_1_, ...), custom_call_target="tpu_custom_call" | custom-call | tf_op jit(solution)/shard_map/pallas_call | solution.py:38
  90.7 6.8 %all-to-all-start.3 = ((bf16[8,56,640]{2,1,0:T(8,128)(2,1)}), bf16[8,56,640]{2,1,0:T(8,128)(2,1)S(1)}, u32[]{:S(2)}, u32[]{:S(2)}) async-start(bf16[8,56,640]{2,1,0:T(8,128)(2,1)} %shard_map.98), calls=%async_computation.3 | async-start | bytes 1146880 | tf_op jit(solution)/shard_map/all_to_all | solution.py:322
  97.5 0.6 shard_map.99
  98.1 3.3 %collective-permute-start.8 = (bf16[4,128,640]{2,1,0:T(8,128)(2,1)S(1)}, bf16[4,128,640]{2,1,0:T(8,128)(2,1)S(1)}, u32[]{:S(2)}, u32[]{:S(2)}) collective-permute-start(bf16[4,128,640]{2,1,0:T(8,128)(2,1)S(1)} %get-tuple-element.73), channel_id=1, source_target_pairs={{0,32},{32,0},{1,33},{33,1},{2,34},{34,2},{3,35},{35,3},{4,36},{36... | collective-permute-start | bytes 1966088 | tf_op jit(solution)/shard_map/ppermute | solution.py:314
  101.5 1.7 %collective-permute-done.8.theirs = bf16[4,128,640]{2,1,0:T(8,128)(2,1)S(1)} collective-permute-done((bf16[4,128,640]{2,1,0:T(8,128)(2,1)S(1)}, bf16[4,128,640]{2,1,0:T(8,128)(2,1)S(1)}, u32[]{:S(2)}, u32[]{:S(2)}) %collective-permute-start.8) | collective-permute-done | bytes 655392 | tf_op jit(solution)/shard_map/ppermute | solution.py:314
  103.2 0.2 shard_map.100
  103.3 2.1 %collective-permute-start.9 = (bf16[128,640]{1,0:T(8,128)(2,1)S(1)}, bf16[128,640]{1,0:T(8,128)(2,1)S(1)}, u32[]{:S(2)}, u32[]{:S(2)}) collective-permute-start(bf16[128,640]{1,0:T(8,128)(2,1)S(1)} %get-tuple-element.74), channel_id=1, source_target_pairs={{0,1},{1,2},{2,3},{3,0},{4,5},{5,6},{6,7},{7,4},{8,9},{9,10},{10,1... | collective-permute-start | bytes 491528 | tf_op jit(solution)/shard_map/ppermute | solution.py:306
  105.5 6.4 %collective-permute-done.9.refs_1_ = bf16[128,640]{1,0:T(8,128)(2,1)S(1)} collective-permute-done((bf16[128,640]{1,0:T(8,128)(2,1)S(1)}, bf16[128,640]{1,0:T(8,128)(2,1)S(1)}, u32[]{:S(2)}, u32[]{:S(2)}) %collective-permute-start.9) | collective-permute-done | bytes 163872 | tf_op jit(solution)/shard_map/ppermute | solution.py:306
  111.8 3.4 %all-to-all-done.3.came = bf16[8,56,640]{2,1,0:T(8,128)(2,1)S(1)} async-done(((bf16[8,56,640]{2,1,0:T(8,128)(2,1)}), bf16[8,56,640]{2,1,0:T(8,128)(2,1)S(1)}, u32[]{:S(2)}, u32[]{:S(2)}) %all-to-all-start.3) | async-done | bytes 573472 | tf_op jit(solution)/shard_map/all_to_all | solution.py:322
  115.2 0.1 slice_reduce_fusion
  115.3 0.8 broadcast_in_dim.2
  116.1 8.9 %all-to-all-start.4 = ((bf16[8,40,640]{2,1,0:T(8,128)(2,1)}), bf16[8,40,640]{2,1,0:T(8,128)(2,1)S(1)}, u32[]{:S(2)}, u32[]{:S(2)}) async-start(bf16[8,40,640]{2,1,0:T(8,128)(2,1)} %broadcast_in_dim.2), calls=%async_computation.4 | async-start | bytes 819200 | tf_op jit(solution)/shard_map/all_to_all | solution.py:322
  125.0 2.8 %collective-permute-start.10 = (bf16[128,640]{1,0:T(8,128)(2,1)S(1)}, bf16[128,640]{1,0:T(8,128)(2,1)S(1)}, u32[]{:S(2)}, u32[]{:S(2)}) collective-permute-start(bf16[128,640]{1,0:T(8,128)(2,1)S(1)} %get-tuple-element.81), channel_id=1, source_target_pairs={{0,2},{1,3},{2,0},{3,1},{4,6},{5,7},{6,4},{7,5},{8,10},{9,11},{10,... | collective-permute-start | bytes 491528 | tf_op jit(solution)/shard_map/ppermute | solution.py:306
  127.8 5.6 %collective-permute-start.11 = (bf16[128,640]{1,0:T(8,128)(2,1)S(1)}, bf16[128,640]{1,0:T(8,128)(2,1)S(1)}, u32[]{:S(2)}, u32[]{:S(2)}) collective-permute-start(bf16[128,640]{1,0:T(8,128)(2,1)S(1)} %get-tuple-element.82), channel_id=1, source_target_pairs={{0,3},{1,0},{2,1},{3,2},{4,7},{5,4},{6,5},{7,6},{8,11},{9,8},{10,9... | collective-permute-start | bytes 491528 | tf_op jit(solution)/shard_map/ppermute | solution.py:306
  133.4 1.5 %shard_map.102 = bf16[256,640]{1,0:T(8,128)(2,1)} custom-call(s32[32]{0:T(128)S(1)} %copy-done.4, bf16[8,56,640]{2,1,0:T(8,128)(2,1)S(1)} %all-to-all-done.3.came), custom_call_target="tpu_custom_call" | custom-call | tf_op jit(solution)/shard_map/pallas_call | solution.py:38
  134.9 2.3 %collective-permute-done.11.refs_3_ = bf16[128,640]{1,0:T(8,128)(2,1)S(1)} collective-permute-done((bf16[128,640]{1,0:T(8,128)(2,1)S(1)}, bf16[128,640]{1,0:T(8,128)(2,1)S(1)}, u32[]{:S(2)}, u32[]{:S(2)}) %collective-permute-start.11) | collective-permute-done | bytes 163872 | tf_op jit(solution)/shard_map/ppermute | solution.py:306
  137.2 0.9 shard_map.101
  138.1 0.1 convert_reduce_fusion
  138.2 4.8 %collective-permute-start.12 = (f32[40,640]{1,0:T(8,128)S(1)}, f32[40,640]{1,0:T(8,128)S(1)}, u32[]{:S(2)}, u32[]{:S(2)}) collective-permute-start(f32[40,640]{1,0:T(8,128)S(1)} %broadcast_multiply_fusion.own), channel_id=1, source_target_pairs={{0,32},{32,0},{1,33},{33,1},{2,34},{34,2},{3,35},{35,3},{4,36},{36... | collective-permute-start | bytes 307208 | tf_op jit(solution)/shard_map/ppermute | solution.py:314
  143.0 0.9 collective-permute-done.12.other
  143.9 0.7 shard_map.103
  (20 shorter events, 0.1 us)
Async XLA Ops:
  0.6 9.8 %copy-start = (bf16[1,128,640]{2,1,0:T(8,128)(2,1)S(1)}, bf16[1,128,640]{2,1,0:T(8,128)(2,1)}, u32[]{:S(2)}) copy-start(bf16[1,128,640]{2,1,0:T(8,128)(2,1)} %param.6) | copy-start | bytes 491524
  2.8 27.9 %all-to-all-start = ((bf16[8,56,640]{2,1,0:T(8,128)(2,1)}), bf16[8,56,640]{2,1,0:T(8,128)(2,1)S(1)}, u32[]{:S(2)}, u32[]{:S(2)}) async-start(bf16[8,56,640]{2,1,0:T(8,128)(2,1)} %shard_map.93), calls=%async_computation | async-start | bytes 1146880 | tf_op jit(solution)/shard_map/all_to_all | solution.py:322
  22.7 8.1 %collective-permute-start = (bf16[512,640]{1,0:T(8,128)(2,1)S(1)}, bf16[512,640]{1,0:T(8,128)(2,1)S(1)}, u32[]{:S(2)}, u32[]{:S(2)}) collective-permute-start(bf16[512,640]{1,0:T(8,128)(2,1)S(1)} %bitcast.7), channel_id=1, source_target_pairs={{0,32},{32,0},{1,33},{33,1},{2,34},{34,2},{3,35},{35,3},{4,36},{36... | collective-permute-start | bytes 1966088 | tf_op jit(solution)/shard_map/ppermute | solution.py:314
  32.9 1.1 copy-start.1
  33.9 23.6 %copy-start.5 = (s32[32]{0:T(128)S(1)}, s32[32]{0:T(128)}, u32[]{:S(2)}) copy-start(s32[32]{0:T(128)} %lengths.5) | copy-start | bytes 388
  33.9 25.9 %copy-start.4 = (s32[32]{0:T(128)S(1)}, s32[32]{0:T(128)}, u32[]{:S(2)}) copy-start(s32[32]{0:T(128)} %offsets.7) | copy-start | bytes 388
  33.9 20.7 %all-to-all-start.1 = ((bf16[8,400,128]{2,1,0:T(8,128)(2,1)}), bf16[8,400,128]{2,1,0:T(8,128)(2,1)S(1)}, u32[]{:S(2)}, u32[]{:S(2)}) async-start(bf16[8,400,128]{2,1,0:T(8,128)(2,1)} %get-tuple-element.46), calls=%async_computation.1 | async-start | bytes 1638400 | tf_op jit(solution)/shard_map/all_to_all | solution.py:322
  37.9 13.4 %collective-permute-start.3 = (bf16[80,640]{1,0:T(8,128)(2,1)S(1)}, bf16[80,640]{1,0:T(8,128)(2,1)S(1)}, u32[]{:S(2)}, u32[]{:S(2)}) collective-permute-start(bf16[80,640]{1,0:T(8,128)(2,1)S(1)} %get-tuple-element.47), channel_id=1, source_target_pairs={{0,3},{1,0},{2,1},{3,2},{4,7},{5,4},{6,5},{7,6},{8,11},{9,8},{10,9... | collective-permute-start | bytes 307208 | tf_op jit(solution)/shard_map/ppermute | solution.py:306
  42.4 10.4 %collective-permute-start.2 = (bf16[80,640]{1,0:T(8,128)(2,1)S(1)}, bf16[80,640]{1,0:T(8,128)(2,1)S(1)}, u32[]{:S(2)}, u32[]{:S(2)}) collective-permute-start(bf16[80,640]{1,0:T(8,128)(2,1)S(1)} %get-tuple-element.47), channel_id=1, source_target_pairs={{0,2},{1,3},{2,0},{3,1},{4,6},{5,7},{6,4},{7,5},{8,10},{9,11},{10,... | collective-permute-start | bytes 307208 | tf_op jit(solution)/shard_map/ppermute | solution.py:306
  44.9 9.8 %collective-permute-start.1 = (bf16[80,640]{1,0:T(8,128)(2,1)S(1)}, bf16[80,640]{1,0:T(8,128)(2,1)S(1)}, u32[]{:S(2)}, u32[]{:S(2)}) collective-permute-start(bf16[80,640]{1,0:T(8,128)(2,1)S(1)} %get-tuple-element.47), channel_id=1, source_target_pairs={{0,1},{1,2},{2,3},{3,0},{4,5},{5,6},{6,7},{7,4},{8,9},{9,10},{10,1... | collective-permute-start | bytes 307208 | tf_op jit(solution)/shard_map/ppermute | solution.py:306
  54.7 5.1 %collective-permute-start.4 = (bf16[320,640]{1,0:T(8,128)(2,1)S(1)}, bf16[320,640]{1,0:T(8,128)(2,1)S(1)}, u32[]{:S(2)}, u32[]{:S(2)}) collective-permute-start(bf16[320,640]{1,0:T(8,128)(2,1)S(1)} %constant_dynamic-update-slice_fusion.out_mine), channel_id=1, source_target_pairs={{0,32},{32,0},{1,33},{33,1},{2,34},{34,2},{3,35},{35,3},{4,36},{36... | collective-permute-start | bytes 1228808 | tf_op jit(solution)/shard_map/ppermute | solution.py:314
  63.9 1.1 copy-start.3
  65.0 22.9 %all-to-all-start.2 = ((bf16[8,640,128]{2,1,0:T(8,128)(2,1)}), bf16[8,640,128]{2,1,0:T(8,128)(2,1)S(1)}, u32[]{:S(2)}, u32[]{:S(2)}) async-start(bf16[8,640,128]{2,1,0:T(8,128)(2,1)} %copy-done.3), calls=%async_computation.2 | async-start | bytes 2621440 | tf_op jit(solution)/shard_map/all_to_all | solution.py:322
  69.8 17.3 %collective-permute-start.5 = (bf16[32,640]{1,0:T(8,128)(2,1)S(1)}, bf16[32,640]{1,0:T(8,128)(2,1)S(1)}, u32[]{:S(2)}, u32[]{:S(2)}) collective-permute-start(bf16[32,640]{1,0:T(8,128)(2,1)S(1)} %get-tuple-element.60), channel_id=1, source_target_pairs={{0,1},{1,2},{2,3},{3,0},{4,5},{5,6},{6,7},{7,4},{8,9},{9,10},{10,1... | collective-permute-start | bytes 122888 | tf_op jit(solution)/shard_map/ppermute | solution.py:306
  73.1 14.8 %collective-permute-start.6 = (bf16[32,640]{1,0:T(8,128)(2,1)S(1)}, bf16[32,640]{1,0:T(8,128)(2,1)S(1)}, u32[]{:S(2)}, u32[]{:S(2)}) collective-permute-start(bf16[32,640]{1,0:T(8,128)(2,1)S(1)} %get-tuple-element.61), channel_id=1, source_target_pairs={{0,2},{1,3},{2,0},{3,1},{4,6},{5,7},{6,4},{7,5},{8,10},{9,11},{10,... | collective-permute-start | bytes 122888 | tf_op jit(solution)/shard_map/ppermute | solution.py:306
  77.4 10.5 %collective-permute-start.7 = (bf16[32,640]{1,0:T(8,128)(2,1)S(1)}, bf16[32,640]{1,0:T(8,128)(2,1)S(1)}, u32[]{:S(2)}, u32[]{:S(2)}) collective-permute-start(bf16[32,640]{1,0:T(8,128)(2,1)S(1)} %get-tuple-element.62), channel_id=1, source_target_pairs={{0,3},{1,0},{2,1},{3,2},{4,7},{5,4},{6,5},{7,6},{8,11},{9,8},{10,9... | collective-permute-start | bytes 122888 | tf_op jit(solution)/shard_map/ppermute | solution.py:306
  87.9 1.3 copy-start.2
  90.7 24.5 %all-to-all-start.3 = ((bf16[8,56,640]{2,1,0:T(8,128)(2,1)}), bf16[8,56,640]{2,1,0:T(8,128)(2,1)S(1)}, u32[]{:S(2)}, u32[]{:S(2)}) async-start(bf16[8,56,640]{2,1,0:T(8,128)(2,1)} %shard_map.98), calls=%async_computation.3 | async-start | bytes 1146880 | tf_op jit(solution)/shard_map/all_to_all | solution.py:322
  98.1 5.1 %collective-permute-start.8 = (bf16[4,128,640]{2,1,0:T(8,128)(2,1)S(1)}, bf16[4,128,640]{2,1,0:T(8,128)(2,1)S(1)}, u32[]{:S(2)}, u32[]{:S(2)}) collective-permute-start(bf16[4,128,640]{2,1,0:T(8,128)(2,1)S(1)} %get-tuple-element.73), channel_id=1, source_target_pairs={{0,32},{32,0},{1,33},{33,1},{2,34},{34,2},{3,35},{35,3},{4,36},{36... | collective-permute-start | bytes 1966088 | tf_op jit(solution)/shard_map/ppermute | solution.py:314
  103.3 8.5 %collective-permute-start.9 = (bf16[128,640]{1,0:T(8,128)(2,1)S(1)}, bf16[128,640]{1,0:T(8,128)(2,1)S(1)}, u32[]{:S(2)}, u32[]{:S(2)}) collective-permute-start(bf16[128,640]{1,0:T(8,128)(2,1)S(1)} %get-tuple-element.74), channel_id=1, source_target_pairs={{0,1},{1,2},{2,3},{3,0},{4,5},{5,6},{6,7},{7,4},{8,9},{9,10},{10,1... | collective-permute-start | bytes 491528 | tf_op jit(solution)/shard_map/ppermute | solution.py:306
  116.1 22.0 %all-to-all-start.4 = ((bf16[8,40,640]{2,1,0:T(8,128)(2,1)}), bf16[8,40,640]{2,1,0:T(8,128)(2,1)S(1)}, u32[]{:S(2)}, u32[]{:S(2)}) async-start(bf16[8,40,640]{2,1,0:T(8,128)(2,1)} %broadcast_in_dim.2), calls=%async_computation.4 | async-start | bytes 819200 | tf_op jit(solution)/shard_map/all_to_all | solution.py:322
  125.0 9.9 %collective-permute-start.10 = (bf16[128,640]{1,0:T(8,128)(2,1)S(1)}, bf16[128,640]{1,0:T(8,128)(2,1)S(1)}, u32[]{:S(2)}, u32[]{:S(2)}) collective-permute-start(bf16[128,640]{1,0:T(8,128)(2,1)S(1)} %get-tuple-element.81), channel_id=1, source_target_pairs={{0,2},{1,3},{2,0},{3,1},{4,6},{5,7},{6,4},{7,5},{8,10},{9,11},{10,... | collective-permute-start | bytes 491528 | tf_op jit(solution)/shard_map/ppermute | solution.py:306
  127.8 9.4 %collective-permute-start.11 = (bf16[128,640]{1,0:T(8,128)(2,1)S(1)}, bf16[128,640]{1,0:T(8,128)(2,1)S(1)}, u32[]{:S(2)}, u32[]{:S(2)}) collective-permute-start(bf16[128,640]{1,0:T(8,128)(2,1)S(1)} %get-tuple-element.82), channel_id=1, source_target_pairs={{0,3},{1,0},{2,1},{3,2},{4,7},{5,4},{6,5},{7,6},{8,11},{9,8},{10,9... | collective-permute-start | bytes 491528 | tf_op jit(solution)/shard_map/ppermute | solution.py:306
  138.2 5.7 %collective-permute-start.12 = (f32[40,640]{1,0:T(8,128)S(1)}, f32[40,640]{1,0:T(8,128)S(1)}, u32[]{:S(2)}, u32[]{:S(2)}) collective-permute-start(f32[40,640]{1,0:T(8,128)S(1)} %broadcast_multiply_fusion.own), channel_id=1, source_target_pairs={{0,32},{32,0},{1,33},{33,1},{2,34},{34,2},{3,35},{35,3},{4,36},{36... | collective-permute-start | bytes 307208 | tf_op jit(solution)/shard_map/ppermute | solution.py:314
